TPU v7x, 32 devices: a whole 2x2x4 slice. The times are simulated.
32 devices in a mesh: group: 2 (over x), inp: 8 (over z, y), out: 2 (over core).
Axes of the slice: x: 2, y: 2, z: 4, core: 2. Of those that a mesh axis runs over, the one named last changes fastest.
Arguments:
- acts: bfloat16 [4, 512, 28672], P(('group', 'out'), None, 'inp'), parts along dimension 0, may hold values from -6 to 6
- grads: bfloat16 [4, 512, 8192], P(('group', 'out'), None, 'inp'), parts along dimension 0, may hold values from -6 to 6
- basis_a: bfloat16 [57344, 4096], P(('group', 'inp')), parts along dimension 0, may hold values from -0.03125 to 0.03125
- basis_g: bfloat16 [16384, 2048], P(('group', 'inp')), parts along dimension 0, may hold values from -0.0625 to 0.0625
- lengths: int32 [4], P(('group', 'out')), parts along dimension 0, may hold values from 128 to 512, as said below
Outputs:
- moments: float32 [4096, 4096], P(('group', 'out'), 'inp'), parts along dimension 0
There are 2 independent parts, one for each index of `group`. A program takes and returns all parts, laid end to end along the dimension named above; each array names one. Nothing has to cross between parts.
Inputs may be any that keep to these rules, and one draw needn't show every extreme that they name: `lengths`: some sequence has all 512 tokens valid.
All inputs are finite; a program needn't handle non-finite values.
Results may differ from a plain program's by a relative error of at most 0.0042.
Values may be sent and summed in bfloat16 or wider, within the bound.
No kernel may reach another device: no remote copies, remote signals or barrier semaphores. Data moves between devices by JAX's collectives and lax.ppermute only.
A program may use at most 128 MiB of HBM per device.

v0:
```python
import jax
import jax.numpy as jnp
from jax import lax
from jax.sharding import PartitionSpec as P

SEQ_LEN = 512
SEQS = 2


def on_device(acts, grads, basis_a, basis_g, lengths):
    local_seqs, seq_len, feat_rows = acts.shape
    tok_rows = local_seqs * seq_len
    flat_acts = acts.reshape(tok_rows, feat_rows)
    flat_grads = grads.reshape(tok_rows, grads.shape[2])
    contract = (((0,), (1,)), ((), ()))
    grad_part = lax.dot_general(basis_g, flat_grads, contract, preferred_element_type=jnp.float32)
    act_rot = lax.psum_scatter(
        lax.dot_general(basis_a, flat_acts, contract, preferred_element_type=jnp.float32),
        "inp",
        scatter_dimension=0,
        tiled=True,
    ).astype(jnp.bfloat16)
    grad_rot = lax.psum(grad_part, "inp").astype(jnp.bfloat16)
    scale = 1.0 / SEQ_LEN**0.5
    positions = lax.broadcasted_iota(jnp.int32, (1, seq_len), 1)
    valid = positions < lengths[0]
    grad_valid = jnp.where(valid, grad_rot, jnp.zeros_like(grad_rot))
    grad_tile = (
        lax.dot_general(
            grad_valid, act_rot, (((1,), (1,)), ((), ())), preferred_element_type=jnp.float32
        )
        * scale
    )
    summed = grad_tile * grad_tile
    return lax.psum_scatter(summed, "out", scatter_dimension=0, tiled=True) / SEQS


def solution(mesh):
    in_specs = (
        P(("group", "out"), None, "inp"),
        P(("group", "out"), None, "inp"),
        P(("group", "inp"), None),
        P(("group", "inp"), None),
        P(("group", "out")),
    )
    out_specs = P(("group", "out"), "inp")
    return jax.shard_map(
        on_device, mesh=mesh, in_specs=in_specs, out_specs=out_specs, check_vma=False
    )
```

profile of v0, /device:TPU:0, one launch (start us, length us, event | category | flops | bytes accessed | tf_op | source)
XLA Modules:
  0.0 301.1 jit_solution(11747765567626545080)
XLA Ops:
  6.5 0.0 copy-start
  6.5 0.0 reduce-scatter.3.cloned.1.call-start
  6.5 22.9 %fusion = f32[4096,512]{1,0:T(8,128)} fusion(bf16[3584,4096]{1,0:T(8,128)(2,1)} %param.7, bf16[1,512,3584]{2,1,0:T(8,128)(2,1)} %param.5), kind=kOutput, calls=%fused_computation.1 | convolution fusion | flops 15032385536 | bytes 41418752 | tf_op jit(solution)/shard_map/dot_general | solution.py:18
  29.4 0.0 reduce-scatter.3.cloned.1.call-update
  29.5 0.0 reduce-scatter.5.cloned.1.call-start
  29.5 0.0 copy-done
  29.5 6.6 %fusion.5 = f32[2048,512]{1,0:T(8,128)} fusion(bf16[1024,2048]{1,0:T(8,128)(2,1)} %param.8, bf16[1,512,1024]{2,1,0:T(8,128)(2,1)S(1)} %copy-done), kind=kOutput, calls=%fused_computation.6 | convolution fusion | flops 2147483648 | bytes 9437184 | tf_op jit(solution)/shard_map/dot_general | solution.py:16
  36.8 221.3 %all-reduce.1 = bf16[2048,512]{1,0:T(8,128)(2,1)S(1)} all-reduce(f32[2048,512]{1,0:T(8,128)} %fusion.5), channel_id=1, replica_groups=mesh['group'=2,'inp'=8,'out'=2] {'inp'}, use_global_device_ids=true, to_apply=%region_0.0 | all-reduce | flops 1048576 | bytes 6291456 | tf_op jit(solution)/shard_map/psum | solution.py:23
  258.1 15.7 %reduce-scatter.3.cloned.1.call-done = f32[512,512]{1,0:T(8,128)} async-done(((f32[4096,512]{1,0:T(8,128)}), f32[512,512]{1,0:T(8,128)}) %reduce-scatter.3.cloned.1.call-update) | async-done | bytes 1048592 | tf_op jit(solution)/shard_map/reduce_scatter | solution.py:17
  273.8 4.4 %multiply_multiply_fusion = f32[2048,512]{1,0:T(8,128)} fusion(bf16[2048,512]{1,0:T(8,128)(2,1)S(1)} %all-reduce.1, pred[512]{0:T(512)(128)(4,1)S(1)} %iota_compare_fusion, f32[512,512]{1,0:T(8,128)} %reduce-scatter.3.cloned.1.call-done), kind=kOutput, calls=%fused_computation | convolution fusion | flops 1077149696 | bytes 7340544 | tf_op jit(solution)/shard_map/dot_general | solution.py:29
  278.3 0.0 reduce-scatter.5.cloned.1.call-update
  278.3 12.9 %reduce-scatter.5.cloned.1.call-done = f32[1024,512]{1,0:T(8,128)} async-done(((f32[2048,512]{1,0:T(8,128)}), f32[1024,512]{1,0:T(8,128)}) %reduce-scatter.5.cloned.1.call-update) | async-done | bytes 2097168 | tf_op jit(solution)/shard_map/reduce_scatter | solution.py:35
  291.2 3.1 %broadcast_multiply_fusion = f32[1024,512]{1,0:T(8,128)} fusion(f32[1024,512]{1,0:T(8,128)} %reduce-scatter.5.cloned.1.call-done), kind=kLoop, calls=%fused_computation.8 | loop fusion | flops 524288 | bytes 4194304 | tf_op jit(solution)/shard_map/div | solution.py:35
  (1 shorter events, 0.0 us)
Async XLA Ops:
  6.5 23.0 %copy-start = (bf16[1,512,1024]{2,1,0:T(8,128)(2,1)S(1)}, bf16[1,512,1024]{2,1,0:T(8,128)(2,1)}, u32[]{:S(2)}) copy-start(bf16[1,512,1024]{2,1,0:T(8,128)(2,1)} %param.6) | copy-start | bytes 3145732
  6.5 267.3 %reduce-scatter.3.cloned.1.call-start = ((), (), s32[]{:S(2)}) async-start(), calls=%async_computation.2 | async-start | bytes 9437184 | tf_op jit(solution)/shard_map/reduce_scatter | solution.py:17
  29.5 261.7 %reduce-scatter.5.cloned.1.call-start = ((), (), s32[]{:S(2)}) async-start(), calls=%async_computation.3 | async-start | bytes 6291456 | tf_op jit(solution)/shard_map/reduce_scatter | solution.py:35
Sparse Core Ops, SparseCore 0:
  29.6 244.2 reduce-scatter.2
  278.4 12.6 reduce-scatter.4
where the time goes:
time: 301 us
  blocking collectives  221 us (73%)
  matrix products  33.9 us (11%)
  waiting for transfers between devices  28.6 us (10%)
  between operations  14.1 us (5%)
  other arithmetic  3.15 us (1%)
    psum x1, blocking collectives, on_device(): grad_rot = lax.psum(grad_part, 'inp').astype(jnp.bfloat16)  221 us
    dot_general x1, matrix products, on_device(): lax.dot_general(basis_a, flat_acts, contract, preferred_element_type=jnp....  22.9 us
    reduce_scatter x1, waiting for transfers between devices, on_device(): lax.psum_scatter(lax.dot_general(basis_a, flat_acts, contract, preferred_...  15.7 us
    reduce_scatter x1, waiting for transfers between devices, on_device(): lax.psum_scatter(summed, 'out', scatter_dimension=0, tiled=True) / SEQS  12.9 us
    dot_general x1, matrix products, on_device(): lax.dot_general(basis_g, flat_grads, contract, preferred_element_type=jnp...  6.57 us
  transfers between devices with their start and end apart: 2, of which 2 were waited for; matrix products, arithmetic and copies ran while one was open for 2% of the time, Pallas kernels for 0%

commit v1 on v0

v1 whole, which is shorter than its diff:
```python
import functools

import jax
import jax.numpy as jnp
from jax import lax
from jax.experimental import pallas as pl
from jax.experimental.pallas import tpu as pltpu
from jax.sharding import PartitionSpec as P

SEQ_LEN = 512
SEQS = 2
TOKEN_CHUNKS = 2
LANES = 128
WIDTH = 256
ROUNDED_STEPS = 2


def reversed_bits(value, bits):
    return sum(((value >> bit) & 1) << (bits - 1 - bit) for bit in range(bits))


def rotate_kernel(order_ref, x_ref, *refs, columns, chunks, sent):
    del order_ref
    basis_refs = refs[:columns]
    send_refs = refs[columns : columns + chunks]
    keep_refs = refs[columns + chunks :]
    basis = jnp.concatenate([ref[...] for ref in basis_refs], axis=1)
    rotated = jnp.dot(x_ref[...], basis, preferred_element_type=jnp.float32)
    rows = rotated.shape[0] // chunks
    step = pl.program_id(0)

    @pl.when(step < sent)
    def _():
        for chunk, ref in enumerate(send_refs):
            ref[0] = rotated[chunk * rows : (chunk + 1) * rows].astype(ref.dtype)

    @pl.when(step >= sent)
    def _():
        for chunk, ref in enumerate(keep_refs):
            ref[0] = rotated[chunk * rows : (chunk + 1) * rows]


def rotate(order, x, basis, width, starts, stride):
    tokens, features = x.shape
    slices = order.shape[0]
    sent = slices // 2
    rows = tokens // TOKEN_CHUNKS
    wide = width * len(starts)

    def column_spec(start):
        return pl.BlockSpec((features, width), lambda step, order: (0, order[step] * stride + start))

    send_spec = pl.BlockSpec((1, rows, wide), lambda step, order: (jnp.minimum(step, sent - 1), 0, 0))
    keep_spec = pl.BlockSpec((1, rows, wide), lambda step, order: (jnp.maximum(step - sent, 0), 0, 0))
    send_shape = jax.ShapeDtypeStruct((sent, rows, wide), jnp.bfloat16)
    keep_shape = jax.ShapeDtypeStruct((sent, rows, wide), jnp.float32)
    outs = pl.pallas_call(
        functools.partial(rotate_kernel, columns=len(starts), chunks=TOKEN_CHUNKS, sent=sent),
        grid_spec=pltpu.PrefetchScalarGridSpec(
            num_scalar_prefetch=1,
            grid=(slices,),
            in_specs=[pl.BlockSpec((tokens, features), lambda step, order: (0, 0))]
            + [column_spec(start) for start in starts],
            out_specs=[send_spec] * TOKEN_CHUNKS + [keep_spec] * TOKEN_CHUNKS,
        ),
        out_shape=[send_shape] * TOKEN_CHUNKS + [keep_shape] * TOKEN_CHUNKS,
        compiler_params=pltpu.CompilerParams(vmem_limit_bytes=32 * 2**20),
        cost_estimate=pl.CostEstimate(
            flops=2 * tokens * features * wide * slices,
            bytes_accessed=2 * features * (wide * slices + tokens) + 6 * tokens * wide * slices // 2,
            transcendentals=0,
        ),
    )(order, x, *[basis] * len(starts))
    return list(zip(outs[:TOKEN_CHUNKS], outs[TOKEN_CHUNKS:]))


def rotate_narrow(order, x, basis, width, halves):
    tokens = x.shape[0]
    slices = order.shape[0]
    sent = slices // 2
    rows = tokens // TOKEN_CHUNKS
    rotated = jnp.dot(x, basis, preferred_element_type=jnp.float32)
    rotated = rotated.reshape(tokens, halves, slices, width).transpose(2, 0, 1, 3)
    rotated = jnp.take(rotated, order, axis=0).reshape(slices, tokens, halves * width)
    return [
        (
            rotated[:sent, chunk * rows : (chunk + 1) * rows].astype(jnp.bfloat16),
            rotated[sent:, chunk * rows : (chunk + 1) * rows],
        )
        for chunk in range(TOKEN_CHUNKS)
    ]


def swap(x, n, bit):
    return lax.ppermute(x, "inp", [(index, index ^ (1 << bit)) for index in range(n)])


def swap_cores(x):
    return lax.ppermute(x, "out", [(0, 1), (1, 0)])


def reduce_slices(send, keep, n, bits):
    for bit in range(bits):
        total = keep + swap(send, n, bit).astype(jnp.float32)
        half = total.shape[0] // 2
        if bit + 1 < bits:
            send, keep = total[:half], total[half:]
            if bit + 1 < ROUNDED_STEPS:
                send = send.astype(jnp.bfloat16)
    return total[0]


def gather_pieces(piece, n, bits):
    held = [piece[None]]
    for bit in reversed(range(bits)):
        held.append(swap(jnp.concatenate(held, axis=0) if len(held) > 1 else held[0], n, bit))
    return held


def moments_kernel(place_ref, *refs, sizes, chunks, blocks):
    groups = len(sizes)
    grad_refs = [refs[chunk * groups : (chunk + 1) * groups] for chunk in range(chunks)]
    act_refs = refs[chunks * groups : -1]
    out_ref = refs[-1]
    scale = 1.0 / SEQ_LEN**0.5
    wide = act_refs[0].shape[1]
    for block in range(blocks):
        high, low = [], []
        for seq in range(SEQS):
            act = jnp.concatenate(
                [act_refs[(block * chunks + chunk) * SEQS + seq][...] for chunk in range(chunks)], axis=0
            )
            high.append(act.astype(jnp.bfloat16))
            low.append((act - high[seq].astype(jnp.float32)).astype(jnp.bfloat16))
        position = 0
        for group, size in enumerate(sizes):
            rows = grad_refs[0][group].shape[2]
            total = None
            for seq in range(SEQS):
                grad = jnp.concatenate(
                    [
                        grad_refs[chunk][group][:, seq].reshape(size * rows, -1)
                        for chunk in range(chunks)
                    ],
                    axis=1,
                )
                rotated = jnp.dot(grad, high[seq], preferred_element_type=jnp.float32)
                rotated = rotated + jnp.dot(grad, low[seq], preferred_element_type=jnp.float32)
                rotated = rotated * scale
                squared = rotated * rotated
                total = squared if total is None else total + squared
            total = total / SEQS
            for index in range(size):
                start = pl.multiple_of(place_ref[position] * rows, rows)
                out_ref[pl.ds(start, rows), block * wide : (block + 1) * wide] = total[
                    index * rows : (index + 1) * rows
                ]
                position += 1


def second_moments(place, grad_pieces, acts, n):
    sizes = tuple(x.shape[0] for x in grad_pieces[0])
    rows = grad_pieces[0][0].shape[2]
    blocks = len(acts)
    wide = acts[0][0][0].shape[1]
    flat_grads = [x for chunk in grad_pieces for x in chunk]
    flat_acts = [x for block in acts for chunk in block for x in chunk]
    vmem = pl.BlockSpec(memory_space=pltpu.VMEM)
    return pl.pallas_call(
        functools.partial(moments_kernel, sizes=sizes, chunks=TOKEN_CHUNKS, blocks=blocks),
        out_shape=jax.ShapeDtypeStruct((n * rows, blocks * wide), jnp.float32),
        in_specs=[pl.BlockSpec(memory_space=pltpu.SMEM)] + [vmem] * (len(flat_grads) + len(flat_acts)),
        out_specs=vmem,
        compiler_params=pltpu.CompilerParams(vmem_limit_bytes=32 * 2**20),
        cost_estimate=pl.CostEstimate(
            flops=4 * SEQS * n * rows * blocks * wide * SEQ_LEN,
            bytes_accessed=4 * n * rows * blocks * wide + 4 * SEQS * SEQ_LEN * blocks * wide + 2 * SEQS * SEQ_LEN * n * rows,
            transcendentals=0,
        ),
    )(place, *flat_grads, *flat_acts)


def on_device(acts, grads, basis_a, basis_g, lengths, *, n):
    bits = n.bit_length() - 1
    me = lax.axis_index("inp")
    core = lax.axis_index("out")
    order = jnp.array([reversed_bits(n - 1 - at, bits) for at in range(n)], jnp.int32) ^ me
    place = jnp.array([reversed_bits(at, bits) for at in range(n)], jnp.int32) ^ me
    x_a, x_g = acts[0], grads[0]
    tokens = x_a.shape[0]
    rows = tokens // TOKEN_CHUNKS
    width_a = basis_a.shape[1] // n
    width_g = basis_g.shape[1] // n // 2

    if width_g % LANES == 0:
        parts_g = rotate(order, x_g, basis_g, width_g, (0, n), 1)
    else:
        parts_g = rotate_narrow(order, x_g, basis_g, width_g, 2)
    wide = min(WIDTH, width_a)
    blocks = width_a // wide
    parts_a = [rotate(order, x_a, basis_a, wide, (block,), blocks) for block in range(blocks)]

    grad_pieces = []
    for chunk, (send, keep) in enumerate(parts_g):
        grad_rot = reduce_slices(send, keep, n, bits).astype(jnp.bfloat16)
        positions = chunk * rows + lax.broadcasted_iota(jnp.int32, (rows, 1), 0)
        grad_valid = jnp.where(positions < lengths[0], grad_rot, jnp.zeros_like(grad_rot))
        grad_valid = grad_valid.T.reshape(2, width_g, rows)
        own = lax.dynamic_index_in_dim(grad_valid, core, 0, keepdims=False)
        other = lax.dynamic_index_in_dim(grad_valid, 1 - core, 0, keepdims=False)
        grad_pieces.append(gather_pieces(jnp.stack([own, swap_cores(other)]), n, bits))

    act_blocks = []
    for block in range(blocks):
        chunks = []
        for send, keep in parts_a[block]:
            act_rot = reduce_slices(send, keep, n, bits)
            chunks.append((act_rot, swap_cores(act_rot)))
        act_blocks.append(chunks)
    return second_moments(place, grad_pieces, act_blocks, n)


def solution(mesh):
    in_specs = (
        P(("group", "out"), None, "inp"),
        P(("group", "out"), None, "inp"),
        P(("group", "inp"), None),
        P(("group", "inp"), None),
        P(("group", "out")),
    )
    out_specs = P(("group", "out"), "inp")
    return jax.shard_map(
        functools.partial(on_device, n=mesh.shape["inp"]),
        mesh=mesh,
        in_specs=in_specs,
        out_specs=out_specs,
        check_vma=False,
    )
```

time: 301 us -> 222 us (0.74)
  blocking collectives: 221 us -> 0 us
  waiting for transfers between devices: 28.6 us -> 130 us
  Pallas kernels: 0 us -> 37.8 us
  matrix products: 33.9 us -> 0 us
  starting transfers between devices: 0.04 us -> 32.1 us
  between operations: 14.1 us -> 1.02 us
  local copies, waits for them, and re-layouts: 0.01 us -> 9.84 us
  other arithmetic: 3.15 us -> 10.9 us
    psum x1 -> x0, blocking collectives: 221 us -> none  [on_device(): grad_rot = lax.psum(grad_part, 'inp').astype(jnp.bfloat16)]
    ppermute x0 -> x30, waiting for transfers between devices: none -> 130 us  [the longest x24 128 us: swap(): lax.ppermute(x, 'inp', [(index, index ^ 1 << bit) for index in range(n)])]
    pallas_call x0 -> x4, Pallas kernels: none -> 37.8 us  [the longest x3 33.5 us: rotate(): pl.pallas_call(functools.partial(rotate_kernel, columns=len(starts), chun...]
    dot_general x3 -> x0, matrix products: 33.9 us -> none  [the longest x1 22.9 us: on_device(): lax.dot_general(basis_a, flat_acts, contract, preferred_element_type=jnp....]
    ppermute x0 -> x30, starting transfers between devices: none -> 32.1 us  [the longest x24 31 us: swap(): lax.ppermute(x, 'inp', [(index, index ^ 1 << bit) for index in range(n)])]
    reduce_scatter x2 -> x0, waiting for transfers between devices: 28.6 us -> none  [the longest x1 15.7 us: on_device(): lax.psum_scatter(lax.dot_general(basis_a, flat_acts, contract, preferred_...]
    add x0 -> x12, other arithmetic: none -> 6.84 us  [reduce_slices(): total = keep + swap(send, n, bit).astype(jnp.float32)]
    unnamed x2 -> x18, local copies, waits for them, and re-layouts: 0.01 us -> 5.81 us
  transfers between devices with their start and end apart: 2 -> 30, of which waited for: 2 -> 17; matrix products, arithmetic and copies ran while one was open for 2% -> 6% of each run, Pallas kernels for 0% -> 9%
where the time goes in v1:
time: 222 us
  waiting for transfers between devices  130 us (59%)
  Pallas kernels  37.8 us (17%)
  starting transfers between devices  32.1 us (14%)
  other arithmetic  10.9 us (5%)
  local copies, waits for them, and re-layouts  9.84 us (4%)
    ppermute x24, waiting for transfers between devices, swap(): lax.ppermute(x, 'inp', [(index, index ^ 1 << bit) for index in range(n)])  128 us
    pallas_call x3, Pallas kernels, rotate(): pl.pallas_call(functools.partial(rotate_kernel, columns=len(starts), chun...  33.5 us
    ppermute x24, starting transfers between devices, swap(): lax.ppermute(x, 'inp', [(index, index ^ 1 << bit) for index in range(n)])  31 us
    add x12, other arithmetic, reduce_slices(): total = keep + swap(send, n, bit).astype(jnp.float32)  6.84 us
    unnamed x18, local copies, waits for them, and re-layouts  5.81 us
  transfers between devices with their start and end apart: 30, of which 17 were waited for; matrix products, arithmetic and copies ran while one was open for 6% of the time, Pallas kernels for 9%

profile of v1, /device:TPU:0, one launch (start us, length us, event | category | flops | bytes accessed | tf_op | source)
XLA Modules:
  0.0 221.5 jit_solution(15632374972076696961)
XLA Ops:
  2.7 13.4 %shard_map.75 = (bf16[4,256,256]{2,1,0:T(8,128)(2,1)}, bf16[4,256,256]{2,1,0:T(8,128)(2,1)}, f32[4,256,256]{2,1,0:T(8,128)S(1)}, f32[4,256,256]{2,1,0:T(8,128)S(1)}) custom-call(s32[8]{0:T(128)S(1)} %broadcast_xor_fusion.order_ref, bf16[512,3584]{1,0:T(8,128)(2,1)S(1)} %bitcast.41, bf16[3584,4096]{1,0:T(8,128)(2,1)} %refs_0_.5), custom_call_target="tpu_custom_call" | custom-call | flops 7516192768 | bytes 21495808 | tf_op jit(solution)/shard_map/pallas_call | solution.py:57
  18.1 3.0 %collective-permute-start.22 = (bf16[4,256,256]{2,1,0:T(8,128)(2,1)}, bf16[4,256,256]{2,1,0:T(8,128)(2,1)}, u32[]{:S(2)}, u32[]{:S(2)}) collective-permute-start(bf16[4,256,256]{2,1,0:T(8,128)(2,1)} %get-tuple-element.26), channel_id=1, source_target_pairs={{0,2},{2,0},{4,6},{6,4},{8,10},{10,8},{12,14},{14,12},{1,3},{3,1},... | collective-permute-start | bytes 1572872 | tf_op jit(solution)/shard_map/ppermute | solution.py:95
  21.1 13.7 %shard_map.74 = (bf16[4,256,256]{2,1,0:T(8,128)(2,1)}, bf16[4,256,256]{2,1,0:T(8,128)(2,1)}, f32[4,256,256]{2,1,0:T(8,128)S(1)}, f32[4,256,256]{2,1,0:T(8,128)S(1)}) custom-call(s32[8]{0:T(128)S(1)} %broadcast_xor_fusion.order_ref, bf16[512,3584]{1,0:T(8,128)(2,1)S(1)} %bitcast.42, bf16[3584,4096]{1,0:T(8,128)(2,1)} %refs_0_.5), custom_call_target="tpu_custom_call" | custom-call | flops 7516192768 | bytes 21495808 | tf_op jit(solution)/shard_map/pallas_call | solution.py:57
  37.8 6.4 %shard_map.73 = (bf16[4,256,256]{2,1,0:T(8,128)(2,1)}, bf16[4,256,256]{2,1,0:T(8,128)(2,1)S(1)}, f32[4,256,256]{2,1,0:T(8,128)S(1)}, f32[4,256,256]{2,1,0:T(8,128)S(1)}) custom-call(s32[8]{0:T(128)S(1)} %broadcast_xor_fusion.order_ref, bf16[512,1024]{1,0:T(8,128)(2,1)S(1)} %bitcast.43, bf16[1024,2048]{1,0:T(8,128)(2,1)S(1)} %copy-done, ...), custom_call_target="tpu_custom_call" | custom-call | flops 2147483648 | bytes 8388608 | tf_op jit(solution)/shard_map/pallas_call | solution.py:57
  49.3 2.3 %collective-permute-start.23 = (bf16[2,256,256]{2,1,0:T(8,128)(2,1)S(1)}, bf16[2,256,256]{2,1,0:T(8,128)(2,1)S(1)}, u32[]{:S(2)}, u32[]{:S(2)}) collective-permute-start(bf16[2,256,256]{2,1,0:T(8,128)(2,1)S(1)} %slice.169), channel_id=1, source_target_pairs={{0,4},{2,6},{4,0},{6,2},{8,12},{10,14},{12,8},{14,10},{1,5},{3,7},... | collective-permute-start | bytes 786440 | tf_op jit(solution)/shard_map/ppermute | solution.py:95
  53.2 3.4 %collective-permute-done.14 = bf16[4,256,256]{2,1,0:T(8,128)(2,1)} collective-permute-done((bf16[4,256,256]{2,1,0:T(8,128)(2,1)}, bf16[4,256,256]{2,1,0:T(8,128)(2,1)}, u32[]{:S(2)}, u32[]{:S(2)}) %collective-permute-start.14) | collective-permute-done | bytes 524320 | tf_op jit(solution)/shard_map/ppermute | solution.py:95
  56.6 2.1 collective-permute-start.27
  59.9 7.9 %collective-permute-done.18 = bf16[4,256,256]{2,1,0:T(8,128)(2,1)} collective-permute-done((bf16[4,256,256]{2,1,0:T(8,128)(2,1)}, bf16[4,256,256]{2,1,0:T(8,128)(2,1)}, u32[]{:S(2)}, u32[]{:S(2)}) %collective-permute-start.18) | collective-permute-done | bytes 524320 | tf_op jit(solution)/shard_map/ppermute | solution.py:95
  67.8 2.1 collective-permute-start.15
  71.1 7.9 %collective-permute-done = bf16[4,256,256]{2,1,0:T(8,128)(2,1)} collective-permute-done((bf16[4,256,256]{2,1,0:T(8,128)(2,1)}, bf16[4,256,256]{2,1,0:T(8,128)(2,1)}, u32[]{:S(2)}, u32[]{:S(2)}) %collective-permute-start) | collective-permute-done | bytes 524320 | tf_op jit(solution)/shard_map/ppermute | solution.py:95
  82.4 7.0 %collective-permute-done.7 = bf16[4,256,256]{2,1,0:T(8,128)(2,1)S(1)} collective-permute-done((bf16[4,256,256]{2,1,0:T(8,128)(2,1)}, bf16[4,256,256]{2,1,0:T(8,128)(2,1)S(1)}, u32[]{:S(2)}, u32[]{:S(2)}) %collective-permute-start.7) | collective-permute-done | bytes 524320 | tf_op jit(solution)/shard_map/ppermute | solution.py:95
  92.4 2.8 %collective-permute-start.24 = (f32[1,256,256]{2,1,0:T(8,128)}, f32[1,256,256]{2,1,0:T(8,128)}, u32[]{:S(2)}, u32[]{:S(2)}) collective-permute-start(f32[1,256,256]{2,1,0:T(8,128)} %slice.121), channel_id=1, source_target_pairs={{0,8},{2,10},{4,12},{6,14},{8,0},{10,2},{12,4},{14,6},{1,9},{3,11}... | collective-permute-start | bytes 786440 | tf_op jit(solution)/shard_map/ppermute | solution.py:95
  96.9 11.4 %collective-permute-done.1 = bf16[2,256,256]{2,1,0:T(8,128)(2,1)S(1)} collective-permute-done((bf16[2,256,256]{2,1,0:T(8,128)(2,1)S(1)}, bf16[2,256,256]{2,1,0:T(8,128)(2,1)S(1)}, u32[]{:S(2)}, u32[]{:S(2)}) %collective-permute-start.1) | collective-permute-done | bytes 262176 | tf_op jit(solution)/shard_map/ppermute | solution.py:95
  108.3 3.0 %collective-permute-start.2 = (f32[1,256,256]{2,1,0:T(8,128)S(1)}, f32[1,256,256]{2,1,0:T(8,128)S(1)}, u32[]{:S(2)}, u32[]{:S(2)}) collective-permute-start(f32[1,256,256]{2,1,0:T(8,128)S(1)} %slice.105), channel_id=1, source_target_pairs={{0,8},{2,10},{4,12},{6,14},{8,0},{10,2},{12,4},{14,6},{1,9},{3,11}... | collective-permute-start | bytes 786440 | tf_op jit(solution)/shard_map/ppermute | solution.py:95
  112.9 34.1 %collective-permute-done.2 = f32[1,256,256]{2,1,0:T(8,128)S(1)} collective-permute-done((f32[1,256,256]{2,1,0:T(8,128)S(1)}, f32[1,256,256]{2,1,0:T(8,128)S(1)}, u32[]{:S(2)}, u32[]{:S(2)}) %collective-permute-start.2) | collective-permute-done | bytes 262176 | tf_op jit(solution)/shard_map/ppermute | solution.py:95
  147.2 15.2 %collective-permute-done.9 = f32[1,256,256]{2,1,0:T(8,128)} collective-permute-done((f32[1,256,256]{2,1,0:T(8,128)}, f32[1,256,256]{2,1,0:T(8,128)}, u32[]{:S(2)}, u32[]{:S(2)}) %collective-permute-start.9) | collective-permute-done | bytes 262176 | tf_op jit(solution)/shard_map/ppermute | solution.py:95
  165.1 3.0 %collective-permute-start.11 = (bf16[1,2,128,256]{3,2,1,0:T(8,128)(2,1)S(1)}, bf16[1,2,128,256]{3,2,1,0:T(8,128)(2,1)S(1)}, u32[]{:S(2)}, u32[]{:S(2)}) collective-permute-start(bf16[1,2,128,256]{3,2,1,0:T(8,128)(2,1)S(1)} %maximum_bitcast_fusion.1.refs_4_), channel_id=1, source_target_pairs={{0,8},{2,10},{4,12},{6,14},{8,0},{10,2},{12,4},{14,6},{1,9},{3,11}... | collective-permute-start | bytes 393224 | tf_op jit(solution)/shard_map/ppermute | solution.py:95
  169.1 8.8 %collective-permute-done.4.refs_1_ = bf16[1,2,128,256]{3,2,1,0:T(8,128)(2,1)S(1)} collective-permute-done((bf16[1,2,128,256]{3,2,1,0:T(8,128)(2,1)S(1)}, bf16[1,2,128,256]{3,2,1,0:T(8,128)(2,1)S(1)}, u32[]{:S(2)}, u32[]{:S(2)}) %collective-permute-start.4) | collective-permute-done | bytes 131104 | tf_op jit(solution)/shard_map/ppermute | solution.py:95
  177.9 2.2 %collective-permute-done.11.refs_5_ = bf16[1,2,128,256]{3,2,1,0:T(8,128)(2,1)S(1)} collective-permute-done((bf16[1,2,128,256]{3,2,1,0:T(8,128)(2,1)S(1)}, bf16[1,2,128,256]{3,2,1,0:T(8,128)(2,1)S(1)}, u32[]{:S(2)}, u32[]{:S(2)}) %collective-permute-start.11) | collective-permute-done | bytes 131104 | tf_op jit(solution)/shard_map/ppermute | solution.py:95
  183.3 6.1 %collective-permute-done.5.refs_2_ = bf16[2,2,128,256]{3,2,1,0:T(8,128)(2,1)S(1)} collective-permute-done((bf16[2,2,128,256]{3,2,1,0:T(8,128)(2,1)S(1)}, bf16[2,2,128,256]{3,2,1,0:T(8,128)(2,1)S(1)}, u32[]{:S(2)}, u32[]{:S(2)}) %collective-permute-start.5) | collective-permute-done | bytes 262176 | tf_op jit(solution)/shard_map/ppermute | solution.py:95
  189.4 4.1 %collective-permute-done.12.refs_6_ = bf16[2,2,128,256]{3,2,1,0:T(8,128)(2,1)S(1)} collective-permute-done((bf16[2,2,128,256]{3,2,1,0:T(8,128)(2,1)S(1)}, bf16[2,2,128,256]{3,2,1,0:T(8,128)(2,1)S(1)}, u32[]{:S(2)}, u32[]{:S(2)}) %collective-permute-start.12) | collective-permute-done | bytes 262176 | tf_op jit(solution)/shard_map/ppermute | solution.py:95
  197.7 10.7 %collective-permute-done.6.refs_3_ = bf16[4,2,128,256]{3,2,1,0:T(8,128)(2,1)S(1)} collective-permute-done((bf16[4,2,128,256]{3,2,1,0:T(8,128)(2,1)S(1)}, bf16[4,2,128,256]{3,2,1,0:T(8,128)(2,1)S(1)}, u32[]{:S(2)}, u32[]{:S(2)}) %collective-permute-start.6) | collective-permute-done | bytes 524320 | tf_op jit(solution)/shard_map/ppermute | solution.py:95
  208.4 8.8 %collective-permute-done.13.refs_7_ = bf16[4,2,128,256]{3,2,1,0:T(8,128)(2,1)S(1)} collective-permute-done((bf16[4,2,128,256]{3,2,1,0:T(8,128)(2,1)S(1)}, bf16[4,2,128,256]{3,2,1,0:T(8,128)(2,1)S(1)}, u32[]{:S(2)}, u32[]{:S(2)}) %collective-permute-start.13) | collective-permute-done | bytes 524320 | tf_op jit(solution)/shard_map/ppermute | solution.py:95
  217.2 4.3 %shard_map.76 = f32[1024,512]{1,0:T(8,128)} custom-call(s32[8]{0:T(128)S(1)} %broadcast_xor_fusion.1.place_ref, bf16[1,2,128,256]{3,2,1,0:T(8,128)(2,1)S(1)} %maximum_bitcast_fusion.refs_0_, bf16[1,2,128,256]{3,2,1,0:T(8,128)(2,1)S(1)} %collective-permute-done.4.refs_1_, bf16[2,2,128,256]{3,2,1,0:T(8,128)(2,1)S(1)} %collective-permute-done.5.refs_2_, ...), custom_call_target="tpu_custom_call" | custom-call | flops 2147483648 | bytes 6291456 | tf_op jit(solution)/shard_map/pallas_call | solution.py:169
  (102 shorter events, 36.8 us)
Async XLA Ops:
  18.1 29.3 %collective-permute-start.22 = (bf16[4,256,256]{2,1,0:T(8,128)(2,1)}, bf16[4,256,256]{2,1,0:T(8,128)(2,1)}, u32[]{:S(2)}, u32[]{:S(2)}) collective-permute-start(bf16[4,256,256]{2,1,0:T(8,128)(2,1)} %get-tuple-element.26), channel_id=1, source_target_pairs={{0,2},{2,0},{4,6},{6,4},{8,10},{10,8},{12,14},{14,12},{1,3},{3,1},... | collective-permute-start | bytes 1572872 | tf_op jit(solution)/shard_map/ppermute | solution.py:95
  21.1 28.2 %collective-permute-start.26 = (bf16[4,256,256]{2,1,0:T(8,128)(2,1)}, bf16[4,256,256]{2,1,0:T(8,128)(2,1)}, u32[]{:S(2)}, u32[]{:S(2)}) collective-permute-start(bf16[4,256,256]{2,1,0:T(8,128)(2,1)} %get-tuple-element.28), channel_id=1, source_target_pairs={{0,2},{2,0},{4,6},{6,4},{8,10},{10,8},{12,14},{14,12},{1,3},{3,1},... | collective-permute-start | bytes 1572872 | tf_op jit(solution)/shard_map/ppermute | solution.py:95
  35.7 20.8 %collective-permute-start.14 = (bf16[4,256,256]{2,1,0:T(8,128)(2,1)}, bf16[4,256,256]{2,1,0:T(8,128)(2,1)}, u32[]{:S(2)}, u32[]{:S(2)}) collective-permute-start(bf16[4,256,256]{2,1,0:T(8,128)(2,1)} %get-tuple-element.22), channel_id=1, source_target_pairs={{0,2},{2,0},{4,6},{6,4},{8,10},{10,8},{12,14},{14,12},{1,3},{3,1},... | collective-permute-start | bytes 1572872 | tf_op jit(solution)/shard_map/ppermute | solution.py:95
  37.5 30.4 %collective-permute-start.18 = (bf16[4,256,256]{2,1,0:T(8,128)(2,1)}, bf16[4,256,256]{2,1,0:T(8,128)(2,1)}, u32[]{:S(2)}, u32[]{:S(2)}) collective-permute-start(bf16[4,256,256]{2,1,0:T(8,128)(2,1)} %get-tuple-element.24), channel_id=1, source_target_pairs={{0,2},{2,0},{4,6},{6,4},{8,10},{10,8},{12,14},{14,12},{1,3},{3,1},... | collective-permute-start | bytes 1572872 | tf_op jit(solution)/shard_map/ppermute | solution.py:95
  45.0 34.1 %collective-permute-start = (bf16[4,256,256]{2,1,0:T(8,128)(2,1)}, bf16[4,256,256]{2,1,0:T(8,128)(2,1)}, u32[]{:S(2)}, u32[]{:S(2)}) collective-permute-start(bf16[4,256,256]{2,1,0:T(8,128)(2,1)} %get-tuple-element.18), channel_id=1, source_target_pairs={{0,2},{2,0},{4,6},{6,4},{8,10},{10,8},{12,14},{14,12},{1,3},{3,1},... | collective-permute-start | bytes 1572872 | tf_op jit(solution)/shard_map/ppermute | solution.py:95
  47.4 42.0 %collective-permute-start.7 = (bf16[4,256,256]{2,1,0:T(8,128)(2,1)}, bf16[4,256,256]{2,1,0:T(8,128)(2,1)S(1)}, u32[]{:S(2)}, u32[]{:S(2)}) collective-permute-start(bf16[4,256,256]{2,1,0:T(8,128)(2,1)} %copy-done.7), channel_id=1, source_target_pairs={{0,2},{2,0},{4,6},{6,4},{8,10},{10,8},{12,14},{14,12},{1,3},{3,1},... | collective-permute-start | bytes 1572872 | tf_op jit(solution)/shard_map/ppermute | solution.py:95
  49.3 42.0 %collective-permute-start.23 = (bf16[2,256,256]{2,1,0:T(8,128)(2,1)S(1)}, bf16[2,256,256]{2,1,0:T(8,128)(2,1)S(1)}, u32[]{:S(2)}, u32[]{:S(2)}) collective-permute-start(bf16[2,256,256]{2,1,0:T(8,128)(2,1)S(1)} %slice.169), channel_id=1, source_target_pairs={{0,4},{2,6},{4,0},{6,2},{8,12},{10,14},{12,8},{14,10},{1,5},{3,7},... | collective-permute-start | bytes 786440 | tf_op jit(solution)/shard_map/ppermute | solution.py:95
  56.6 35.8 %collective-permute-start.27 = (bf16[2,256,256]{2,1,0:T(8,128)(2,1)S(1)}, bf16[2,256,256]{2,1,0:T(8,128)(2,1)S(1)}, u32[]{:S(2)}, u32[]{:S(2)}) collective-permute-start(bf16[2,256,256]{2,1,0:T(8,128)(2,1)S(1)} %slice.168), channel_id=1, source_target_pairs={{0,4},{2,6},{4,0},{6,2},{8,12},{10,14},{12,8},{14,10},{1,5},{3,7},... | collective-permute-start | bytes 786440 | tf_op jit(solution)/shard_map/ppermute | solution.py:95
  67.8 28.2 %collective-permute-start.15 = (bf16[2,256,256]{2,1,0:T(8,128)(2,1)S(1)}, bf16[2,256,256]{2,1,0:T(8,128)(2,1)S(1)}, u32[]{:S(2)}, u32[]{:S(2)}) collective-permute-start(bf16[2,256,256]{2,1,0:T(8,128)(2,1)S(1)} %slice.171), channel_id=1, source_target_pairs={{0,4},{2,6},{4,0},{6,2},{8,12},{10,14},{12,8},{14,10},{1,5},{3,7},... | collective-permute-start | bytes 786440 | tf_op jit(solution)/shard_map/ppermute | solution.py:95
  79.1 29.3 %collective-permute-start.19 = (bf16[2,256,256]{2,1,0:T(8,128)(2,1)S(1)}, bf16[2,256,256]{2,1,0:T(8,128)(2,1)S(1)}, u32[]{:S(2)}, u32[]{:S(2)}) collective-permute-start(bf16[2,256,256]{2,1,0:T(8,128)(2,1)S(1)} %slice.170), channel_id=1, source_target_pairs={{0,4},{2,6},{4,0},{6,2},{8,12},{10,14},{12,8},{14,10},{1,5},{3,7},... | collective-permute-start | bytes 786440 | tf_op jit(solution)/shard_map/ppermute | solution.py:95
  89.4 18.9 %collective-permute-start.1 = (bf16[2,256,256]{2,1,0:T(8,128)(2,1)S(1)}, bf16[2,256,256]{2,1,0:T(8,128)(2,1)S(1)}, u32[]{:S(2)}, u32[]{:S(2)}) collective-permute-start(bf16[2,256,256]{2,1,0:T(8,128)(2,1)S(1)} %slice.173), channel_id=1, source_target_pairs={{0,4},{2,6},{4,0},{6,2},{8,12},{10,14},{12,8},{14,10},{1,5},{3,7},... | collective-permute-start | bytes 786440 | tf_op jit(solution)/shard_map/ppermute | solution.py:95
  91.3 20.8 %collective-permute-start.8 = (bf16[2,256,256]{2,1,0:T(8,128)(2,1)S(1)}, bf16[2,256,256]{2,1,0:T(8,128)(2,1)S(1)}, u32[]{:S(2)}, u32[]{:S(2)}) collective-permute-start(bf16[2,256,256]{2,1,0:T(8,128)(2,1)S(1)} %slice.172), channel_id=1, source_target_pairs={{0,4},{2,6},{4,0},{6,2},{8,12},{10,14},{12,8},{14,10},{1,5},{3,7},... | collective-permute-start | bytes 786440 | tf_op jit(solution)/shard_map/ppermute | solution.py:95
  92.4 72.7 %collective-permute-start.24 = (f32[1,256,256]{2,1,0:T(8,128)}, f32[1,256,256]{2,1,0:T(8,128)}, u32[]{:S(2)}, u32[]{:S(2)}) collective-permute-start(f32[1,256,256]{2,1,0:T(8,128)} %slice.121), channel_id=1, source_target_pairs={{0,8},{2,10},{4,12},{6,14},{8,0},{10,2},{12,4},{14,6},{1,9},{3,11}... | collective-permute-start | bytes 786440 | tf_op jit(solution)/shard_map/ppermute | solution.py:95
  96.0 84.2 %collective-permute-start.28 = (f32[1,256,256]{2,1,0:T(8,128)}, f32[1,256,256]{2,1,0:T(8,128)}, u32[]{:S(2)}, u32[]{:S(2)}) collective-permute-start(f32[1,256,256]{2,1,0:T(8,128)} %slice.125), channel_id=1, source_target_pairs={{0,8},{2,10},{4,12},{6,14},{8,0},{10,2},{12,4},{14,6},{1,9},{3,11}... | collective-permute-start | bytes 786440 | tf_op jit(solution)/shard_map/ppermute | solution.py:95
  108.2 86.8 %collective-permute-start.16 = (f32[1,256,256]{2,1,0:T(8,128)}, f32[1,256,256]{2,1,0:T(8,128)S(1)}, u32[]{:S(2)}, u32[]{:S(2)}) collective-permute-start(f32[1,256,256]{2,1,0:T(8,128)} %slice.113), channel_id=1, source_target_pairs={{0,8},{2,10},{4,12},{6,14},{8,0},{10,2},{12,4},{14,6},{1,9},{3,11}... | collective-permute-start | bytes 786440 | tf_op jit(solution)/shard_map/ppermute | solution.py:95
  108.3 38.6 %collective-permute-start.2 = (f32[1,256,256]{2,1,0:T(8,128)S(1)}, f32[1,256,256]{2,1,0:T(8,128)S(1)}, u32[]{:S(2)}, u32[]{:S(2)}) collective-permute-start(f32[1,256,256]{2,1,0:T(8,128)S(1)} %slice.105), channel_id=1, source_target_pairs={{0,8},{2,10},{4,12},{6,14},{8,0},{10,2},{12,4},{14,6},{1,9},{3,11}... | collective-permute-start | bytes 786440 | tf_op jit(solution)/shard_map/ppermute | solution.py:95
  112.1 83.6 %collective-permute-start.20 = (f32[1,256,256]{2,1,0:T(8,128)}, f32[1,256,256]{2,1,0:T(8,128)S(1)}, u32[]{:S(2)}, u32[]{:S(2)}) collective-permute-start(f32[1,256,256]{2,1,0:T(8,128)} %slice.117), channel_id=1, source_target_pairs={{0,8},{2,10},{4,12},{6,14},{8,0},{10,2},{12,4},{14,6},{1,9},{3,11}... | collective-permute-start | bytes 786440 | tf_op jit(solution)/shard_map/ppermute | solution.py:95
  147.0 15.4 %collective-permute-start.9 = (f32[1,256,256]{2,1,0:T(8,128)}, f32[1,256,256]{2,1,0:T(8,128)}, u32[]{:S(2)}, u32[]{:S(2)}) collective-permute-start(f32[1,256,256]{2,1,0:T(8,128)} %slice.109), channel_id=1, source_target_pairs={{0,8},{2,10},{4,12},{6,14},{8,0},{10,2},{12,4},{14,6},{1,9},{3,11}... | collective-permute-start | bytes 786440 | tf_op jit(solution)/shard_map/ppermute | solution.py:95
  165.1 12.8 %collective-permute-start.4 = (bf16[1,2,128,256]{3,2,1,0:T(8,128)(2,1)S(1)}, bf16[1,2,128,256]{3,2,1,0:T(8,128)(2,1)S(1)}, u32[]{:S(2)}, u32[]{:S(2)}) collective-permute-start(bf16[1,2,128,256]{3,2,1,0:T(8,128)(2,1)S(1)} %maximum_bitcast_fusion.refs_0_), channel_id=1, source_target_pairs={{0,8},{2,10},{4,12},{6,14},{8,0},{10,2},{12,4},{14,6},{1,9},{3,11}... | collective-permute-start | bytes 393224 | tf_op jit(solution)/shard_map/ppermute | solution.py:95
  165.1 15.0 %collective-permute-start.11 = (bf16[1,2,128,256]{3,2,1,0:T(8,128)(2,1)S(1)}, bf16[1,2,128,256]{3,2,1,0:T(8,128)(2,1)S(1)}, u32[]{:S(2)}, u32[]{:S(2)}) collective-permute-start(bf16[1,2,128,256]{3,2,1,0:T(8,128)(2,1)S(1)} %maximum_bitcast_fusion.1.refs_4_), channel_id=1, source_target_pairs={{0,8},{2,10},{4,12},{6,14},{8,0},{10,2},{12,4},{14,6},{1,9},{3,11}... | collective-permute-start | bytes 393224 | tf_op jit(solution)/shard_map/ppermute | solution.py:95
  177.9 18.0 %collective-permute-start.25 = (f32[256,256]{1,0:T(8,128)S(1)}, f32[256,256]{1,0:T(8,128)S(1)}, u32[]{:S(2)}, u32[]{:S(2)}) collective-permute-start(f32[256,256]{1,0:T(8,128)S(1)} %fusion.1.refs_12_), channel_id=1, source_target_pairs={{0,1},{1,0},{2,3},{3,2},{4,5},{5,4},{6,7},{7,6},{8,9},{9,8},{10,11... | collective-permute-start | bytes 786440 | tf_op jit(solution)/shard_map/ppermute | solution.py:99
  180.2 13.3 %collective-permute-start.12 = (bf16[2,2,128,256]{3,2,1,0:T(8,128)(2,1)S(1)}, bf16[2,2,128,256]{3,2,1,0:T(8,128)(2,1)S(1)}, u32[]{:S(2)}, u32[]{:S(2)}) collective-permute-start(bf16[2,2,128,256]{3,2,1,0:T(8,128)(2,1)S(1)} %pad_maximum_fusion.3), channel_id=1, source_target_pairs={{0,4},{2,6},{4,0},{6,2},{8,12},{10,14},{12,8},{14,10},{1,5},{3,7},... | collective-permute-start | bytes 786440 | tf_op jit(solution)/shard_map/ppermute | solution.py:95
  193.5 14.9 %collective-permute-start.6 = (bf16[4,2,128,256]{3,2,1,0:T(8,128)(2,1)S(1)}, bf16[4,2,128,256]{3,2,1,0:T(8,128)(2,1)S(1)}, u32[]{:S(2)}, u32[]{:S(2)}) collective-permute-start(bf16[4,2,128,256]{3,2,1,0:T(8,128)(2,1)S(1)} %pad_maximum_fusion), channel_id=1, source_target_pairs={{0,2},{2,0},{4,6},{6,4},{8,10},{10,8},{12,14},{14,12},{1,3},{3,1},... | collective-permute-start | bytes 1572872 | tf_op jit(solution)/shard_map/ppermute | solution.py:95
  195.0 22.2 %collective-permute-start.13 = (bf16[4,2,128,256]{3,2,1,0:T(8,128)(2,1)S(1)}, bf16[4,2,128,256]{3,2,1,0:T(8,128)(2,1)S(1)}, u32[]{:S(2)}, u32[]{:S(2)}) collective-permute-start(bf16[4,2,128,256]{3,2,1,0:T(8,128)(2,1)S(1)} %pad_maximum_fusion.1), channel_id=1, source_target_pairs={{0,2},{2,0},{4,6},{6,4},{8,10},{10,8},{12,14},{14,12},{1,3},{3,1},... | collective-permute-start | bytes 1572872 | tf_op jit(solution)/shard_map/ppermute | solution.py:95
  (15 other events, 122.3 us)

commit v2 on v0

v2 whole, which is shorter than its diff:
```python
import functools

import jax
import jax.numpy as jnp
from jax import lax
from jax.experimental import pallas as pl
from jax.experimental.pallas import tpu as pltpu
from jax.sharding import PartitionSpec as P

SEQ_LEN = 512
SEQS = 2
TOKEN_CHUNKS = 2
LANES = 128
WIDTH = 256
ROUNDED_STEPS_G = 2
ROUNDED_STEPS_A = 3
ANY = pl.BlockSpec(memory_space=pl.ANY)
VMEM = pl.BlockSpec(memory_space=pltpu.VMEM)
SMEM = pl.BlockSpec(memory_space=pltpu.SMEM)
MIB = 2**20
LIGHT = pl.CostEstimate(flops=0, bytes_accessed=0, transcendentals=0)


def reversed_bits(value, bits):
    return sum(((value >> bit) & 1) << (bits - 1 - bit) for bit in range(bits))


class Chain:
    def __init__(self):
        self.last = []
        self.clock = 0.0
        self.expected = []

    def expect(self, array, wait):
        self.expected.append((self.clock + wait, array))
        return array

    def waited_for(self):
        arrived = [array for due, array in self.expected if due <= self.clock]
        self.expected = [(due, array) for due, array in self.expected if due > self.clock]
        return self.last + arrived

    def call(self, body, out_shape, inputs, specs, out_specs=None, scratch=(), limit=12 * MIB, aliases=None):
        unread = self.waited_for()
        deps = len(unread)

        def kernel(*refs):
            body(*refs[: len(inputs)], *refs[len(inputs) + deps :])

        outs = pl.pallas_call(
            kernel,
            out_shape=out_shape,
            in_specs=list(specs) + [ANY] * deps,
            out_specs=out_specs or [VMEM] * len(out_shape),
            scratch_shapes=scratch,
            input_output_aliases=aliases or {},
            compiler_params=pltpu.CompilerParams(vmem_limit_bytes=limit),
            cost_estimate=LIGHT,
        )(*inputs, *unread)
        self.last = [outs[0]]
        return outs

    def rotate(self, order, x, basis, width, starts, stride, per_step, dtype):
        tokens, features = x.shape
        count = order.shape[0]
        rows = tokens // TOKEN_CHUNKS
        pieces = len(starts)
        wide = width * pieces
        unread = self.waited_for()
        deps = len(unread)

        def kernel(order_ref, x_ref, *refs):
            del order_ref
            columns = jnp.concatenate([ref[...] for ref in refs[: per_step * pieces]], axis=1)
            rotated = jnp.dot(x_ref[...], columns, preferred_element_type=jnp.float32)
            for at in range(per_step):
                for chunk, ref in enumerate(refs[per_step * pieces + deps :]):
                    ref[at] = rotated[
                        chunk * rows : (chunk + 1) * rows, at * wide : (at + 1) * wide
                    ].astype(ref.dtype)

        def column_spec(at, start):
            return pl.BlockSpec(
                (features, width), lambda step, order: (0, order[step * per_step + at] * stride + start)
            )

        column_specs = [column_spec(at, start) for at in range(per_step) for start in starts]
        outs = pl.pallas_call(
            kernel,
            grid_spec=pltpu.PrefetchScalarGridSpec(
                num_scalar_prefetch=1,
                grid=(count // per_step,),
                in_specs=[pl.BlockSpec((tokens, features), lambda step, order: (0, 0))] + column_specs + [ANY] * deps,
                out_specs=[pl.BlockSpec((per_step, rows, wide), lambda step, order: (step, 0, 0))] * TOKEN_CHUNKS,
            ),
            out_shape=[jax.ShapeDtypeStruct((count, rows, wide), dtype)] * TOKEN_CHUNKS,
            compiler_params=pltpu.CompilerParams(vmem_limit_bytes=32 * MIB),
            cost_estimate=LIGHT,
        )(order, x, *[basis] * len(column_specs), *unread)
        self.last = [outs[0]]
        return outs

    def combine(self, received, kept, dtype):
        count, rows, wide = kept.shape
        half = count // 2

        def body(received_ref, kept_ref, send_ref, hold_ref):
            send_ref[...] = (kept_ref[:half] + received_ref[:half].astype(jnp.float32)).astype(send_ref.dtype)
            hold_ref[...] = kept_ref[half:] + received_ref[half:].astype(jnp.float32)

        return self.call(
            body,
            [
                jax.ShapeDtypeStruct((half, rows, wide), dtype),
                jax.ShapeDtypeStruct((half, rows, wide), jnp.float32),
            ],
            [received, kept],
            [VMEM] * 2,
        )

    def finish(self, received, kept):
        rows, wide = kept[0].shape[1:]

        def body(*refs):
            out_ref = refs[-1]
            for chunk in range(TOKEN_CHUNKS):
                total = refs[TOKEN_CHUNKS + chunk][0] + refs[chunk][0].astype(jnp.float32)
                out_ref[chunk * rows : (chunk + 1) * rows] = total

        shape = jax.ShapeDtypeStruct((rows * TOKEN_CHUNKS, wide), jnp.float32)
        return self.call(body, [shape], [*received, *kept], [VMEM] * (2 * TOKEN_CHUNKS))[0]

    def finish_grads(self, scalars, received, kept):
        rows, wide = kept[0].shape[1:]
        half = wide // 2

        def body(scalars_ref, *refs):
            columns = []
            for chunk in range(TOKEN_CHUNKS):
                total = refs[TOKEN_CHUNKS + chunk][0] + refs[chunk][0].astype(jnp.float32)
                positions = chunk * rows + lax.broadcasted_iota(jnp.int32, (rows, wide), 0)
                total = jnp.where(positions < scalars_ref[0], total, jnp.zeros_like(total))
                columns.append(total.T.astype(jnp.bfloat16))
            grad = jnp.concatenate(columns, axis=1)
            mine_ref, other_ref = refs[2 * TOKEN_CHUNKS :]

            @pl.when(scalars_ref[1] == 0)
            def _():
                mine_ref[...] = grad[:half]
                other_ref[...] = grad[half:]

            @pl.when(scalars_ref[1] != 0)
            def _():
                mine_ref[...] = grad[half:]
                other_ref[...] = grad[:half]

        shape = jax.ShapeDtypeStruct((half, rows * TOKEN_CHUNKS), jnp.bfloat16)
        return self.call(
            body, [shape] * 2, [scalars, *received, *kept], [SMEM] + [VMEM] * (2 * TOKEN_CHUNKS)
        )

    def pair(self, mine, other):
        def body(mine_ref, other_ref, out_ref):
            out_ref[0, 0] = mine_ref[...]
            out_ref[0, 1] = other_ref[...]

        shape = jax.ShapeDtypeStruct((1, 2) + mine.shape, mine.dtype)
        return self.call(body, [shape], [mine, other], [VMEM] * 2)[0]

    def join(self, held, received):
        count = held.shape[0]

        def body(held_ref, received_ref, out_ref):
            out_ref[:count] = held_ref[...]
            out_ref[count:] = received_ref[...]

        shape = jax.ShapeDtypeStruct((2 * count,) + held.shape[1:], held.dtype)
        return self.call(body, [shape], [held, received], [VMEM] * 2)[0]

    def moments(self, place, grads, acts, out_shape, earlier=None):
        rows, tokens = grads[0].shape[2:]
        count = sum(x.shape[0] for x in grads)
        blocks = len(acts)
        flat_acts = [x for block in acts for x in block]
        scale = 1.0 / SEQ_LEN**0.5

        def body(place_ref, *refs):
            grad_refs = refs[: len(grads)]
            act_refs = refs[len(grads) : len(grads) + len(flat_acts)]
            out_ref, result_ref, sems = refs[-3:]
            total = None
            for seq in range(SEQS):
                act = jnp.concatenate([act_refs[block * SEQS + seq][...] for block in range(blocks)], axis=1)
                high = act.astype(jnp.bfloat16)
                low = (act - high.astype(jnp.float32)).astype(jnp.bfloat16)
                grad = jnp.concatenate([ref[:, seq].reshape(-1, tokens) for ref in grad_refs], axis=0)
                rotated = jnp.dot(grad, high, preferred_element_type=jnp.float32)
                rotated = rotated + jnp.dot(grad, low, preferred_element_type=jnp.float32)
                rotated = rotated * scale
                squared = rotated * rotated
                total = squared if total is None else total + squared
            result_ref[...] = total / SEQS
            copies = []
            for at in range(count):
                start = pl.multiple_of(place_ref[at] * rows, rows)
                copies.append(
                    pltpu.make_async_copy(
                        result_ref.at[pl.ds(at * rows, rows)], out_ref.at[pl.ds(start, rows)], sems.at[at]
                    )
                )
                copies[-1].start()
            for copy in copies:
                copy.wait()

        inputs = [place, *grads, *flat_acts]
        specs = [SMEM] + [VMEM] * (len(inputs) - 1)
        aliases = {}
        if earlier is not None:
            aliases = {len(inputs): 0}
            inputs.append(earlier)
            specs.append(ANY)
        return self.call(
            body,
            [out_shape],
            inputs,
            specs,
            out_specs=[ANY],
            scratch=[
                pltpu.VMEM((count * rows, out_shape.shape[1]), jnp.float32),
                pltpu.SemaphoreType.DMA((count,)),
            ],
            limit=24 * MIB,
            aliases=aliases,
        )[0]


def rotate_narrow(order, x, basis, width, halves, slices, dtype):
    tokens = x.shape[0]
    rows = tokens // TOKEN_CHUNKS
    rotated = jnp.dot(x, basis, preferred_element_type=jnp.float32)
    rotated = rotated.reshape(tokens, halves, slices, width).transpose(2, 0, 1, 3)
    rotated = jnp.take(rotated, order, axis=0).reshape(-1, tokens, halves * width).astype(dtype)
    return [rotated[:, chunk * rows : (chunk + 1) * rows] for chunk in range(TOKEN_CHUNKS)]


def swap(x, n, bit):
    return lax.ppermute(x, "inp", [(index, index ^ (1 << bit)) for index in range(n)])


def swap_cores(x):
    return lax.ppermute(x, "out", [(0, 1), (1, 0)])


def on_device(acts, grads, basis_a, basis_g, lengths, *, n):
    bits = n.bit_length() - 1
    me = lax.axis_index("inp")
    core = lax.axis_index("out")
    order = jnp.array([reversed_bits(n - 1 - at, bits) for at in range(n)], jnp.int32) ^ me
    orders = (order[: n // 2], order[n // 2 :])
    scalars = jnp.stack([lengths[0], core]).astype(jnp.int32)
    x_a, x_g = acts[0], grads[0]
    width_a = basis_a.shape[1] // n
    width_g = basis_g.shape[1] // n // 2
    wide = min(WIDTH, width_a)
    blocks = width_a // wide
    chain = Chain()

    sending, kept, received, finished = {}, {}, {}, {}
    grad_keys = [("g", 0, chunk) for chunk in range(TOKEN_CHUNKS)]
    act_keys = [("a", block, chunk) for block in range(blocks) for chunk in range(TOKEN_CHUNKS)]

    def rotate_grads(part):
        dtype = (jnp.bfloat16, jnp.float32)[part]
        if width_g % LANES == 0:
            outs = chain.rotate(orders[part], x_g, basis_g, width_g, (0, n), 1, 2, dtype)
        else:
            outs = rotate_narrow(orders[part], x_g, basis_g, width_g, 2, n, dtype)
        for key, x in zip(grad_keys, outs):
            if part == 0:
                received[key] = swap(x, n, 0)
            else:
                kept[key] = x

    def rotate_acts(block, part):
        dtype = (jnp.bfloat16, jnp.float32)[part]
        outs = chain.rotate(orders[part], x_a, basis_a, wide, (block,), blocks, 2, dtype)
        for chunk, x in enumerate(outs):
            if part == 0:
                received["a", block, chunk] = swap(x, n, 0)
            else:
                kept["a", block, chunk] = x

    def advance(key, step):
        rounded = ROUNDED_STEPS_G if key[0] == "g" else ROUNDED_STEPS_A
        dtype = jnp.bfloat16 if step + 1 < rounded else jnp.float32
        send, kept[key] = chain.combine(received[key], kept[key], dtype)
        wait = (0.8 if dtype == jnp.bfloat16 else 1.05) if step else 0.56
        received[key] = chain.expect(swap(send, n, step + 1), wait)

    def finish_acts(block):
        keys = [("a", block, chunk) for chunk in range(TOKEN_CHUNKS)]
        own = chain.finish([received[key] for key in keys], [kept[key] for key in keys])
        finished[block] = (own, chain.expect(swap_cores(own), 0.2))

    gathered = {}

    def finish_grads():
        mine, other = chain.finish_grads(
            scalars, [received[key] for key in grad_keys], [kept[key] for key in grad_keys]
        )
        gathered["mine"], gathered["other"] = mine, swap_cores(other)

    def pair_grads():
        gathered["held"] = chain.pair(gathered["mine"], gathered["other"])
        gathered["order"] = [0]
        gathered["in"] = swap(gathered["held"], n, bits - 1)

    def join_grads(bit):
        gathered["held"] = chain.join(gathered["held"], gathered["in"])
        gathered["order"] = gathered["order"] + [at ^ (1 << bit) for at in gathered["order"]]
        gathered["in"] = swap(gathered["held"], n, bit - 1)
        if bit == 2:
            gathered["side"] = chain.expect(swap(gathered["held"], n, 0), 1.7)

    def relay_grads():
        chain.last.append(gathered["in"])
        gathered["across"] = swap(gathered["in"], n, 0)

    tasks = [(-2.0, rotate_grads, (0,)), (-1.0, rotate_grads, (1,))]
    for block in range(blocks):
        tasks.append((0.1 + 1.0 * block, rotate_acts, (block, 0)))
        tasks.append((2.1 + 2.2 * block, rotate_acts, (block, 1)))
    for at, key in enumerate(grad_keys + act_keys):
        pace = 0.55 if key in (grad_keys[-1], act_keys[-1]) else 1.01
        for step in range(bits - 1):
            tasks.append((1.0 + at + pace * step, advance, (key, step)))
        if key in act_keys and key[2] == TOKEN_CHUNKS - 1:
            tasks.append((1.0 + at + pace * (bits - 1) + 0.01, finish_acts, (key[1],)))
    clock = TOKEN_CHUNKS + 0.55 * (bits - 1) + 0.95
    tasks.append((clock, finish_grads, ()))
    clock += 0.15
    tasks.append((clock, pair_grads, ()))
    for bit in range(bits - 1, 1, -1):
        clock += 1.1
        tasks.append((clock, join_grads, (bit,)))
    tasks.append((clock + 1.0, relay_grads, ()))
    for chain.clock, task, arguments in sorted(tasks, key=lambda task: task[0]):
        task(*arguments)

    low = gathered["order"]
    offsets = low + [at ^ 2 for at in low] + [at ^ 1 for at in low] + [at ^ 3 for at in low]
    place = jnp.array(offsets, jnp.int32) ^ me
    act_blocks = [finished[block] for block in range(blocks)]
    first = 3 * len(low)
    out_shape = jax.ShapeDtypeStruct((n * width_g, width_a), jnp.float32)
    out = chain.moments(
        place[:first], [gathered["held"], gathered["in"], gathered["side"]], act_blocks, out_shape
    )
    chain.last = []
    return chain.moments(place[first:], [gathered["across"]], act_blocks, out_shape, earlier=out)


def solution(mesh):
    in_specs = (
        P(("group", "out"), None, "inp"),
        P(("group", "out"), None, "inp"),
        P(("group", "inp"), None),
        P(("group", "inp"), None),
        P(("group", "out")),
    )
    out_specs = P(("group", "out"), "inp")
    return jax.shard_map(
        functools.partial(on_device, n=mesh.shape["inp"]),
        mesh=mesh,
        in_specs=in_specs,
        out_specs=out_specs,
        check_vma=False,
    )
```

time: 301 us -> 140 us (0.47)
  blocking collectives: 221 us -> 0 us
  Pallas kernels: 0 us -> 42.3 us
  matrix products: 33.9 us -> 0 us
  starting transfers between devices: 0.04 us -> 31.6 us
  waiting for transfers between devices: 28.6 us -> 57.4 us
  between operations: 14.1 us -> 0.91 us
  local copies, waits for them, and re-layouts: 0.01 us -> 6.56 us
    psum x1 -> x0, blocking collectives: 221 us -> none  [on_device(): grad_rot = lax.psum(grad_part, 'inp').astype(jnp.bfloat16)]
    ppermute x0 -> x25, waiting for transfers between devices: none -> 57.4 us  [the longest x22 57.1 us: swap(): lax.ppermute(x, 'inp', [(index, index ^ 1 << bit) for index in range(n)])]
    pallas_call x0 -> x25, Pallas kernels: none -> 42.3 us  [the longest x6 33.2 us: rotate(): pl.pallas_call(kernel, grid_spec=pltpu.PrefetchScalarGridSpec(num_scalar_...]
    dot_general x3 -> x0, matrix products: 33.9 us -> none  [the longest x1 22.9 us: on_device(): lax.dot_general(basis_a, flat_acts, contract, preferred_element_type=jnp....]
    ppermute x0 -> x25, starting transfers between devices: none -> 31.6 us  [the longest x22 31.3 us: swap(): lax.ppermute(x, 'inp', [(index, index ^ 1 << bit) for index in range(n)])]
    reduce_scatter x2 -> x0, waiting for transfers between devices: 28.6 us -> none  [the longest x1 15.7 us: on_device(): lax.psum_scatter(lax.dot_general(basis_a, flat_acts, contract, preferred_...]
    unnamed x2 -> x16, local copies, waits for them, and re-layouts: 0.01 us -> 6.41 us
    div x1 -> x0, other arithmetic: 3.14 us -> none  [on_device(): lax.psum_scatter(summed, 'out', scatter_dimension=0, tiled=True) / SEQS]
  transfers between devices with their start and end apart: 2 -> 25, of which waited for: 2 -> 12; matrix products, arithmetic and copies ran while one was open for 2% -> 0% of each run, Pallas kernels for 0% -> 27%
where the time goes in v2:
time: 140 us
  waiting for transfers between devices  57.4 us (41%)
  Pallas kernels  42.3 us (30%)
  starting transfers between devices  31.6 us (23%)
  local copies, waits for them, and re-layouts  6.56 us (5%)
    ppermute x22, waiting for transfers between devices, swap(): lax.ppermute(x, 'inp', [(index, index ^ 1 << bit) for index in range(n)])  57.1 us
    pallas_call x6, Pallas kernels, rotate(): pl.pallas_call(kernel, grid_spec=pltpu.PrefetchScalarGridSpec(num_scalar_...  33.2 us
    ppermute x22, starting transfers between devices, swap(): lax.ppermute(x, 'inp', [(index, index ^ 1 << bit) for index in range(n)])  31.3 us
    pallas_call x19, Pallas kernels, call(): pl.pallas_call(kernel, out_shape=out_shape, in_specs=list(specs) + [ANY]...  9.14 us
    unnamed x16, local copies, waits for them, and re-layouts  6.41 us
  transfers between devices with their start and end apart: 25, of which 12 were waited for; matrix products, arithmetic and copies ran while one was open for 0% of the time, Pallas kernels for 27%

profile of v2, /device:TPU:0, one launch (start us, length us, event | category | flops | bytes accessed | tf_op | source)
XLA Modules:
  0.0 139.5 jit_solution(15709458592396519801)
XLA Ops:
  0.7 2.2 %copy-done = bf16[1024,2048]{1,0:T(8,128)(2,1)S(1)} copy-done((bf16[1024,2048]{1,0:T(8,128)(2,1)S(1)}, bf16[1024,2048]{1,0:T(8,128)(2,1)}, u32[]{:S(2)}) %copy-start) | copy-done | bytes 4194328
  4.1 2.7 %shard_map.73 = (bf16[4,256,256]{2,1,0:T(8,128)(2,1)S(1)}, bf16[4,256,256]{2,1,0:T(8,128)(2,1)S(1)}) custom-call(s32[4]{0:T(128)S(1)} %get-tuple-element.82.order_ref, bf16[512,1024]{1,0:T(8,128)(2,1)S(1)} %bitcast.8, bf16[1024,2048]{1,0:T(8,128)(2,1)S(1)} %copy-done, bf16[1024,2048]{1,0:T(8,128)(2,1)S(1)} %copy-done, bf16[1024,2048]{1,0:T(8,128)(2,1)S(1)} %copy-done, ...), custom_call_target="tpu_custom_call" | custom-call | tf_op jit(solution)/shard_map/pallas_call | solution.py:88
  6.8 3.0 %collective-permute-start = (bf16[4,256,256]{2,1,0:T(8,128)(2,1)S(1)}, bf16[4,256,256]{2,1,0:T(8,128)(2,1)S(1)}, u32[]{:S(2)}, u32[]{:S(2)}) collective-permute-start(bf16[4,256,256]{2,1,0:T(8,128)(2,1)S(1)} %get-tuple-element.43.refs_4_), channel_id=1, source_target_pairs={{0,2},{2,0},{4,6},{6,4},{8,10},{10,8},{12,14},{14,12},{1,3},{3,1},... | collective-permute-start | bytes 1572872 | tf_op jit(solution)/shard_map/ppermute | solution.py:247
  9.9 2.7 %shard_map.74 = (f32[4,256,256]{2,1,0:T(8,128)S(1)}, f32[4,256,256]{2,1,0:T(8,128)S(1)}) custom-call(s32[4]{0:T(128)S(1)} %get-tuple-element.81.order_ref, bf16[512,1024]{1,0:T(8,128)(2,1)S(1)} %bitcast.9, bf16[1024,2048]{1,0:T(8,128)(2,1)S(1)} %copy-done.1, bf16[1024,2048]{1,0:T(8,128)(2,1)S(1)} %copy-done.1, bf16[1024,2048]{1,0:T(8,128)(2,1)S(1)} %copy-done.1, ...), custom_call_target="tpu_custom_call" | custom-call | tf_op jit(solution)/shard_map/pallas_call | solution.py:88
  12.6 6.8 %shard_map.75 = (bf16[4,256,256]{2,1,0:T(8,128)(2,1)S(1)}, bf16[4,256,256]{2,1,0:T(8,128)(2,1)S(1)}) custom-call(s32[4]{0:T(128)S(1)} %get-tuple-element.82.order_ref, bf16[512,3584]{1,0:T(8,128)(2,1)S(1)} %bitcast.4, bf16[3584,4096]{1,0:T(8,128)(2,1)} %refs_1_.11, bf16[3584,4096]{1,0:T(8,128)(2,1)} %refs_1_.11, ...), custom_call_target="tpu_custom_call" | custom-call | tf_op jit(solution)/shard_map/pallas_call | solution.py:88
  19.4 3.2 %collective-permute-done.refs_0_ = bf16[4,256,256]{2,1,0:T(8,128)(2,1)S(1)} collective-permute-done((bf16[4,256,256]{2,1,0:T(8,128)(2,1)S(1)}, bf16[4,256,256]{2,1,0:T(8,128)(2,1)S(1)}, u32[]{:S(2)}, u32[]{:S(2)}) %collective-permute-start) | collective-permute-done | bytes 524320 | tf_op jit(solution)/shard_map/ppermute | solution.py:247
  22.7 2.2 %collective-permute-start.1 = (bf16[2,256,256]{2,1,0:T(8,128)(2,1)S(1)}, bf16[2,256,256]{2,1,0:T(8,128)(2,1)S(1)}, u32[]{:S(2)}, u32[]{:S(2)}) collective-permute-start(bf16[2,256,256]{2,1,0:T(8,128)(2,1)S(1)} %get-tuple-element.46.refs_2_), channel_id=1, source_target_pairs={{0,4},{2,6},{4,0},{6,2},{8,12},{10,14},{12,8},{14,10},{1,5},{3,7},... | collective-permute-start | bytes 786440 | tf_op jit(solution)/shard_map/ppermute | solution.py:247
  26.4 7.5 %shard_map.77 = (bf16[4,256,256]{2,1,0:T(8,128)(2,1)S(1)}, bf16[4,256,256]{2,1,0:T(8,128)(2,1)}) custom-call(s32[4]{0:T(128)S(1)} %get-tuple-element.82.order_ref, bf16[512,3584]{1,0:T(8,128)(2,1)S(1)} %bitcast.5, bf16[3584,4096]{1,0:T(8,128)(2,1)} %refs_1_.11, bf16[3584,4096]{1,0:T(8,128)(2,1)} %refs_1_.11, bf16[2,256,256]{2,1,0:T(8,128)(2,1)S(1)} %get-tuple-element.46.refs_2_), custom_call_target="tpu_custom_call" | custom-call | tf_op jit(solution)/shard_map/pallas_call | solution.py:88
  34.0 2.1 %collective-permute-start.4 = (bf16[2,256,256]{2,1,0:T(8,128)(2,1)S(1)}, bf16[2,256,256]{2,1,0:T(8,128)(2,1)S(1)}, u32[]{:S(2)}, u32[]{:S(2)}) collective-permute-start(bf16[2,256,256]{2,1,0:T(8,128)(2,1)S(1)} %get-tuple-element.51.refs_2_), channel_id=1, source_target_pairs={{0,4},{2,6},{4,0},{6,2},{8,12},{10,14},{12,8},{14,10},{1,5},{3,7},... | collective-permute-start | bytes 786440 | tf_op jit(solution)/shard_map/ppermute | solution.py:247
  37.7 2.6 %collective-permute-start.3 = (f32[1,256,256]{2,1,0:T(8,128)S(1)}, f32[1,256,256]{2,1,0:T(8,128)S(1)}, u32[]{:S(2)}, u32[]{:S(2)}) collective-permute-start(f32[1,256,256]{2,1,0:T(8,128)S(1)} %get-tuple-element.52.refs_2_), channel_id=1, source_target_pairs={{0,8},{2,10},{4,12},{6,14},{8,0},{10,2},{12,4},{14,6},{1,9},{3,11}... | collective-permute-start | bytes 786440 | tf_op jit(solution)/shard_map/ppermute | solution.py:247
  40.3 6.8 %shard_map.80 = (f32[4,256,256]{2,1,0:T(8,128)S(1)}, f32[4,256,256]{2,1,0:T(8,128)S(1)}) custom-call(s32[4]{0:T(128)S(1)} %get-tuple-element.81.order_ref, bf16[512,3584]{1,0:T(8,128)(2,1)S(1)} %bitcast.6, bf16[3584,4096]{1,0:T(8,128)(2,1)} %refs_1_.11, bf16[3584,4096]{1,0:T(8,128)(2,1)} %refs_1_.11, f32[1,256,256]{2,1,0:T(8,128)S(1)} %get-tuple-element.52.refs_2_), custom_call_target="tpu_custom_call" | custom-call | tf_op jit(solution)/shard_map/pallas_call | solution.py:88
  51.5 4.9 %collective-permute-done.8.refs_0_ = bf16[4,256,256]{2,1,0:T(8,128)(2,1)S(1)} collective-permute-done((bf16[4,256,256]{2,1,0:T(8,128)(2,1)S(1)}, bf16[4,256,256]{2,1,0:T(8,128)(2,1)S(1)}, u32[]{:S(2)}, u32[]{:S(2)}) %collective-permute-start.8) | collective-permute-done | bytes 524320 | tf_op jit(solution)/shard_map/ppermute | solution.py:247
  58.1 2.9 %collective-permute-done.5.refs_4_.refs_2_ = f32[1,256,256]{2,1,0:T(8,128)S(1)} collective-permute-done((f32[1,256,256]{2,1,0:T(8,128)S(1)}, f32[1,256,256]{2,1,0:T(8,128)S(1)}, u32[]{:S(2)}, u32[]{:S(2)}) %collective-permute-start.5) | collective-permute-done | bytes 262176 | tf_op jit(solution)/shard_map/ppermute | solution.py:247
  65.0 3.0 %collective-permute-start.13 = (bf16[1,256,256]{2,1,0:T(8,128)(2,1)S(1)}, bf16[1,256,256]{2,1,0:T(8,128)(2,1)S(1)}, u32[]{:S(2)}, u32[]{:S(2)}) collective-permute-start(bf16[1,256,256]{2,1,0:T(8,128)(2,1)S(1)} %get-tuple-element.63.refs_5_), channel_id=1, source_target_pairs={{0,8},{2,10},{4,12},{6,14},{8,0},{10,2},{12,4},{14,6},{1,9},{3,11}... | collective-permute-start | bytes 393224 | tf_op jit(solution)/shard_map/ppermute | solution.py:247
  71.4 6.8 %shard_map.87 = (f32[4,256,256]{2,1,0:T(8,128)S(1)}, f32[4,256,256]{2,1,0:T(8,128)S(1)}) custom-call(s32[4]{0:T(128)S(1)} %get-tuple-element.81.order_ref, bf16[512,3584]{1,0:T(8,128)(2,1)S(1)} %bitcast.7, bf16[3584,4096]{1,0:T(8,128)(2,1)} %refs_1_.11, bf16[3584,4096]{1,0:T(8,128)(2,1)} %refs_1_.11, bf16[1,2,128,512]{3,2,1,0:T(8,128)(2,1)S(1)} %shard_map.86.refs_2_.refs_0_), custom_call_target="tpu_custom_call" | custom-call | tf_op jit(solution)/shard_map/pallas_call | solution.py:88
  78.2 2.6 %collective-permute-done.13.refs_4_.refs_0_ = bf16[1,256,256]{2,1,0:T(8,128)(2,1)S(1)} collective-permute-done((bf16[1,256,256]{2,1,0:T(8,128)(2,1)S(1)}, bf16[1,256,256]{2,1,0:T(8,128)(2,1)S(1)}, u32[]{:S(2)}, u32[]{:S(2)}) %collective-permute-start.13) | collective-permute-done | bytes 131104 | tf_op jit(solution)/shard_map/ppermute | solution.py:247
  82.0 2.9 %collective-permute-start.16 = (bf16[1,256,256]{2,1,0:T(8,128)(2,1)S(1)}, bf16[1,256,256]{2,1,0:T(8,128)(2,1)S(1)}, u32[]{:S(2)}, u32[]{:S(2)}) collective-permute-start(bf16[1,256,256]{2,1,0:T(8,128)(2,1)S(1)} %get-tuple-element.69.refs_2_), channel_id=1, source_target_pairs={{0,8},{2,10},{4,12},{6,14},{8,0},{10,2},{12,4},{14,6},{1,9},{3,11}... | collective-permute-start | bytes 393224 | tf_op jit(solution)/shard_map/ppermute | solution.py:247
  86.6 4.9 %collective-permute-done.16.refs_4_.refs_1_ = bf16[1,256,256]{2,1,0:T(8,128)(2,1)S(1)} collective-permute-done((bf16[1,256,256]{2,1,0:T(8,128)(2,1)S(1)}, bf16[1,256,256]{2,1,0:T(8,128)(2,1)S(1)}, u32[]{:S(2)}, u32[]{:S(2)}) %collective-permute-start.16) | collective-permute-done | bytes 131104 | tf_op jit(solution)/shard_map/ppermute | solution.py:247
  91.5 3.1 %collective-permute-done.17.refs_3_.refs_0_ = bf16[2,256,256]{2,1,0:T(8,128)(2,1)S(1)} collective-permute-done((bf16[2,256,256]{2,1,0:T(8,128)(2,1)S(1)}, bf16[2,256,256]{2,1,0:T(8,128)(2,1)S(1)}, u32[]{:S(2)}, u32[]{:S(2)}) %collective-permute-start.17) | collective-permute-done | bytes 262176 | tf_op jit(solution)/shard_map/ppermute | solution.py:247
  96.8 2.4 %collective-permute-start.20 = (bf16[1,256,256]{2,1,0:T(8,128)(2,1)S(1)}, bf16[1,256,256]{2,1,0:T(8,128)(2,1)S(1)}, u32[]{:S(2)}, u32[]{:S(2)}) collective-permute-start(bf16[1,256,256]{2,1,0:T(8,128)(2,1)S(1)} %get-tuple-element.76.refs_4_), channel_id=1, source_target_pairs={{0,8},{2,10},{4,12},{6,14},{8,0},{10,2},{12,4},{14,6},{1,9},{3,11}... | collective-permute-start | bytes 393224 | tf_op jit(solution)/shard_map/ppermute | solution.py:247
  99.2 15.0 %collective-permute-done.21.refs_0_.refs_6_ = bf16[2,256,256]{2,1,0:T(8,128)(2,1)S(1)} collective-permute-done((bf16[2,256,256]{2,1,0:T(8,128)(2,1)S(1)}, bf16[2,256,256]{2,1,0:T(8,128)(2,1)S(1)}, u32[]{:S(2)}, u32[]{:S(2)}) %collective-permute-start.21) | collective-permute-done | bytes 262176 | tf_op jit(solution)/shard_map/ppermute | solution.py:247
  114.5 8.4 %collective-permute-done.22.refs_1_ = bf16[1,256,256]{2,1,0:T(8,128)(2,1)S(1)} collective-permute-done((bf16[1,256,256]{2,1,0:T(8,128)(2,1)S(1)}, bf16[1,256,256]{2,1,0:T(8,128)(2,1)S(1)}, u32[]{:S(2)}, u32[]{:S(2)}) %collective-permute-start.22) | collective-permute-done | bytes 131104 | tf_op jit(solution)/shard_map/ppermute | solution.py:247
  125.0 3.6 %shard_map.96.refs_6_ = f32[1024,512]{1,0:T(8,128)} custom-call(s32[6]{0:T(128)S(1)} %bitcast.10, bf16[2,2,128,512]{3,2,1,0:T(8,128)(2,1)S(1)} %shard_map.90.refs_2_.refs_1_, bf16[2,2,128,512]{3,2,1,0:T(8,128)(2,1)S(1)} %collective-permute-done.14.refs_3_.refs_2_, bf16[2,2,128,512]{3,2,1,0:T(8,128)(2,1)S(1)} %collective-permute-done.23.refs_5_.refs_3_, ...), custom_call_target="tpu_custom_call" | custom-call | tf_op jit(solution)/shard_map/pallas_call | solution.py:50
  128.6 8.8 %collective-permute-done.15.refs_1_ = bf16[2,2,128,512]{3,2,1,0:T(8,128)(2,1)S(1)} collective-permute-done((bf16[2,2,128,512]{3,2,1,0:T(8,128)(2,1)S(1)}, bf16[2,2,128,512]{3,2,1,0:T(8,128)(2,1)S(1)}, u32[]{:S(2)}, u32[]{:S(2)}) %collective-permute-start.15) | collective-permute-done | bytes 524320 | tf_op jit(solution)/shard_map/ppermute | solution.py:247
  (72 shorter events, 27.5 us)
Async XLA Ops:
  6.8 15.8 %collective-permute-start = (bf16[4,256,256]{2,1,0:T(8,128)(2,1)S(1)}, bf16[4,256,256]{2,1,0:T(8,128)(2,1)S(1)}, u32[]{:S(2)}, u32[]{:S(2)}) collective-permute-start(bf16[4,256,256]{2,1,0:T(8,128)(2,1)S(1)} %get-tuple-element.43.refs_4_), channel_id=1, source_target_pairs={{0,2},{2,0},{4,6},{6,4},{8,10},{10,8},{12,14},{14,12},{1,3},{3,1},... | collective-permute-start | bytes 1572872 | tf_op jit(solution)/shard_map/ppermute | solution.py:247
  9.9 24.0 %collective-permute-start.2 = (bf16[4,256,256]{2,1,0:T(8,128)(2,1)S(1)}, bf16[4,256,256]{2,1,0:T(8,128)(2,1)S(1)}, u32[]{:S(2)}, u32[]{:S(2)}) collective-permute-start(bf16[4,256,256]{2,1,0:T(8,128)(2,1)S(1)} %get-tuple-element.48), channel_id=1, source_target_pairs={{0,2},{2,0},{4,6},{6,4},{8,10},{10,8},{12,14},{14,12},{1,3},{3,1},... | collective-permute-start | bytes 1572872 | tf_op jit(solution)/shard_map/ppermute | solution.py:247
  22.7 11.2 %collective-permute-start.1 = (bf16[2,256,256]{2,1,0:T(8,128)(2,1)S(1)}, bf16[2,256,256]{2,1,0:T(8,128)(2,1)S(1)}, u32[]{:S(2)}, u32[]{:S(2)}) collective-permute-start(bf16[2,256,256]{2,1,0:T(8,128)(2,1)S(1)} %get-tuple-element.46.refs_2_), channel_id=1, source_target_pairs={{0,4},{2,6},{4,0},{6,2},{8,12},{10,14},{12,8},{14,10},{1,5},{3,7},... | collective-permute-start | bytes 786440 | tf_op jit(solution)/shard_map/ppermute | solution.py:247
  24.9 22.3 %collective-permute-start.6 = (bf16[4,256,256]{2,1,0:T(8,128)(2,1)S(1)}, bf16[4,256,256]{2,1,0:T(8,128)(2,1)S(1)}, u32[]{:S(2)}, u32[]{:S(2)}) collective-permute-start(bf16[4,256,256]{2,1,0:T(8,128)(2,1)S(1)} %get-tuple-element.45.refs_2_), channel_id=1, source_target_pairs={{0,2},{2,0},{4,6},{6,4},{8,10},{10,8},{12,14},{14,12},{1,3},{3,1},... | collective-permute-start | bytes 1572872 | tf_op jit(solution)/shard_map/ppermute | solution.py:247
  34.0 13.1 %collective-permute-start.4 = (bf16[2,256,256]{2,1,0:T(8,128)(2,1)S(1)}, bf16[2,256,256]{2,1,0:T(8,128)(2,1)S(1)}, u32[]{:S(2)}, u32[]{:S(2)}) collective-permute-start(bf16[2,256,256]{2,1,0:T(8,128)(2,1)S(1)} %get-tuple-element.51.refs_2_), channel_id=1, source_target_pairs={{0,4},{2,6},{4,0},{6,2},{8,12},{10,14},{12,8},{14,10},{1,5},{3,7},... | collective-permute-start | bytes 786440 | tf_op jit(solution)/shard_map/ppermute | solution.py:247
  36.1 20.2 %collective-permute-start.8 = (bf16[4,256,256]{2,1,0:T(8,128)(2,1)S(1)}, bf16[4,256,256]{2,1,0:T(8,128)(2,1)S(1)}, u32[]{:S(2)}, u32[]{:S(2)}) collective-permute-start(bf16[4,256,256]{2,1,0:T(8,128)(2,1)S(1)} %get-tuple-element.60), channel_id=1, source_target_pairs={{0,2},{2,0},{4,6},{6,4},{8,10},{10,8},{12,14},{14,12},{1,3},{3,1},... | collective-permute-start | bytes 1572872 | tf_op jit(solution)/shard_map/ppermute | solution.py:247
  37.7 18.6 %collective-permute-start.3 = (f32[1,256,256]{2,1,0:T(8,128)S(1)}, f32[1,256,256]{2,1,0:T(8,128)S(1)}, u32[]{:S(2)}, u32[]{:S(2)}) collective-permute-start(f32[1,256,256]{2,1,0:T(8,128)S(1)} %get-tuple-element.52.refs_2_), channel_id=1, source_target_pairs={{0,8},{2,10},{4,12},{6,14},{8,0},{10,2},{12,4},{14,6},{1,9},{3,11}... | collective-permute-start | bytes 786440 | tf_op jit(solution)/shard_map/ppermute | solution.py:247
  47.3 10.8 %collective-permute-start.7 = (bf16[2,256,256]{2,1,0:T(8,128)(2,1)S(1)}, bf16[2,256,256]{2,1,0:T(8,128)(2,1)S(1)}, u32[]{:S(2)}, u32[]{:S(2)}) collective-permute-start(bf16[2,256,256]{2,1,0:T(8,128)(2,1)S(1)} %get-tuple-element.58.refs_2_), channel_id=1, source_target_pairs={{0,4},{2,6},{4,0},{6,2},{8,12},{10,14},{12,8},{14,10},{1,5},{3,7},... | collective-permute-start | bytes 786440 | tf_op jit(solution)/shard_map/ppermute | solution.py:247
  47.8 13.2 %collective-permute-start.5 = (f32[1,256,256]{2,1,0:T(8,128)S(1)}, f32[1,256,256]{2,1,0:T(8,128)S(1)}, u32[]{:S(2)}, u32[]{:S(2)}) collective-permute-start(f32[1,256,256]{2,1,0:T(8,128)S(1)} %get-tuple-element.55.refs_2_), channel_id=1, source_target_pairs={{0,8},{2,10},{4,12},{6,14},{8,0},{10,2},{12,4},{14,6},{1,9},{3,11}... | collective-permute-start | bytes 786440 | tf_op jit(solution)/shard_map/ppermute | solution.py:247
  49.9 28.2 %collective-permute-start.12 = (bf16[4,256,256]{2,1,0:T(8,128)(2,1)S(1)}, bf16[4,256,256]{2,1,0:T(8,128)(2,1)}, u32[]{:S(2)}, u32[]{:S(2)}) collective-permute-start(bf16[4,256,256]{2,1,0:T(8,128)(2,1)S(1)} %get-tuple-element.50.refs_2_), channel_id=1, source_target_pairs={{0,2},{2,0},{4,6},{6,4},{8,10},{10,8},{12,14},{14,12},{1,3},{3,1},... | collective-permute-start | bytes 1572872 | tf_op jit(solution)/shard_map/ppermute | solution.py:247
  61.8 18.9 %collective-permute-start.11 = (bf16[2,256,256]{2,1,0:T(8,128)(2,1)}, bf16[2,256,256]{2,1,0:T(8,128)(2,1)S(1)}, u32[]{:S(2)}, u32[]{:S(2)}) collective-permute-start(bf16[2,256,256]{2,1,0:T(8,128)(2,1)} %get-tuple-element.62.refs_2_), channel_id=1, source_target_pairs={{0,4},{2,6},{4,0},{6,2},{8,12},{10,14},{12,8},{14,10},{1,5},{3,7},... | collective-permute-start | bytes 786440 | tf_op jit(solution)/shard_map/ppermute | solution.py:247
  61.8 24.7 %collective-permute-start.18 = (bf16[4,256,256]{2,1,0:T(8,128)(2,1)}, bf16[4,256,256]{2,1,0:T(8,128)(2,1)S(1)}, u32[]{:S(2)}, u32[]{:S(2)}) collective-permute-start(bf16[4,256,256]{2,1,0:T(8,128)(2,1)} %get-tuple-element.73), channel_id=1, source_target_pairs={{0,2},{2,0},{4,6},{6,4},{8,10},{10,8},{12,14},{14,12},{1,3},{3,1},... | collective-permute-start | bytes 1572872 | tf_op jit(solution)/shard_map/ppermute | solution.py:247
  64.9 3.1 %collective-permute-start.9 = (bf16[128,512]{1,0:T(8,128)(2,1)S(1)}, bf16[128,512]{1,0:T(8,128)(2,1)S(1)}, u32[]{:S(2)}, u32[]{:S(2)}) collective-permute-start(bf16[128,512]{1,0:T(8,128)(2,1)S(1)} %get-tuple-element.65), channel_id=1, source_target_pairs={{0,1},{1,0},{2,3},{3,2},{4,5},{5,4},{6,7},{7,6},{8,9},{9,8},{10,11... | collective-permute-start | bytes 393224 | tf_op jit(solution)/shard_map/ppermute | solution.py:251
  65.0 15.8 %collective-permute-start.13 = (bf16[1,256,256]{2,1,0:T(8,128)(2,1)S(1)}, bf16[1,256,256]{2,1,0:T(8,128)(2,1)S(1)}, u32[]{:S(2)}, u32[]{:S(2)}) collective-permute-start(bf16[1,256,256]{2,1,0:T(8,128)(2,1)S(1)} %get-tuple-element.63.refs_5_), channel_id=1, source_target_pairs={{0,8},{2,10},{4,12},{6,14},{8,0},{10,2},{12,4},{14,6},{1,9},{3,11}... | collective-permute-start | bytes 393224 | tf_op jit(solution)/shard_map/ppermute | solution.py:247
  68.0 18.5 %collective-permute-start.10 = (bf16[1,2,128,512]{3,2,1,0:T(8,128)(2,1)S(1)}, bf16[1,2,128,512]{3,2,1,0:T(8,128)(2,1)S(1)}, u32[]{:S(2)}, u32[]{:S(2)}) collective-permute-start(bf16[1,2,128,512]{3,2,1,0:T(8,128)(2,1)S(1)} %shard_map.86.refs_2_.refs_0_), channel_id=1, source_target_pairs={{0,8},{2,10},{4,12},{6,14},{8,0},{10,2},{12,4},{14,6},{1,9},{3,11}... | collective-permute-start | bytes 786440 | tf_op jit(solution)/shard_map/ppermute | solution.py:247
  81.9 12.7 %collective-permute-start.17 = (bf16[2,256,256]{2,1,0:T(8,128)(2,1)S(1)}, bf16[2,256,256]{2,1,0:T(8,128)(2,1)S(1)}, u32[]{:S(2)}, u32[]{:S(2)}) collective-permute-start(bf16[2,256,256]{2,1,0:T(8,128)(2,1)S(1)} %get-tuple-element.68.refs_2_), channel_id=1, source_target_pairs={{0,4},{2,6},{4,0},{6,2},{8,12},{10,14},{12,8},{14,10},{1,5},{3,7},... | collective-permute-start | bytes 786440 | tf_op jit(solution)/shard_map/ppermute | solution.py:247
  82.0 9.5 %collective-permute-start.16 = (bf16[1,256,256]{2,1,0:T(8,128)(2,1)S(1)}, bf16[1,256,256]{2,1,0:T(8,128)(2,1)S(1)}, u32[]{:S(2)}, u32[]{:S(2)}) collective-permute-start(bf16[1,256,256]{2,1,0:T(8,128)(2,1)S(1)} %get-tuple-element.69.refs_2_), channel_id=1, source_target_pairs={{0,8},{2,10},{4,12},{6,14},{8,0},{10,2},{12,4},{14,6},{1,9},{3,11}... | collective-permute-start | bytes 393224 | tf_op jit(solution)/shard_map/ppermute | solution.py:247
  86.5 27.7 %collective-permute-start.14 = (bf16[2,2,128,512]{3,2,1,0:T(8,128)(2,1)S(1)}, bf16[2,2,128,512]{3,2,1,0:T(8,128)(2,1)S(1)}, u32[]{:S(2)}, u32[]{:S(2)}) collective-permute-start(bf16[2,2,128,512]{3,2,1,0:T(8,128)(2,1)S(1)} %shard_map.90.refs_2_.refs_1_), channel_id=1, source_target_pairs={{0,4},{2,6},{4,0},{6,2},{8,12},{10,14},{12,8},{14,10},{1,5},{3,7},... | collective-permute-start | bytes 1572872 | tf_op jit(solution)/shard_map/ppermute | solution.py:247
  94.8 19.3 %collective-permute-start.19 = (f32[512,256]{1,0:T(8,128)S(1)}, f32[512,256]{1,0:T(8,128)S(1)}, u32[]{:S(2)}, u32[]{:S(2)}) collective-permute-start(f32[512,256]{1,0:T(8,128)S(1)} %shard_map.93.refs_2_.refs_4_), channel_id=1, source_target_pairs={{0,1},{1,0},{2,3},{3,2},{4,5},{5,4},{6,7},{7,6},{8,9},{9,8},{10,11... | collective-permute-start | bytes 1572872 | tf_op jit(solution)/shard_map/ppermute | solution.py:251
  94.9 19.6 %collective-permute-start.23 = (bf16[2,2,128,512]{3,2,1,0:T(8,128)(2,1)S(1)}, bf16[2,2,128,512]{3,2,1,0:T(8,128)(2,1)S(1)}, u32[]{:S(2)}, u32[]{:S(2)}) collective-permute-start(bf16[2,2,128,512]{3,2,1,0:T(8,128)(2,1)S(1)} %shard_map.90.refs_2_.refs_1_), channel_id=1, source_target_pairs={{0,2},{2,0},{4,6},{6,4},{8,10},{10,8},{12,14},{14,12},{1,3},{3,1},... | collective-permute-start | bytes 1572872 | tf_op jit(solution)/shard_map/ppermute | solution.py:247
  96.5 17.7 %collective-permute-start.21 = (bf16[2,256,256]{2,1,0:T(8,128)(2,1)S(1)}, bf16[2,256,256]{2,1,0:T(8,128)(2,1)S(1)}, u32[]{:S(2)}, u32[]{:S(2)}) collective-permute-start(bf16[2,256,256]{2,1,0:T(8,128)(2,1)S(1)} %get-tuple-element.75.refs_2_), channel_id=1, source_target_pairs={{0,4},{2,6},{4,0},{6,2},{8,12},{10,14},{12,8},{14,10},{1,5},{3,7},... | collective-permute-start | bytes 786440 | tf_op jit(solution)/shard_map/ppermute | solution.py:247
  96.8 17.8 %collective-permute-start.20 = (bf16[1,256,256]{2,1,0:T(8,128)(2,1)S(1)}, bf16[1,256,256]{2,1,0:T(8,128)(2,1)S(1)}, u32[]{:S(2)}, u32[]{:S(2)}) collective-permute-start(bf16[1,256,256]{2,1,0:T(8,128)(2,1)S(1)} %get-tuple-element.76.refs_4_), channel_id=1, source_target_pairs={{0,8},{2,10},{4,12},{6,14},{8,0},{10,2},{12,4},{14,6},{1,9},{3,11}... | collective-permute-start | bytes 393224 | tf_op jit(solution)/shard_map/ppermute | solution.py:247
  114.2 8.7 %collective-permute-start.22 = (bf16[1,256,256]{2,1,0:T(8,128)(2,1)S(1)}, bf16[1,256,256]{2,1,0:T(8,128)(2,1)S(1)}, u32[]{:S(2)}, u32[]{:S(2)}) collective-permute-start(bf16[1,256,256]{2,1,0:T(8,128)(2,1)S(1)} %get-tuple-element.78.refs_4_), channel_id=1, source_target_pairs={{0,8},{2,10},{4,12},{6,14},{8,0},{10,2},{12,4},{14,6},{1,9},{3,11}... | collective-permute-start | bytes 393224 | tf_op jit(solution)/shard_map/ppermute | solution.py:247
  123.1 14.3 %collective-permute-start.15 = (bf16[2,2,128,512]{3,2,1,0:T(8,128)(2,1)S(1)}, bf16[2,2,128,512]{3,2,1,0:T(8,128)(2,1)S(1)}, u32[]{:S(2)}, u32[]{:S(2)}) collective-permute-start(bf16[2,2,128,512]{3,2,1,0:T(8,128)(2,1)S(1)} %collective-permute-done.14.refs_3_.refs_2_), channel_id=1, source_target_pairs={{0,2},{2,0},{4,6},{6,4},{8,10},{10,8},{12,14},{14,12},{1,3},{3,1},... | collective-permute-start | bytes 1572872 | tf_op jit(solution)/shard_map/ppermute | solution.py:247
  (9 other events, 61.4 us)

commit v3 on v2

v3 whole, which is shorter than its diff:
```python
import functools

import jax
import jax.numpy as jnp
from jax import lax
from jax.experimental import pallas as pl
from jax.experimental.pallas import tpu as pltpu
from jax.sharding import PartitionSpec as P

SEQ_LEN = 512
SEQS = 2
TOKEN_CHUNKS = 2
LANES = 128
WIDTH = 256
ROUNDED_STEPS = {"g": 2, "a": 3}
ANY = pl.BlockSpec(memory_space=pl.ANY)
CODE_ROWS = 16
CODE_TOP = 2.0**15
CODE_LEAST = 2.0**-100
VMEM = pl.BlockSpec(memory_space=pltpu.VMEM)
SMEM = pl.BlockSpec(memory_space=pltpu.SMEM)
MIB = 2**20
LIGHT = pl.CostEstimate(flops=0, bytes_accessed=2**17, transcendentals=0)


SEND_AT = (9.0, 22.0)
KEEP_AT = (31.0, 46.0)
GRAD_STEPS_AT = ((17.0, 29.0), (18.0, 30.0))
ACT_STEPS_AT = ((51.0, 66.0, 76.0, 90.0), (74.0, 83.0, 89.2, 97.8))
GRADS_AT = 44.0
RELAY_WAIT = 30.0
ACROSS_WAIT = 24.0
BEHIND = {
    ("a", 0): (("g", 1), 0),
}


def decode(ref, rows):
    arrived = ref[...].astype(jnp.float32)
    if arrived.shape[1] == rows:
        return arrived
    return arrived[:, :rows] * jnp.exp2(-arrived[:, rows : rows + 1])


class Chain:
    def __init__(self):
        self.last = []
        self.clock = 0.0
        self.expected = []

    def expect(self, array, wait):
        self.expected.append((self.clock + wait, array))
        return array

    def waited_for(self):
        arrived = [array for due, array in self.expected if due <= self.clock]
        self.expected = [(due, array) for due, array in self.expected if due > self.clock]
        return self.last + arrived

    def call(self, body, out_shape, inputs, specs, out_specs=None, scratch=(), limit=12 * MIB, aliases=None, carry=()):
        unread = self.waited_for()
        deps = len(unread)

        carried = len(carry)
        aliases = dict(aliases or {})
        for at in range(carried):
            aliases[len(inputs) + deps + at] = len(out_shape) + at

        def kernel(*refs):
            rest = refs[len(inputs) + deps + carried :]
            body(*refs[: len(inputs)], *rest[: len(out_shape)], *rest[len(out_shape) + carried :])

        outs = pl.pallas_call(
            kernel,
            out_shape=list(out_shape) + [jax.ShapeDtypeStruct(x.shape, x.dtype) for x in carry],
            in_specs=list(specs) + [ANY] * (deps + carried),
            out_specs=(out_specs or [VMEM] * len(out_shape)) + [ANY] * carried,
            scratch_shapes=scratch,
            input_output_aliases=aliases,
            compiler_params=pltpu.CompilerParams(vmem_limit_bytes=limit),
            cost_estimate=LIGHT,
        )(*inputs, *unread, *carry)
        self.last = [outs[0]]
        return outs

    def rotate(self, order, x, basis, width, start, stride, per_step, chunks, dtype, limit=32 * MIB):
        tokens, features = x.shape
        count = order.shape[0]
        rows = tokens // chunks
        unread = self.waited_for()
        deps = len(unread)

        def kernel(order_ref, x_ref, *refs):
            del order_ref
            columns = jnp.concatenate([ref[...] for ref in refs[:per_step]], axis=1)
            rotated = jnp.dot(x_ref[...], columns, preferred_element_type=jnp.float32)
            for at in range(per_step):
                for chunk, ref in enumerate(refs[per_step + deps :]):
                    ref[at] = rotated[
                        chunk * rows : (chunk + 1) * rows, at * width : (at + 1) * width
                    ].astype(ref.dtype)

        def column_spec(at):
            return pl.BlockSpec(
                (features, width), lambda step, order: (0, order[step * per_step + at] * stride + start)
            )

        outs = pl.pallas_call(
            kernel,
            grid_spec=pltpu.PrefetchScalarGridSpec(
                num_scalar_prefetch=1,
                grid=(count // per_step,),
                in_specs=[pl.BlockSpec((tokens, features), lambda step, order: (0, 0))]
                + [column_spec(at) for at in range(per_step)]
                + [ANY] * deps,
                out_specs=[pl.BlockSpec((per_step, rows, width), lambda step, order: (step, 0, 0))] * chunks,
            ),
            out_shape=[jax.ShapeDtypeStruct((count, rows, width), dtype)] * chunks,
            compiler_params=pltpu.CompilerParams(vmem_limit_bytes=limit),
            cost_estimate=LIGHT,
        )(order, x, *[basis] * per_step, *unread)
        self.last = [outs[0]]
        return outs

    def combine(self, received, kept, dtype, parts=1, carry=()):
        count, rows, wide = kept.shape
        part_rows = rows // parts
        half = count // 2
        coded = dtype == jnp.float16

        def body(received_ref, kept_ref, *refs):
            arrived = decode(received_ref, rows)
            for part in range(parts):
                send_ref, hold_ref = refs[part], refs[parts + part]
                at = slice(part * part_rows, (part + 1) * part_rows)
                total = kept_ref[:half, at] + arrived[:half, at]
                hold_ref[...] = kept_ref[half:, at] + arrived[half:, at]
                if coded:
                    largest = jnp.full((half, CODE_ROWS, wide), jnp.max(jnp.abs(total)))
                    exponent = jnp.floor(jnp.log2(CODE_TOP / jnp.maximum(largest, CODE_LEAST)))
                    send_ref[:, :part_rows] = total * jnp.exp2(exponent[:, :1])
                    send_ref[:, part_rows:] = exponent
                else:
                    send_ref[...] = total.astype(send_ref.dtype)

        send_shape = (half, part_rows + CODE_ROWS * coded, wide)
        outs = self.call(
            body,
            [jax.ShapeDtypeStruct(send_shape, jnp.float32 if coded else dtype)] * parts
            + [jax.ShapeDtypeStruct((half, part_rows, wide), jnp.float32)] * parts,
            [received, kept],
            [VMEM] * 2,
            carry=carry,
        )
        return [x.astype(dtype) for x in outs[:parts]], outs[parts : 2 * parts], outs[2 * parts :]

    def finish(self, received, kept):
        rows, wide = kept[0].shape[1:]

        def body(*refs):
            out_ref = refs[-1]
            for chunk in range(TOKEN_CHUNKS):
                total = refs[TOKEN_CHUNKS + chunk][0] + refs[chunk][0].astype(jnp.float32)
                out_ref[chunk * rows : (chunk + 1) * rows] = total

        shape = jax.ShapeDtypeStruct((rows * TOKEN_CHUNKS, wide), jnp.float32)
        return self.call(body, [shape], [*received, *kept], [VMEM] * (2 * TOKEN_CHUNKS))[0]

    def finish_grads(self, scalars, received, kept):
        tokens, wide = kept[0].shape[1:]

        def body(scalars_ref, *refs):
            positions = lax.broadcasted_iota(jnp.int32, (tokens, wide), 0)
            valid = positions < scalars_ref[0]

            def grad(core):
                total = refs[2 + core][0] + decode(refs[core], tokens)[0]
                total = jnp.where(valid, total, jnp.zeros_like(total))
                return total.T.astype(jnp.bfloat16)

            mine_ref, other_ref = refs[4:]

            @pl.when(scalars_ref[1] == 0)
            def _():
                mine_ref[...] = grad(0)
                other_ref[...] = grad(1)

            @pl.when(scalars_ref[1] != 0)
            def _():
                mine_ref[...] = grad(1)
                other_ref[...] = grad(0)

        shape = jax.ShapeDtypeStruct((wide, tokens), jnp.bfloat16)
        return self.call(body, [shape] * 2, [scalars, *received, *kept], [SMEM] + [VMEM] * 4)

    def pair(self, mine, other):
        def body(mine_ref, other_ref, out_ref):
            out_ref[0, 0] = mine_ref[...]
            out_ref[0, 1] = other_ref[...]

        shape = jax.ShapeDtypeStruct((1, 2) + mine.shape, mine.dtype)
        return self.call(body, [shape], [mine, other], [VMEM] * 2)[0]

    def relay(self, x):
        def body(out_ref):
            out_ref[...] = jnp.zeros_like(out_ref)

        return self.call(body, [jax.ShapeDtypeStruct((8, LANES), jnp.float32)], [], [], carry=[x])[1]

    def moments(self, place, grads, acts, out_shape):
        rows, tokens = grads[0].shape[2:]
        count = sum(x.shape[0] for x in grads)
        blocks = len(acts)
        flat_acts = [x for block in acts for x in block]
        scale = 1.0 / SEQ_LEN**0.5

        def body(place_ref, *refs):
            grad_refs = refs[: len(grads)]
            act_refs = refs[len(grads) : len(grads) + len(flat_acts)]
            out_ref, result_ref, sems = refs[-3:]
            total = None
            for seq in range(SEQS):
                act = jnp.concatenate([act_refs[block * SEQS + seq][...] for block in range(blocks)], axis=1)
                high = act.astype(jnp.bfloat16)
                low = (act - high.astype(jnp.float32)).astype(jnp.bfloat16)
                grad = jnp.concatenate([ref[:, seq].reshape(-1, tokens) for ref in grad_refs], axis=0)
                rotated = jnp.dot(grad, high, preferred_element_type=jnp.float32)
                rotated = rotated + jnp.dot(grad, low, preferred_element_type=jnp.float32)
                rotated = rotated * scale
                squared = rotated * rotated
                total = squared if total is None else total + squared
            result_ref[...] = total / SEQS
            copies = []
            for at in range(count):
                start = pl.multiple_of(place_ref[at] * rows, rows)
                copies.append(
                    pltpu.make_async_copy(
                        result_ref.at[pl.ds(at * rows, rows)], out_ref.at[pl.ds(start, rows)], sems.at[at]
                    )
                )
                copies[-1].start()
            for copy in copies:
                copy.wait()

        inputs = [place, *grads, *flat_acts]
        specs = [SMEM] + [VMEM] * (len(inputs) - 1)
        return self.call(
            body,
            [out_shape],
            inputs,
            specs,
            out_specs=[ANY],
            scratch=[
                pltpu.VMEM((count * rows, out_shape.shape[1]), jnp.float32),
                pltpu.SemaphoreType.DMA((count,)),
            ],
            limit=24 * MIB,
        )[0]


def rotate_narrow(order, x, basis, width, start, slices, dtype):
    columns = basis[:, start * width : (start + slices) * width]
    rotated = jnp.dot(x, columns, preferred_element_type=jnp.float32)
    rotated = rotated.reshape(x.shape[0], slices, width).transpose(1, 0, 2)
    return [jnp.take(rotated, order, axis=0).astype(dtype)]


def halving_order(n, steps):
    bits = len(steps)
    return [
        sum((1 - ((at >> (bits - 1 - step)) & 1)) << bit for step, bit in enumerate(steps)) for at in range(n)
    ]


def swap(x, n, bit):
    return lax.ppermute(x, "inp", [(index, index ^ (1 << bit)) for index in range(n)])


def swap_cores(x):
    return lax.ppermute(x, "out", [(0, 1), (1, 0)])


def on_device(acts, grads, basis_a, basis_g, lengths, *, n):
    bits = n.bit_length() - 1
    me = lax.axis_index("inp")
    core = lax.axis_index("out")
    scalars = jnp.stack([lengths[0], core]).astype(jnp.int32)
    x_a, x_g = acts[0], grads[0]
    width_a = basis_a.shape[1] // n
    width_g = basis_g.shape[1] // n // 2
    wide = min(WIDTH, width_a)
    blocks = width_a // wide
    chain = Chain()

    forward = list(range(bits))
    crossed = [1, 0] + forward[2:]
    grad_keys = [("g", 0), ("g", 1)]
    act_keys = [("a", block) for block in range(blocks)]
    steps_of = {key: forward for key in grad_keys + act_keys}
    steps_of["g", 0] = crossed
    orders = {}
    for steps in (forward, crossed):
        order = jnp.array(halving_order(n, steps), jnp.int32) ^ me
        orders[tuple(steps)] = (order[: n // 2], order[n // 2 :])
    kept, received, finished, gathered = {}, {}, {}, {}
    waiting, worked = {}, set()

    def at_work(task):
        return task not in worked

    def keep_or_send(key, x, part):
        if part == 0 and key in BEHIND and at_work(BEHIND[key]):
            waiting.setdefault(BEHIND[key], []).append((key, x))
        elif part == 0:
            received[key] = swap(x, n, steps_of[key][0])
        else:
            kept[key] = x

    def rotate_grads(half, part):
        key = ("g", half)
        order = orders[tuple(steps_of[key])][part]
        dtype = (jnp.bfloat16, jnp.float32)[part]
        if width_g % LANES == 0:
            (x,) = chain.rotate(order, x_g, basis_g, width_g, half * n, 1, order.shape[0] // 2, 1, dtype)
        else:
            (x,) = rotate_narrow(order, x_g, basis_g, width_g, half * n, n, dtype)
        keep_or_send(key, x, part)

    def rotate_acts(block, part):
        order = orders[tuple(forward)][part]
        dtype = (jnp.bfloat16, jnp.float32)[part]
        (x,) = chain.rotate(order, x_a, basis_a, wide, block, blocks, 2, 1, dtype)
        keep_or_send(("a", block), x, part)

    def advance(key, step, chunk=None):
        worked.add((key, step))
        wider = jnp.float16 if key[0] == "g" else jnp.float32
        dtype = jnp.bfloat16 if step + 1 < ROUNDED_STEPS[key[0]] else wider
        behind = waiting.pop((key, step), [])
        split = TOKEN_CHUNKS if key[0] == "a" and step == 0 else 1
        name = key if chunk is None else key + (chunk,)
        sends, holds, carried = chain.combine(received[name], kept[name], dtype, split, [x for _, x in behind])
        for (other, _), x in zip(behind, carried):
            received[other] = swap(x, n, steps_of[other][0])
        for part in range(split):
            name = key + (part,) if split > 1 else name
            arrived = swap(sends[part], n, steps_of[key][step + 1])
            received[name] = arrived.astype(jnp.float32) if dtype == jnp.float16 else arrived
            kept[name] = holds[part]

    def finish_acts(block):
        keys = [("a", block, chunk) for chunk in range(TOKEN_CHUNKS)]
        own = chain.finish([received[key] for key in keys], [kept[key] for key in keys])
        finished[block] = (own, chain.expect(swap_cores(own), 4.0))

    def finish_grads():
        mine, other = chain.finish_grads(
            scalars, [received[key] for key in grad_keys], [kept[key] for key in grad_keys]
        )
        gathered["mine"], gathered["other"] = mine, swap_cores(other)

    def pair_grads():
        held = chain.pair(gathered["mine"], gathered["other"])
        sides = [[at for at in range(n) if at % 2 == side] for side in range(2)]
        gathered["held"] = lax.all_gather(held, "inp", axis_index_groups=sides, tiled=True)

    def relay_grads():
        gathered["held"] = chain.relay(gathered["held"])
        gathered["across"] = chain.expect(swap(gathered["held"], n, 0), ACROSS_WAIT)

    tasks = [
        (0.0, rotate_grads, (0, 0)),
        (1.0, rotate_grads, (1, 0)),
        (2.0, rotate_grads, (0, 1)),
        (3.0, rotate_grads, (1, 1)),
    ]
    for block in range(blocks):
        tasks.append((SEND_AT[block], rotate_acts, (block, 0)))
        tasks.append((KEEP_AT[block], rotate_acts, (block, 1)))
    for key, times in zip(grad_keys, GRAD_STEPS_AT):
        for step in range(bits - 1):
            tasks.append((times[min(step, 1)] + 8.0 * max(step - 1, 0), advance, (key, step)))
    for key, times in zip(act_keys, ACT_STEPS_AT):
        tasks.append((times[0], advance, (key, 0)))
        for step in range(1, bits - 1):
            for chunk in range(TOKEN_CHUNKS):
                tasks.append((times[1 + chunk] + 8.0 * (step - 1), advance, (key, step, chunk)))
        tasks.append((times[-1] + 8.0 * (bits - 3), finish_acts, (key[1],)))
    clock = GRADS_AT + 8.0 * (bits - 3)
    tasks.append((clock, finish_grads, ()))
    clock += 1.0
    tasks.append((clock, pair_grads, ()))
    tasks.append((clock + RELAY_WAIT, relay_grads, ()))
    for chain.clock, task, arguments in sorted(tasks, key=lambda task: task[0]):
        task(*arguments)

    same_side = 2 * jnp.arange(n // 2, dtype=jnp.int32) + me % 2
    place = jnp.concatenate([same_side, same_side ^ 1])
    act_blocks = [finished[block] for block in range(blocks)]
    out_shape = jax.ShapeDtypeStruct((n * width_g, width_a), jnp.float32)
    grads = [gathered[name] for name in ("held", "across")]
    return chain.moments(place, grads, act_blocks, out_shape)


def solution(mesh):
    in_specs = (
        P(("group", "out"), None, "inp"),
        P(("group", "out"), None, "inp"),
        P(("group", "inp"), None),
        P(("group", "inp"), None),
        P(("group", "out")),
    )
    out_specs = P(("group", "out"), "inp")
    return jax.shard_map(
        functools.partial(on_device, n=mesh.shape["inp"]),
        mesh=mesh,
        in_specs=in_specs,
        out_specs=out_specs,
        check_vma=False,
    )
```

time: 140 us -> 165 us (1.18)
  between operations: 0.91 us -> 14.3 us
  waiting for transfers between devices: 57.4 us -> 68.1 us
  starting transfers between devices: 31.6 us -> 22.4 us
  local copies, waits for them, and re-layouts: 6.56 us -> 12.2 us
  other arithmetic: 0.74 us -> 3.21 us
  Pallas kernels: 42.3 us -> 44.7 us
    ppermute x22 -> x17, waiting for transfers between devices: 57.1 us -> 66.7 us  [swap(): lax.ppermute(x, 'inp', [(index, index ^ 1 << bit) for index in range(n)])]
    ppermute x22 -> x17, starting transfers between devices: 31.3 us -> 22.2 us  [swap(): lax.ppermute(x, 'inp', [(index, index ^ 1 << bit) for index in range(n)])]
    unnamed x16 -> x32, local copies, waits for them, and re-layouts: 6.41 us -> 12 us
    convert_element_type x0 -> x4, other arithmetic: none -> 2.37 us  [the longest x2 1.43 us: combine(): x.astype(dtype)]
    pallas_call x19 -> x16, Pallas kernels: 9.14 us -> 10.4 us  [call(): pl.pallas_call(kernel, out_shape=list(out_shape) + [jax.ShapeDtypeStruct(...]
    pallas_call x6 -> x8, Pallas kernels: 33.2 us -> 34.3 us  [rotate(): pl.pallas_call(kernel, grid_spec=pltpu.PrefetchScalarGridSpec(num_scalar_...]
  transfers between devices with their start and end apart: 25 -> 21, of which waited for: 12 -> 11; matrix products, arithmetic and copies ran while one was open for 0% -> 1% of each run, Pallas kernels for 27% -> 21%
where the time goes in v3:
time: 165 us
  waiting for transfers between devices  68.1 us (41%)
  Pallas kernels  44.7 us (27%)
  starting transfers between devices  22.4 us (14%)
  between operations  14.3 us (9%)
  local copies, waits for them, and re-layouts  12.2 us (7%)
  other arithmetic  3.21 us (2%)
    ppermute x17, waiting for transfers between devices, swap(): lax.ppermute(x, 'inp', [(index, index ^ 1 << bit) for index in range(n)])  66.7 us
    pallas_call x8, Pallas kernels, rotate(): pl.pallas_call(kernel, grid_spec=pltpu.PrefetchScalarGridSpec(num_scalar_...  34.3 us
    ppermute x17, starting transfers between devices, swap(): lax.ppermute(x, 'inp', [(index, index ^ 1 << bit) for index in range(n)])  22.2 us
    unnamed x32, local copies, waits for them, and re-layouts  12 us
    pallas_call x16, Pallas kernels, call(): pl.pallas_call(kernel, out_shape=list(out_shape) + [jax.ShapeDtypeStruct(...  10.4 us
  transfers between devices with their start and end apart: 21, of which 11 were waited for; matrix products, arithmetic and copies ran while one was open for 1% of the time, Pallas kernels for 21%

profile of v3, /device:TPU:0, one launch (start us, length us, event | category | flops | bytes accessed | tf_op | source)
XLA Modules:
  0.0 164.9 jit_solution(1886477043215336750)
XLA Ops:
  7.3 2.2 %copy-done = bf16[1024,2048]{1,0:T(8,128)(2,1)S(1)} copy-done((bf16[1024,2048]{1,0:T(8,128)(2,1)S(1)}, bf16[1024,2048]{1,0:T(8,128)(2,1)}, u32[]{:S(2)}) %copy-start) | copy-done | bytes 4194328
  10.7 1.8 %shard_map.73.refs_2_ = bf16[4,512,128]{2,1,0:T(8,128)(2,1)S(1)} custom-call(s32[4]{0:T(128)S(1)} %get-tuple-element.64.order_ref, bf16[512,1024]{1,0:T(8,128)(2,1)S(1)} %bitcast.7, bf16[1024,2048]{1,0:T(8,128)(2,1)S(1)} %copy-done, bf16[1024,2048]{1,0:T(8,128)(2,1)S(1)} %copy-done), custom_call_target="tpu_custom_call" | custom-call | bytes 131072 | tf_op jit(solution)/shard_map/pallas_call | solution.py:108
  12.5 3.1 %collective-permute-start.1 = (bf16[4,512,128]{2,1,0:T(8,128)(2,1)S(1)}, bf16[4,512,128]{2,1,0:T(8,128)(2,1)S(1)}, u32[]{:S(2)}, u32[]{:S(2)}) collective-permute-start(bf16[4,512,128]{2,1,0:T(8,128)(2,1)S(1)} %shard_map.73.refs_2_), channel_id=1, source_target_pairs={{0,4},{2,6},{4,0},{6,2},{8,12},{10,14},{12,8},{14,10},{1,5},{3,7},... | collective-permute-start | bytes 1572872 | tf_op jit(solution)/shard_map/ppermute | solution.py:276
  15.7 1.8 %shard_map.74.refs_2_ = bf16[4,512,128]{2,1,0:T(8,128)(2,1)S(1)} custom-call(s32[4]{0:T(128)S(1)} %get-tuple-element.66.order_ref, bf16[512,1024]{1,0:T(8,128)(2,1)S(1)} %bitcast.8, bf16[1024,2048]{1,0:T(8,128)(2,1)S(1)} %copy-done.1, bf16[1024,2048]{1,0:T(8,128)(2,1)S(1)} %copy-done.1, bf16[4,512,128]{2,1,0:T(8,128)(2,1)S(1)} %shard_map.73.refs_2_), custom_call_target="tpu_custom_call" | custom-call | bytes 131072 | tf_op jit(solution)/shard_map/pallas_call | solution.py:108
  19.0 1.8 %shard_map.75.refs_2_.refs_1_ = f32[4,512,128]{2,1,0:T(8,128)S(1)} custom-call(s32[4]{0:T(128)S(1)} %get-tuple-element.63.order_ref, bf16[512,1024]{1,0:T(8,128)(2,1)S(1)} %bitcast.9, bf16[1024,2048]{1,0:T(8,128)(2,1)S(1)} %copy-done.1, bf16[1024,2048]{1,0:T(8,128)(2,1)S(1)} %copy-done.1, bf16[4,512,128]{2,1,0:T(8,128)(2,1)S(1)} %shard_map.74.refs_2_), custom_call_target="tpu_custom_call" | custom-call | bytes 131072 | tf_op jit(solution)/shard_map/pallas_call | solution.py:108
  20.8 1.8 %shard_map.76.refs_2_.refs_1_ = f32[4,512,128]{2,1,0:T(8,128)S(1)} custom-call(s32[4]{0:T(128)S(1)} %get-tuple-element.65.order_ref, bf16[512,1024]{1,0:T(8,128)(2,1)S(1)} %bitcast.10, bf16[1024,2048]{1,0:T(8,128)(2,1)S(1)} %copy-done.1, bf16[1024,2048]{1,0:T(8,128)(2,1)S(1)} %copy-done.1, f32[4,512,128]{2,1,0:T(8,128)S(1)} %shard_map.75.refs_2_.refs_1_), custom_call_target="tpu_custom_call" | custom-call | bytes 131072 | tf_op jit(solution)/shard_map/pallas_call | solution.py:108
  22.9 6.8 %shard_map.77.refs_2_.refs_3_ = bf16[4,512,256]{2,1,0:T(8,128)(2,1)S(1)} custom-call(s32[4]{0:T(128)S(1)} %get-tuple-element.66.order_ref, bf16[512,3584]{1,0:T(8,128)(2,1)S(1)} %bitcast.3, bf16[3584,4096]{1,0:T(8,128)(2,1)} %refs_1_.15, bf16[3584,4096]{1,0:T(8,128)(2,1)} %refs_1_.15, f32[4,512,128]{2,1,0:T(8,128)S(1)} %shard_map.76.refs_2_.refs_1_), custom_call_target="tpu_custom_call" | custom-call | bytes 131072 | tf_op jit(solution)/shard_map/pallas_call | solution.py:108
  31.6 6.8 %shard_map.80.refs_2_ = bf16[4,512,256]{2,1,0:T(8,128)(2,1)S(1)} custom-call(s32[4]{0:T(128)S(1)} %get-tuple-element.66.order_ref, bf16[512,3584]{1,0:T(8,128)(2,1)S(1)} %bitcast.4, bf16[3584,4096]{1,0:T(8,128)(2,1)} %refs_1_.15, bf16[3584,4096]{1,0:T(8,128)(2,1)} %refs_1_.15, bf16[2,512,128]{2,1,0:T(8,128)(2,1)S(1)} %get-tuple-element.35.refs_2_), custom_call_target="tpu_custom_call" | custom-call | bytes 131072 | tf_op jit(solution)/shard_map/pallas_call | solution.py:108
  40.6 2.6 %collective-permute-start.6 = (f16[1,528,128]{2,1,0:T(8,128)(2,1)}, f16[1,528,128]{2,1,0:T(8,128)(2,1)S(1)}, u32[]{:S(2)}, u32[]{:S(2)}) collective-permute-start(f16[1,528,128]{2,1,0:T(8,128)(2,1)} %convert_element_type.14), channel_id=1, source_target_pairs={{0,8},{2,10},{4,12},{6,14},{8,0},{10,2},{12,4},{14,6},{1,9},{3,11}... | collective-permute-start | bytes 405512 | tf_op jit(solution)/shard_map/ppermute | solution.py:276
  45.0 2.0 %copy-done.3 = bf16[1,512,3584]{2,1,0:T(8,128)(2,1)S(1)} copy-done((bf16[1,512,3584]{2,1,0:T(8,128)(2,1)S(1)}, bf16[1,512,3584]{2,1,0:T(8,128)(2,1)}, u32[]{:S(2)}) %copy-start.3) | copy-done | bytes 3670040
  47.0 6.8 %shard_map.83.refs_5_.refs_1_ = f32[4,512,256]{2,1,0:T(8,128)S(1)} custom-call(s32[4]{0:T(128)S(1)} %get-tuple-element.65.order_ref, bf16[512,3584]{1,0:T(8,128)(2,1)S(1)} %bitcast.5, bf16[3584,4096]{1,0:T(8,128)(2,1)} %refs_1_.15, bf16[3584,4096]{1,0:T(8,128)(2,1)} %refs_1_.15, f32[1,528,128]{2,1,0:T(8,128)S(1)} %get-tuple-element.39.refs_2_), custom_call_target="tpu_custom_call" | custom-call | bytes 131072 | tf_op jit(solution)/shard_map/pallas_call | solution.py:108
  60.8 2.0 %copy-done.4 = bf16[1,512,3584]{2,1,0:T(8,128)(2,1)S(1)} copy-done((bf16[1,512,3584]{2,1,0:T(8,128)(2,1)S(1)}, bf16[1,512,3584]{2,1,0:T(8,128)(2,1)}, u32[]{:S(2)}) %copy-start.4) | copy-done | bytes 3670040
  62.9 6.8 %shard_map.86.refs_2_.refs_1_ = f32[4,512,256]{2,1,0:T(8,128)S(1)} custom-call(s32[4]{0:T(128)S(1)} %get-tuple-element.65.order_ref, bf16[512,3584]{1,0:T(8,128)(2,1)S(1)} %bitcast.6, bf16[3584,4096]{1,0:T(8,128)(2,1)} %refs_1_.15, bf16[3584,4096]{1,0:T(8,128)(2,1)} %refs_1_.15, bf16[1,2,128,512]{3,2,1,0:T(8,128)(2,1)} %shard_map.85.refs_2_), custom_call_target="tpu_custom_call" | custom-call | bytes 131072 | tf_op jit(solution)/shard_map/pallas_call | solution.py:108
  69.7 15.1 %collective-permute-done.8.refs_0_ = bf16[4,512,256]{2,1,0:T(8,128)(2,1)S(1)} collective-permute-done((bf16[4,512,256]{2,1,0:T(8,128)(2,1)S(1)}, bf16[4,512,256]{2,1,0:T(8,128)(2,1)S(1)}, u32[]{:S(2)}, u32[]{:S(2)}) %collective-permute-start.8) | collective-permute-done | bytes 1048608 | tf_op jit(solution)/shard_map/ppermute | solution.py:276
  87.7 7.2 %collective-permute-done.9.refs_0_ = bf16[2,256,256]{2,1,0:T(8,128)(2,1)S(1)} collective-permute-done((bf16[2,256,256]{2,1,0:T(8,128)(2,1)S(1)}, bf16[2,256,256]{2,1,0:T(8,128)(2,1)S(1)}, u32[]{:S(2)}, u32[]{:S(2)}) %collective-permute-start.9) | collective-permute-done | bytes 262176 | tf_op jit(solution)/shard_map/ppermute | solution.py:276
  95.0 11.5 %collective-permute-done.2.refs_0_ = bf16[4,512,256]{2,1,0:T(8,128)(2,1)S(1)} collective-permute-done((bf16[4,512,256]{2,1,0:T(8,128)(2,1)}, bf16[4,512,256]{2,1,0:T(8,128)(2,1)S(1)}, u32[]{:S(2)}, u32[]{:S(2)}) %collective-permute-start.2) | collective-permute-done | bytes 1048608 | tf_op jit(solution)/shard_map/ppermute | solution.py:276
  109.4 1.8 %collective-permute-start.11 = (bf16[1,256,256]{2,1,0:T(8,128)(2,1)S(1)}, bf16[1,256,256]{2,1,0:T(8,128)(2,1)}, u32[]{:S(2)}, u32[]{:S(2)}) collective-permute-start(bf16[1,256,256]{2,1,0:T(8,128)(2,1)S(1)} %get-tuple-element.47.refs_2_), channel_id=1, source_target_pairs={{0,8},{2,10},{4,12},{6,14},{8,0},{10,2},{12,4},{14,6},{1,9},{3,11}... | collective-permute-start | bytes 393224 | tf_op jit(solution)/shard_map/ppermute | solution.py:276
  115.8 6.5 %collective-permute-done.15.refs_0_ = bf16[2,256,256]{2,1,0:T(8,128)(2,1)S(1)} collective-permute-done((bf16[2,256,256]{2,1,0:T(8,128)(2,1)S(1)}, bf16[2,256,256]{2,1,0:T(8,128)(2,1)S(1)}, u32[]{:S(2)}, u32[]{:S(2)}) %collective-permute-start.15) | collective-permute-done | bytes 262176 | tf_op jit(solution)/shard_map/ppermute | solution.py:276
  122.3 3.9 %collective-permute-done.14.refs_0_ = bf16[2,256,256]{2,1,0:T(8,128)(2,1)S(1)} collective-permute-done((bf16[2,256,256]{2,1,0:T(8,128)(2,1)}, bf16[2,256,256]{2,1,0:T(8,128)(2,1)S(1)}, u32[]{:S(2)}, u32[]{:S(2)}) %collective-permute-start.14) | collective-permute-done | bytes 262176 | tf_op jit(solution)/shard_map/ppermute | solution.py:276
  128.7 1.8 %collective-permute-start.18 = (bf16[1,256,256]{2,1,0:T(8,128)(2,1)S(1)}, bf16[1,256,256]{2,1,0:T(8,128)(2,1)S(1)}, u32[]{:S(2)}, u32[]{:S(2)}) collective-permute-start(bf16[1,256,256]{2,1,0:T(8,128)(2,1)S(1)} %get-tuple-element.60.refs_4_), channel_id=1, source_target_pairs={{0,8},{2,10},{4,12},{6,14},{8,0},{10,2},{12,4},{14,6},{1,9},{3,11}... | collective-permute-start | bytes 393224 | tf_op jit(solution)/shard_map/ppermute | solution.py:276
  131.6 9.9 %collective-permute-done.18.refs_1_ = bf16[1,256,256]{2,1,0:T(8,128)(2,1)S(1)} collective-permute-done((bf16[1,256,256]{2,1,0:T(8,128)(2,1)S(1)}, bf16[1,256,256]{2,1,0:T(8,128)(2,1)S(1)}, u32[]{:S(2)}, u32[]{:S(2)}) %collective-permute-start.18) | collective-permute-done | bytes 131104 | tf_op jit(solution)/shard_map/ppermute | solution.py:276
  141.5 2.0 %collective-permute-done.17.refs_0_ = bf16[1,256,256]{2,1,0:T(8,128)(2,1)S(1)} collective-permute-done((bf16[1,256,256]{2,1,0:T(8,128)(2,1)S(1)}, bf16[1,256,256]{2,1,0:T(8,128)(2,1)S(1)}, u32[]{:S(2)}, u32[]{:S(2)}) %collective-permute-start.17) | collective-permute-done | bytes 131104 | tf_op jit(solution)/shard_map/ppermute | solution.py:276
  143.8 9.2 %collective-permute-done.10.refs_2_ = bf16[4,2,128,512]{3,2,1,0:T(8,128)(2,1)} collective-permute-done((bf16[4,2,128,512]{3,2,1,0:T(8,128)(2,1)S(1)}, bf16[4,2,128,512]{3,2,1,0:T(8,128)(2,1)}, u32[]{:S(2)}, u32[]{:S(2)}) %collective-permute-start.10) | collective-permute-done | bytes 1048608 | tf_op jit(solution)/shard_map/ppermute | solution.py:276
  153.0 5.0 %shard_map.96 = f32[1024,512]{1,0:T(8,128)} custom-call(s32[8]{0:T(128)S(1)} %pad_add_fusion.refs_0_, bf16[4,2,128,512]{3,2,1,0:T(8,128)(2,1)S(1)} %copy-done.9, bf16[4,2,128,512]{3,2,1,0:T(8,128)(2,1)} %collective-permute-done.10.refs_2_, f32[512,256]{1,0:T(8,128)S(1)} %shard_map.94.refs_4_.refs_3_, f32[512,256]{1,0:T(8,128)S(1)} %collective-permute-done.16.refs_5_.refs_4_, ...), custom_call_target="tpu_custom_call" | custom-call | bytes 131072 | tf_op jit(solution)/shard_map/pallas_call | solution.py:73
  (85 shorter events, 30.4 us)
Async XLA Ops:
  6.5 104.7 %all-gather.2.cloned.1.call-start = ((), (), s32[]{:S(2)}) async-start(), calls=%async_computation | async-start | bytes 1310720 | tf_op jit(solution)/shard_map/all_gather | solution.py:365
  12.5 17.2 %collective-permute-start.1 = (bf16[4,512,128]{2,1,0:T(8,128)(2,1)S(1)}, bf16[4,512,128]{2,1,0:T(8,128)(2,1)S(1)}, u32[]{:S(2)}, u32[]{:S(2)}) collective-permute-start(bf16[4,512,128]{2,1,0:T(8,128)(2,1)S(1)} %shard_map.73.refs_2_), channel_id=1, source_target_pairs={{0,4},{2,6},{4,0},{6,2},{8,12},{10,14},{12,8},{14,10},{1,5},{3,7},... | collective-permute-start | bytes 1572872 | tf_op jit(solution)/shard_map/ppermute | solution.py:276
  17.5 13.4 %collective-permute-start = (bf16[4,512,128]{2,1,0:T(8,128)(2,1)S(1)}, bf16[4,512,128]{2,1,0:T(8,128)(2,1)S(1)}, u32[]{:S(2)}, u32[]{:S(2)}) collective-permute-start(bf16[4,512,128]{2,1,0:T(8,128)(2,1)S(1)} %shard_map.74.refs_2_), channel_id=1, source_target_pairs={{0,2},{2,0},{4,6},{6,4},{8,10},{10,8},{12,14},{14,12},{1,3},{3,1},... | collective-permute-start | bytes 1572872 | tf_op jit(solution)/shard_map/ppermute | solution.py:276
  29.8 8.6 %collective-permute-start.3 = (bf16[2,512,128]{2,1,0:T(8,128)(2,1)S(1)}, bf16[2,512,128]{2,1,0:T(8,128)(2,1)S(1)}, u32[]{:S(2)}, u32[]{:S(2)}) collective-permute-start(bf16[2,512,128]{2,1,0:T(8,128)(2,1)S(1)} %get-tuple-element.34.refs_2_), channel_id=1, source_target_pairs={{0,2},{2,0},{4,6},{6,4},{8,10},{10,8},{12,14},{14,12},{1,3},{3,1},... | collective-permute-start | bytes 786440 | tf_op jit(solution)/shard_map/ppermute | solution.py:276
  31.0 8.6 %collective-permute-start.5 = (bf16[2,512,128]{2,1,0:T(8,128)(2,1)S(1)}, bf16[2,512,128]{2,1,0:T(8,128)(2,1)S(1)}, u32[]{:S(2)}, u32[]{:S(2)}) collective-permute-start(bf16[2,512,128]{2,1,0:T(8,128)(2,1)S(1)} %get-tuple-element.35.refs_2_), channel_id=1, source_target_pairs={{0,4},{2,6},{4,0},{6,2},{8,12},{10,14},{12,8},{14,10},{1,5},{3,7},... | collective-permute-start | bytes 786440 | tf_op jit(solution)/shard_map/ppermute | solution.py:276
  40.6 13.2 %collective-permute-start.6 = (f16[1,528,128]{2,1,0:T(8,128)(2,1)}, f16[1,528,128]{2,1,0:T(8,128)(2,1)S(1)}, u32[]{:S(2)}, u32[]{:S(2)}) collective-permute-start(f16[1,528,128]{2,1,0:T(8,128)(2,1)} %convert_element_type.14), channel_id=1, source_target_pairs={{0,8},{2,10},{4,12},{6,14},{8,0},{10,2},{12,4},{14,6},{1,9},{3,11}... | collective-permute-start | bytes 405512 | tf_op jit(solution)/shard_map/ppermute | solution.py:276
  43.9 10.8 %collective-permute-start.4 = (f16[1,528,128]{2,1,0:T(8,128)(2,1)}, f16[1,528,128]{2,1,0:T(8,128)(2,1)}, u32[]{:S(2)}, u32[]{:S(2)}) collective-permute-start(f16[1,528,128]{2,1,0:T(8,128)(2,1)} %convert_element_type.12), channel_id=1, source_target_pairs={{0,8},{2,10},{4,12},{6,14},{8,0},{10,2},{12,4},{14,6},{1,9},{3,11}... | collective-permute-start | bytes 405512 | tf_op jit(solution)/shard_map/ppermute | solution.py:276
  47.0 8.6 %copy-start.15 = (f32[1,512,128]{2,1,0:T(8,128)S(1)}, f32[1,512,128]{2,1,0:T(8,128)}, u32[]{:S(2)}) copy-start(f32[1,512,128]{2,1,0:T(8,128)} %copy-done.14) | copy-start | bytes 786436
  56.6 1.4 collective-permute-start.7
  58.7 26.1 %collective-permute-start.8 = (bf16[4,512,256]{2,1,0:T(8,128)(2,1)S(1)}, bf16[4,512,256]{2,1,0:T(8,128)(2,1)S(1)}, u32[]{:S(2)}, u32[]{:S(2)}) collective-permute-start(bf16[4,512,256]{2,1,0:T(8,128)(2,1)S(1)} %get-tuple-element.44), channel_id=1, source_target_pairs={{0,2},{2,0},{4,6},{6,4},{8,10},{10,8},{12,14},{14,12},{1,3},{3,1},... | collective-permute-start | bytes 3145736 | tf_op jit(solution)/shard_map/ppermute | solution.py:276
  60.1 46.4 %collective-permute-start.2 = (bf16[4,512,256]{2,1,0:T(8,128)(2,1)}, bf16[4,512,256]{2,1,0:T(8,128)(2,1)S(1)}, u32[]{:S(2)}, u32[]{:S(2)}) collective-permute-start(bf16[4,512,256]{2,1,0:T(8,128)(2,1)} %copy-done.6), channel_id=1, source_target_pairs={{0,2},{2,0},{4,6},{6,4},{8,10},{10,8},{12,14},{14,12},{1,3},{3,1},... | collective-permute-start | bytes 3145736 | tf_op jit(solution)/shard_map/ppermute | solution.py:276
  85.7 21.7 %copy-start.10 = (f32[2,256,256]{2,1,0:T(8,128)}, f32[2,256,256]{2,1,0:T(8,128)S(1)}, u32[]{:S(2)}) copy-start(f32[2,256,256]{2,1,0:T(8,128)S(1)} %get-tuple-element.51.refs_1_) | copy-start | bytes 1572868
  85.7 9.2 %collective-permute-start.9 = (bf16[2,256,256]{2,1,0:T(8,128)(2,1)S(1)}, bf16[2,256,256]{2,1,0:T(8,128)(2,1)S(1)}, u32[]{:S(2)}, u32[]{:S(2)}) collective-permute-start(bf16[2,256,256]{2,1,0:T(8,128)(2,1)S(1)} %get-tuple-element.45.refs_2_), channel_id=1, source_target_pairs={{0,4},{2,6},{4,0},{6,2},{8,12},{10,14},{12,8},{14,10},{1,5},{3,7},... | collective-permute-start | bytes 786440 | tf_op jit(solution)/shard_map/ppermute | solution.py:276
  86.4 27.1 %collective-permute-start.12 = (bf16[2,256,256]{2,1,0:T(8,128)(2,1)}, bf16[2,256,256]{2,1,0:T(8,128)(2,1)S(1)}, u32[]{:S(2)}, u32[]{:S(2)}) collective-permute-start(bf16[2,256,256]{2,1,0:T(8,128)(2,1)} %get-tuple-element.50), channel_id=1, source_target_pairs={{0,4},{2,6},{4,0},{6,2},{8,12},{10,14},{12,8},{14,10},{1,5},{3,7},... | collective-permute-start | bytes 786440 | tf_op jit(solution)/shard_map/ppermute | solution.py:276
  107.4 14.9 %collective-permute-start.15 = (bf16[2,256,256]{2,1,0:T(8,128)(2,1)S(1)}, bf16[2,256,256]{2,1,0:T(8,128)(2,1)S(1)}, u32[]{:S(2)}, u32[]{:S(2)}) collective-permute-start(bf16[2,256,256]{2,1,0:T(8,128)(2,1)S(1)} %get-tuple-element.48.refs_0_), channel_id=1, source_target_pairs={{0,4},{2,6},{4,0},{6,2},{8,12},{10,14},{12,8},{14,10},{1,5},{3,7},... | collective-permute-start | bytes 786440 | tf_op jit(solution)/shard_map/ppermute | solution.py:276
  108.1 18.1 %collective-permute-start.14 = (bf16[2,256,256]{2,1,0:T(8,128)(2,1)}, bf16[2,256,256]{2,1,0:T(8,128)(2,1)S(1)}, u32[]{:S(2)}, u32[]{:S(2)}) collective-permute-start(bf16[2,256,256]{2,1,0:T(8,128)(2,1)} %get-tuple-element.56), channel_id=1, source_target_pairs={{0,4},{2,6},{4,0},{6,2},{8,12},{10,14},{12,8},{14,10},{1,5},{3,7},... | collective-permute-start | bytes 786440 | tf_op jit(solution)/shard_map/ppermute | solution.py:276
  109.4 16.8 %collective-permute-start.11 = (bf16[1,256,256]{2,1,0:T(8,128)(2,1)S(1)}, bf16[1,256,256]{2,1,0:T(8,128)(2,1)}, u32[]{:S(2)}, u32[]{:S(2)}) collective-permute-start(bf16[1,256,256]{2,1,0:T(8,128)(2,1)S(1)} %get-tuple-element.47.refs_2_), channel_id=1, source_target_pairs={{0,8},{2,10},{4,12},{6,14},{8,0},{10,2},{12,4},{14,6},{1,9},{3,11}... | collective-permute-start | bytes 393224 | tf_op jit(solution)/shard_map/ppermute | solution.py:276
  113.4 13.9 %copy-start.9 = (bf16[4,2,128,512]{3,2,1,0:T(8,128)(2,1)S(1)}, bf16[4,2,128,512]{3,2,1,0:T(8,128)(2,1)}, u32[]{:S(2)}) copy-start(bf16[4,2,128,512]{3,2,1,0:T(8,128)(2,1)} %copy-done.8) | copy-start | bytes 3145732
  114.6 11.6 %collective-permute-start.13 = (bf16[1,256,256]{2,1,0:T(8,128)(2,1)S(1)}, bf16[1,256,256]{2,1,0:T(8,128)(2,1)S(1)}, u32[]{:S(2)}, u32[]{:S(2)}) collective-permute-start(bf16[1,256,256]{2,1,0:T(8,128)(2,1)S(1)} %get-tuple-element.53.refs_2_), channel_id=1, source_target_pairs={{0,8},{2,10},{4,12},{6,14},{8,0},{10,2},{12,4},{14,6},{1,9},{3,11}... | collective-permute-start | bytes 393224 | tf_op jit(solution)/shard_map/ppermute | solution.py:276
  127.2 16.3 %collective-permute-start.16 = (f32[512,256]{1,0:T(8,128)S(1)}, f32[512,256]{1,0:T(8,128)S(1)}, u32[]{:S(2)}, u32[]{:S(2)}) collective-permute-start(f32[512,256]{1,0:T(8,128)S(1)} %shard_map.94.refs_4_.refs_3_), channel_id=1, source_target_pairs={{0,1},{1,0},{2,3},{3,2},{4,5},{5,4},{6,7},{7,6},{8,9},{9,8},{10,11... | collective-permute-start | bytes 1572872 | tf_op jit(solution)/shard_map/ppermute | solution.py:280
  127.3 25.7 %collective-permute-start.10 = (bf16[4,2,128,512]{3,2,1,0:T(8,128)(2,1)S(1)}, bf16[4,2,128,512]{3,2,1,0:T(8,128)(2,1)}, u32[]{:S(2)}, u32[]{:S(2)}) collective-permute-start(bf16[4,2,128,512]{3,2,1,0:T(8,128)(2,1)S(1)} %copy-done.9), channel_id=1, source_target_pairs={{0,2},{2,0},{4,6},{6,4},{8,10},{10,8},{12,14},{14,12},{1,3},{3,1},... | collective-permute-start | bytes 3145736 | tf_op jit(solution)/shard_map/ppermute | solution.py:276
  128.7 12.9 %collective-permute-start.18 = (bf16[1,256,256]{2,1,0:T(8,128)(2,1)S(1)}, bf16[1,256,256]{2,1,0:T(8,128)(2,1)S(1)}, u32[]{:S(2)}, u32[]{:S(2)}) collective-permute-start(bf16[1,256,256]{2,1,0:T(8,128)(2,1)S(1)} %get-tuple-element.60.refs_4_), channel_id=1, source_target_pairs={{0,8},{2,10},{4,12},{6,14},{8,0},{10,2},{12,4},{14,6},{1,9},{3,11}... | collective-permute-start | bytes 393224 | tf_op jit(solution)/shard_map/ppermute | solution.py:276
  130.4 13.1 %collective-permute-start.17 = (bf16[1,256,256]{2,1,0:T(8,128)(2,1)S(1)}, bf16[1,256,256]{2,1,0:T(8,128)(2,1)S(1)}, u32[]{:S(2)}, u32[]{:S(2)}) collective-permute-start(bf16[1,256,256]{2,1,0:T(8,128)(2,1)S(1)} %get-tuple-element.59.refs_2_), channel_id=1, source_target_pairs={{0,8},{2,10},{4,12},{6,14},{8,0},{10,2},{12,4},{14,6},{1,9},{3,11}... | collective-permute-start | bytes 393224 | tf_op jit(solution)/shard_map/ppermute | solution.py:276
  143.6 9.4 %collective-permute-start.19 = (f32[512,256]{1,0:T(8,128)S(1)}, f32[512,256]{1,0:T(8,128)S(1)}, u32[]{:S(2)}, u32[]{:S(2)}) collective-permute-start(f32[512,256]{1,0:T(8,128)S(1)} %shard_map.95.refs_5_.refs_7_), channel_id=1, source_target_pairs={{0,1},{1,0},{2,3},{3,2},{4,5},{5,4},{6,7},{7,6},{8,9},{9,8},{10,11... | collective-permute-start | bytes 1572872 | tf_op jit(solution)/shard_map/ppermute | solution.py:280
  (13 other events, 35.7 us)
Sparse Core Ops, SparseCore 0:
  58.9 28.7 all-gather.1

commit v4 on v3

--- a/solution.py
+++ b/solution.py
@@ -23,16 +23,16 @@
 LIGHT = pl.CostEstimate(flops=0, bytes_accessed=2**17, transcendentals=0)
 
 
-SEND_AT = (9.0, 22.0)
-KEEP_AT = (31.0, 46.0)
-GRAD_STEPS_AT = ((17.0, 29.0), (18.0, 30.0))
-ACT_STEPS_AT = ((51.0, 66.0, 76.0, 90.0), (74.0, 83.0, 89.2, 97.8))
-GRADS_AT = 44.0
-RELAY_WAIT = 30.0
-ACROSS_WAIT = 24.0
-BEHIND = {
-    ("a", 0): (("g", 1), 0),
-}
+SEND_AT = (9.0, 43.0)
+KEEP_AT = (22.0, 59.0)
+STEPS_AT = ((21.0, 29.0), (30.0, 39.0), (42.0, 47.9), (48.5, 66.5), (66.2, 90.0), (74.0, 95.0))
+FINISH_AT = (99.0, 100.0)
+GRADS_AT = 48.0
+JOIN_WAIT = 18.0
+RELAY_WAIT = 14.0
+SIDE_WAIT = 20.0
+ACROSS_WAIT = 100.0
+EXPECTED = {("g", 0): 9.5, ("a", 0, 0): 18.0, ("a", 0, 1): 28.0}
 
 
 def decode(ref, rows):
@@ -122,49 +122,43 @@
         self.last = [outs[0]]
         return outs
 
-    def combine(self, received, kept, dtype, parts=1, carry=()):
+    def combine(self, received, kept, dtype):
         count, rows, wide = kept.shape
-        part_rows = rows // parts
         half = count // 2
         coded = dtype == jnp.float16
 
-        def body(received_ref, kept_ref, *refs):
+        def body(received_ref, kept_ref, send_ref, hold_ref):
             arrived = decode(received_ref, rows)
-            for part in range(parts):
-                send_ref, hold_ref = refs[part], refs[parts + part]
-                at = slice(part * part_rows, (part + 1) * part_rows)
-                total = kept_ref[:half, at] + arrived[:half, at]
-                hold_ref[...] = kept_ref[half:, at] + arrived[half:, at]
-                if coded:
-                    largest = jnp.full((half, CODE_ROWS, wide), jnp.max(jnp.abs(total)))
-                    exponent = jnp.floor(jnp.log2(CODE_TOP / jnp.maximum(largest, CODE_LEAST)))
-                    send_ref[:, :part_rows] = total * jnp.exp2(exponent[:, :1])
-                    send_ref[:, part_rows:] = exponent
-                else:
-                    send_ref[...] = total.astype(send_ref.dtype)
-
-        send_shape = (half, part_rows + CODE_ROWS * coded, wide)
-        outs = self.call(
+            total = kept_ref[:half] + arrived[:half]
+            hold_ref[...] = kept_ref[half:] + arrived[half:]
+            if coded:
+                largest = jnp.full((half, CODE_ROWS, wide), jnp.max(jnp.abs(total)))
+                exponent = jnp.floor(jnp.log2(CODE_TOP / jnp.maximum(largest, CODE_LEAST)))
+                send_ref[:, :rows] = total * jnp.exp2(exponent[:, :1])
+                send_ref[:, rows:] = exponent
+            else:
+                send_ref[...] = total.astype(send_ref.dtype)
+
+        send, hold = self.call(
             body,
-            [jax.ShapeDtypeStruct(send_shape, jnp.float32 if coded else dtype)] * parts
-            + [jax.ShapeDtypeStruct((half, part_rows, wide), jnp.float32)] * parts,
+            [
+                jax.ShapeDtypeStruct((half, rows + CODE_ROWS * coded, wide), jnp.float32 if coded else dtype),
+                jax.ShapeDtypeStruct((half, rows, wide), jnp.float32),
+            ],
             [received, kept],
             [VMEM] * 2,
-            carry=carry,
         )
-        return [x.astype(dtype) for x in outs[:parts]], outs[parts : 2 * parts], outs[2 * parts :]
+        return send.astype(dtype), hold
 
     def finish(self, received, kept):
-        rows, wide = kept[0].shape[1:]
+        parts = len(kept)
 
         def body(*refs):
-            out_ref = refs[-1]
-            for chunk in range(TOKEN_CHUNKS):
-                total = refs[TOKEN_CHUNKS + chunk][0] + refs[chunk][0].astype(jnp.float32)
-                out_ref[chunk * rows : (chunk + 1) * rows] = total
-
-        shape = jax.ShapeDtypeStruct((rows * TOKEN_CHUNKS, wide), jnp.float32)
-        return self.call(body, [shape], [*received, *kept], [VMEM] * (2 * TOKEN_CHUNKS))[0]
+            for part in range(parts):
+                refs[2 * parts + part][...] = refs[parts + part][0] + refs[part][0].astype(jnp.float32)
+
+        shape = jax.ShapeDtypeStruct(kept[0].shape[1:], jnp.float32)
+        return self.call(body, [shape] * parts, [*received, *kept], [VMEM] * (2 * parts))
 
     def finish_grads(self, scalars, received, kept):
         tokens, wide = kept[0].shape[1:]
@@ -201,6 +195,16 @@
         shape = jax.ShapeDtypeStruct((1, 2) + mine.shape, mine.dtype)
         return self.call(body, [shape], [mine, other], [VMEM] * 2)[0]
 
+    def join(self, held, received):
+        count = held.shape[0]
+
+        def body(held_ref, received_ref, out_ref):
+            out_ref[:count] = held_ref[...]
+            out_ref[count:] = received_ref[...]
+
+        shape = jax.ShapeDtypeStruct((2 * count,) + held.shape[1:], held.dtype)
+        return self.call(body, [shape], [held, received], [VMEM] * 2)[0]
+
     def relay(self, x):
         def body(out_ref):
             out_ref[...] = jnp.zeros_like(out_ref)
@@ -211,7 +215,7 @@
         rows, tokens = grads[0].shape[2:]
         count = sum(x.shape[0] for x in grads)
         blocks = len(acts)
-        flat_acts = [x for block in acts for x in block]
+        flat_acts = [x for block in acts for chunk in block for x in chunk]
         scale = 1.0 / SEQ_LEN**0.5
 
         def body(place_ref, *refs):
@@ -220,7 +224,9 @@
             out_ref, result_ref, sems = refs[-3:]
             total = None
             for seq in range(SEQS):
-                act = jnp.concatenate([act_refs[block * SEQS + seq][...] for block in range(blocks)], axis=1)
+                own = iter(act_refs[seq::SEQS])
+                columns = [[next(own)[...] for _ in range(len(acts[block]))] for block in range(blocks)]
+                act = jnp.concatenate([jnp.concatenate(column, axis=0) for column in columns], axis=1)
                 high = act.astype(jnp.bfloat16)
                 low = (act - high.astype(jnp.float32)).astype(jnp.bfloat16)
                 grad = jnp.concatenate([ref[:, seq].reshape(-1, tokens) for ref in grad_refs], axis=0)
@@ -265,11 +271,8 @@
     return [jnp.take(rotated, order, axis=0).astype(dtype)]
 
 
-def halving_order(n, steps):
-    bits = len(steps)
-    return [
-        sum((1 - ((at >> (bits - 1 - step)) & 1)) << bit for step, bit in enumerate(steps)) for at in range(n)
-    ]
+def halving_order(n, bits):
+    return [sum((1 - ((at >> (bits - 1 - bit)) & 1)) << bit for bit in range(bits)) for at in range(n)]
 
 
 def swap(x, n, bit):
@@ -292,66 +295,47 @@
     blocks = width_a // wide
     chain = Chain()
 
-    forward = list(range(bits))
-    crossed = [1, 0] + forward[2:]
     grad_keys = [("g", 0), ("g", 1)]
-    act_keys = [("a", block) for block in range(blocks)]
-    steps_of = {key: forward for key in grad_keys + act_keys}
-    steps_of["g", 0] = crossed
-    orders = {}
-    for steps in (forward, crossed):
-        order = jnp.array(halving_order(n, steps), jnp.int32) ^ me
-        orders[tuple(steps)] = (order[: n // 2], order[n // 2 :])
+    act_keys = [("a", block, chunk) for block in range(blocks) for chunk in range(TOKEN_CHUNKS)]
+    order = jnp.array(halving_order(n, bits), jnp.int32) ^ me
+    orders = (order[: n // 2], order[n // 2 :])
     kept, received, finished, gathered = {}, {}, {}, {}
-    waiting, worked = {}, set()
-
-    def at_work(task):
-        return task not in worked
-
     def keep_or_send(key, x, part):
-        if part == 0 and key in BEHIND and at_work(BEHIND[key]):
-            waiting.setdefault(BEHIND[key], []).append((key, x))
-        elif part == 0:
-            received[key] = swap(x, n, steps_of[key][0])
+        if part == 0:
+            received[key] = swap(x, n, 0)
         else:
             kept[key] = x
 
     def rotate_grads(half, part):
         key = ("g", half)
-        order = orders[tuple(steps_of[key])][part]
+        order = orders[part]
         dtype = (jnp.bfloat16, jnp.float32)[part]
         if width_g % LANES == 0:
-            (x,) = chain.rotate(order, x_g, basis_g, width_g, half * n, 1, order.shape[0] // 2, 1, dtype)
+            (x,) = chain.rotate(order, x_g, basis_g, width_g, half * n, 1, order.shape[0], 1, dtype, 60 * MIB)
         else:
             (x,) = rotate_narrow(order, x_g, basis_g, width_g, half * n, n, dtype)
         keep_or_send(key, x, part)
 
     def rotate_acts(block, part):
-        order = orders[tuple(forward)][part]
+        order = orders[part]
         dtype = (jnp.bfloat16, jnp.float32)[part]
-        (x,) = chain.rotate(order, x_a, basis_a, wide, block, blocks, 2, 1, dtype)
-        keep_or_send(("a", block), x, part)
-
-    def advance(key, step, chunk=None):
-        worked.add((key, step))
+        outs = chain.rotate(order, x_a, basis_a, wide, block, blocks, 2, TOKEN_CHUNKS, dtype)
+        for chunk, x in enumerate(outs):
+            keep_or_send(("a", block, chunk), x, part)
+
+    def advance(key, step):
         wider = jnp.float16 if key[0] == "g" else jnp.float32
         dtype = jnp.bfloat16 if step + 1 < ROUNDED_STEPS[key[0]] else wider
-        behind = waiting.pop((key, step), [])
-        split = TOKEN_CHUNKS if key[0] == "a" and step == 0 else 1
-        name = key if chunk is None else key + (chunk,)
-        sends, holds, carried = chain.combine(received[name], kept[name], dtype, split, [x for _, x in behind])
-        for (other, _), x in zip(behind, carried):
-            received[other] = swap(x, n, steps_of[other][0])
-        for part in range(split):
-            name = key + (part,) if split > 1 else name
-            arrived = swap(sends[part], n, steps_of[key][step + 1])
-            received[name] = arrived.astype(jnp.float32) if dtype == jnp.float16 else arrived
-            kept[name] = holds[part]
+        send, kept[key] = chain.combine(received[key], kept[key], dtype)
+        arrived = swap(send, n, step + 1)
+        received[key] = arrived.astype(jnp.float32) if dtype == jnp.float16 else arrived
+        if key in EXPECTED and step + 2 == bits:
+            chain.expect(received[key], EXPECTED[key])
 
     def finish_acts(block):
         keys = [("a", block, chunk) for chunk in range(TOKEN_CHUNKS)]
         own = chain.finish([received[key] for key in keys], [kept[key] for key in keys])
-        finished[block] = (own, chain.expect(swap_cores(own), 4.0))
+        finished[block] = [(x, swap_cores(x)) for x in own]
 
     def finish_grads():
         mine, other = chain.finish_grads(
@@ -360,13 +344,20 @@
         gathered["mine"], gathered["other"] = mine, swap_cores(other)
 
     def pair_grads():
-        held = chain.pair(gathered["mine"], gathered["other"])
-        sides = [[at for at in range(n) if at % 2 == side] for side in range(2)]
-        gathered["held"] = lax.all_gather(held, "inp", axis_index_groups=sides, tiled=True)
+        gathered["held"] = chain.pair(gathered["mine"], gathered["other"])
+        gathered["order"] = [0]
+        gathered["in"] = swap(gathered["held"], n, bits - 1)
+
+    def join_grads(bit):
+        gathered["held"] = chain.join(gathered["held"], gathered["in"])
+        gathered["order"] = gathered["order"] + [at ^ (1 << bit) for at in gathered["order"]]
+        gathered["in"] = swap(gathered["held"], n, bit - 1)
+        if bit == 2:
+            gathered["side"] = chain.expect(swap(gathered["held"], n, 0), SIDE_WAIT)
 
     def relay_grads():
-        gathered["held"] = chain.relay(gathered["held"])
-        gathered["across"] = chain.expect(swap(gathered["held"], n, 0), ACROSS_WAIT)
+        gathered["in"] = chain.relay(gathered["in"])
+        gathered["across"] = chain.expect(swap(gathered["in"], n, 0), ACROSS_WAIT)
 
     tasks = [
         (0.0, rotate_grads, (0, 0)),
@@ -377,28 +368,28 @@
     for block in range(blocks):
         tasks.append((SEND_AT[block], rotate_acts, (block, 0)))
         tasks.append((KEEP_AT[block], rotate_acts, (block, 1)))
-    for key, times in zip(grad_keys, GRAD_STEPS_AT):
+    for key, times in zip(grad_keys + act_keys, STEPS_AT):
         for step in range(bits - 1):
             tasks.append((times[min(step, 1)] + 8.0 * max(step - 1, 0), advance, (key, step)))
-    for key, times in zip(act_keys, ACT_STEPS_AT):
-        tasks.append((times[0], advance, (key, 0)))
-        for step in range(1, bits - 1):
-            for chunk in range(TOKEN_CHUNKS):
-                tasks.append((times[1 + chunk] + 8.0 * (step - 1), advance, (key, step, chunk)))
-        tasks.append((times[-1] + 8.0 * (bits - 3), finish_acts, (key[1],)))
+    for block in range(blocks):
+        tasks.append((FINISH_AT[block] + 8.0 * (bits - 3), finish_acts, (block,)))
     clock = GRADS_AT + 8.0 * (bits - 3)
     tasks.append((clock, finish_grads, ()))
     clock += 1.0
     tasks.append((clock, pair_grads, ()))
+    for bit in range(bits - 1, 1, -1):
+        clock += JOIN_WAIT
+        tasks.append((clock, join_grads, (bit,)))
     tasks.append((clock + RELAY_WAIT, relay_grads, ()))
     for chain.clock, task, arguments in sorted(tasks, key=lambda task: task[0]):
         task(*arguments)
 
-    same_side = 2 * jnp.arange(n // 2, dtype=jnp.int32) + me % 2
-    place = jnp.concatenate([same_side, same_side ^ 1])
+    low = gathered["order"]
+    offsets = low + [at ^ 2 for at in low] + [at ^ 1 for at in low] + [at ^ 3 for at in low]
+    place = jnp.array(offsets, jnp.int32) ^ me
     act_blocks = [finished[block] for block in range(blocks)]
     out_shape = jax.ShapeDtypeStruct((n * width_g, width_a), jnp.float32)
-    grads = [gathered[name] for name in ("held", "across")]
+    grads = [gathered[name] for name in ("held", "in", "side", "across")]
     return chain.moments(place, grads, act_blocks, out_shape)
 
 

time: 165 us -> 144 us (0.87)
  waiting for transfers between devices: 68.1 us -> 44.4 us
  between operations: 14.3 us -> 1.27 us
  Pallas kernels: 44.7 us -> 55.8 us
  starting transfers between devices: 22.4 us -> 32.4 us
  local copies, waits for them, and re-layouts: 12.2 us -> 7.6 us
    ppermute x17 -> x22, waiting for transfers between devices: 66.7 us -> 43 us  [swap(): lax.ppermute(x, 'inp', [(index, index ^ 1 << bit) for index in range(n)])]
    pallas_call x8, Pallas kernels: 34.3 us -> 44.1 us  [rotate(): pl.pallas_call(kernel, grid_spec=pltpu.PrefetchScalarGridSpec(num_scalar_...]
    ppermute x17 -> x22, starting transfers between devices: 22.2 us -> 31.2 us  [swap(): lax.ppermute(x, 'inp', [(index, index ^ 1 << bit) for index in range(n)])]
    unnamed x32, local copies, waits for them, and re-layouts: 12 us -> 7.01 us
    pallas_call x16 -> x19, Pallas kernels: 10.4 us -> 11.7 us  [call(): pl.pallas_call(kernel, out_shape=list(out_shape) + [jax.ShapeDtypeStruct(...]
  transfers between devices with their start and end apart: 21 -> 27, of which waited for: 11 -> 11; matrix products, arithmetic and copies ran while one was open for 1% -> 1% of each run, Pallas kernels for 21% -> 33%
where the time goes in v4:
time: 144 us; the launch traced here: 143 us
  Pallas kernels  55.8 us (39%)
  waiting for transfers between devices  44.4 us (31%)
  starting transfers between devices  32.4 us (22%)
  local copies, waits for them, and re-layouts  7.6 us (5%)
  other arithmetic  1.93 us (1%)
    pallas_call x8, Pallas kernels, rotate(): pl.pallas_call(kernel, grid_spec=pltpu.PrefetchScalarGridSpec(num_scalar_...  44.1 us
    ppermute x22, waiting for transfers between devices, swap(): lax.ppermute(x, 'inp', [(index, index ^ 1 << bit) for index in range(n)])  43 us
    ppermute x22, starting transfers between devices, swap(): lax.ppermute(x, 'inp', [(index, index ^ 1 << bit) for index in range(n)])  31.2 us
    pallas_call x19, Pallas kernels, call(): pl.pallas_call(kernel, out_shape=list(out_shape) + [jax.ShapeDtypeStruct(...  11.7 us
    unnamed x32, local copies, waits for them, and re-layouts  7.01 us
  transfers between devices with their start and end apart: 27, of which 11 were waited for; matrix products, arithmetic and copies ran while one was open for 1% of the time, Pallas kernels for 33%

profile of v4, /device:TPU:0, one launch (start us, length us, event | category | flops | bytes accessed | tf_op | source)
XLA Modules:
  0.0 143.4 jit_solution(16395210044720943929)
XLA Ops:
  1.3 3.7 %shard_map.73.refs_4_ = bf16[4,512,128]{2,1,0:T(8,128)(2,1)} custom-call(s32[4]{0:T(128)} %get-tuple-element.86.order_ref, bf16[512,1024]{1,0:T(8,128)(2,1)} %bitcast.7, bf16[1024,2048]{1,0:T(8,128)(2,1)} %refs_3_.7, bf16[1024,2048]{1,0:T(8,128)(2,1)} %refs_3_.7, bf16[1024,2048]{1,0:T(8,128)(2,1)} %refs_3_.7, bf16[1024,2048]{1,0:T(8,128)(2,1)} %refs_3_.7), custom_call_target="tpu_custom_call" | custom-call | bytes 131072 | tf_op jit(solution)/shard_map/pallas_call | solution.py:108
  4.9 3.0 %collective-permute-start = (bf16[4,512,128]{2,1,0:T(8,128)(2,1)}, bf16[4,512,128]{2,1,0:T(8,128)(2,1)}, u32[]{:S(2)}, u32[]{:S(2)}) collective-permute-start(bf16[4,512,128]{2,1,0:T(8,128)(2,1)} %shard_map.73.refs_4_), channel_id=1, source_target_pairs={{0,2},{2,0},{4,6},{6,4},{8,10},{10,8},{12,14},{14,12},{1,3},{3,1},... | collective-permute-start | bytes 1572872 | tf_op jit(solution)/shard_map/ppermute | solution.py:279
  7.9 3.7 %shard_map.74.refs_4_ = bf16[4,512,128]{2,1,0:T(8,128)(2,1)} custom-call(s32[4]{0:T(128)} %get-tuple-element.86.order_ref, bf16[512,1024]{1,0:T(8,128)(2,1)} %bitcast.8, bf16[1024,2048]{1,0:T(8,128)(2,1)} %refs_3_.7, bf16[1024,2048]{1,0:T(8,128)(2,1)} %refs_3_.7, bf16[1024,2048]{1,0:T(8,128)(2,1)} %refs_3_.7, bf16[1024,2048]{1,0:T(8,128)(2,1)} %refs_3_.7, ...), custom_call_target="tpu_custom_call" | custom-call | bytes 131072 | tf_op jit(solution)/shard_map/pallas_call | solution.py:108
  11.6 3.9 %shard_map.75.refs_4_.refs_1_ = f32[4,512,128]{2,1,0:T(8,128)} custom-call(s32[4]{0:T(128)} %get-tuple-element.85.order_ref, bf16[512,1024]{1,0:T(8,128)(2,1)} %bitcast.9, bf16[1024,2048]{1,0:T(8,128)(2,1)} %refs_3_.7, bf16[1024,2048]{1,0:T(8,128)(2,1)} %refs_3_.7, bf16[1024,2048]{1,0:T(8,128)(2,1)} %refs_3_.7, bf16[1024,2048]{1,0:T(8,128)(2,1)} %refs_3_.7, ...), custom_call_target="tpu_custom_call" | custom-call | bytes 131072 | tf_op jit(solution)/shard_map/pallas_call | solution.py:108
  15.5 4.4 %shard_map.76.refs_2_.refs_1_ = f32[4,512,128]{2,1,0:T(8,128)} custom-call(s32[4]{0:T(128)} %get-tuple-element.85.order_ref, bf16[512,1024]{1,0:T(8,128)(2,1)} %bitcast.10, bf16[1024,2048]{1,0:T(8,128)(2,1)} %refs_3_.7, bf16[1024,2048]{1,0:T(8,128)(2,1)} %refs_3_.7, bf16[1024,2048]{1,0:T(8,128)(2,1)} %refs_3_.7, bf16[1024,2048]{1,0:T(8,128)(2,1)} %refs_3_.7, ...), custom_call_target="tpu_custom_call" | custom-call | bytes 131072 | tf_op jit(solution)/shard_map/pallas_call | solution.py:108
  21.1 7.5 %shard_map.77 = (bf16[4,256,256]{2,1,0:T(8,128)(2,1)S(1)}, bf16[4,256,256]{2,1,0:T(8,128)(2,1)}) custom-call(s32[4]{0:T(128)S(1)} %copy-done.13, bf16[512,3584]{1,0:T(8,128)(2,1)S(1)} %bitcast.3, bf16[3584,4096]{1,0:T(8,128)(2,1)} %refs_1_.15, bf16[3584,4096]{1,0:T(8,128)(2,1)} %refs_1_.15, f32[4,512,128]{2,1,0:T(8,128)S(1)} %copy-done.2), custom_call_target="tpu_custom_call" | custom-call | bytes 131072 | tf_op jit(solution)/shard_map/pallas_call | solution.py:108
  29.8 2.1 %collective-permute-start.1 = (bf16[2,512,128]{2,1,0:T(8,128)(2,1)S(1)}, bf16[2,512,128]{2,1,0:T(8,128)(2,1)S(1)}, u32[]{:S(2)}, u32[]{:S(2)}) collective-permute-start(bf16[2,512,128]{2,1,0:T(8,128)(2,1)S(1)} %get-tuple-element.46.refs_2_), channel_id=1, source_target_pairs={{0,4},{2,6},{4,0},{6,2},{8,12},{10,14},{12,8},{14,10},{1,5},{3,7},... | collective-permute-start | bytes 786440 | tf_op jit(solution)/shard_map/ppermute | solution.py:279
  33.5 6.8 %shard_map.79 = (f32[4,256,256]{2,1,0:T(8,128)S(1)}, f32[4,256,256]{2,1,0:T(8,128)S(1)}) custom-call(s32[4]{0:T(128)S(1)} %copy-done.12, bf16[512,3584]{1,0:T(8,128)(2,1)S(1)} %bitcast.4, bf16[3584,4096]{1,0:T(8,128)(2,1)} %refs_1_.15, bf16[3584,4096]{1,0:T(8,128)(2,1)} %refs_1_.15, bf16[2,512,128]{2,1,0:T(8,128)(2,1)S(1)} %get-tuple-element.46.refs_2_), custom_call_target="tpu_custom_call" | custom-call | bytes 131072 | tf_op jit(solution)/shard_map/pallas_call | solution.py:108
  42.5 2.7 %collective-permute-start.2 = (f16[1,528,128]{2,1,0:T(8,128)(2,1)S(1)}, f16[1,528,128]{2,1,0:T(8,128)(2,1)S(1)}, u32[]{:S(2)}, u32[]{:S(2)}) collective-permute-start(f16[1,528,128]{2,1,0:T(8,128)(2,1)S(1)} %convert_element_type.12), channel_id=1, source_target_pairs={{0,8},{2,10},{4,12},{6,14},{8,0},{10,2},{12,4},{14,6},{1,9},{3,11}... | collective-permute-start | bytes 405512 | tf_op jit(solution)/shard_map/ppermute | solution.py:279
  45.6 4.2 %collective-permute-done.2 = f16[1,528,128]{2,1,0:T(8,128)(2,1)S(1)} collective-permute-done((f16[1,528,128]{2,1,0:T(8,128)(2,1)S(1)}, f16[1,528,128]{2,1,0:T(8,128)(2,1)S(1)}, u32[]{:S(2)}, u32[]{:S(2)}) %collective-permute-start.2) | collective-permute-done | bytes 135200 | tf_op jit(solution)/shard_map/ppermute | solution.py:279
  49.8 2.0 %collective-permute-done.4.refs_0_ = bf16[2,512,128]{2,1,0:T(8,128)(2,1)S(1)} collective-permute-done((bf16[2,512,128]{2,1,0:T(8,128)(2,1)S(1)}, bf16[2,512,128]{2,1,0:T(8,128)(2,1)S(1)}, u32[]{:S(2)}, u32[]{:S(2)}) %collective-permute-start.4) | collective-permute-done | bytes 262176 | tf_op jit(solution)/shard_map/ppermute | solution.py:279
  53.6 2.6 %collective-permute-start.7 = (bf16[2,256,256]{2,1,0:T(8,128)(2,1)}, bf16[2,256,256]{2,1,0:T(8,128)(2,1)}, u32[]{:S(2)}, u32[]{:S(2)}) collective-permute-start(bf16[2,256,256]{2,1,0:T(8,128)(2,1)} %get-tuple-element.55.refs_2_), channel_id=1, source_target_pairs={{0,4},{2,6},{4,0},{6,2},{8,12},{10,14},{12,8},{14,10},{1,5},{3,7},... | collective-permute-start | bytes 786440 | tf_op jit(solution)/shard_map/ppermute | solution.py:279
  56.7 7.4 %shard_map.84 = (bf16[4,256,256]{2,1,0:T(8,128)(2,1)}, bf16[4,256,256]{2,1,0:T(8,128)(2,1)S(1)}) custom-call(s32[4]{0:T(128)S(1)} %copy-done.13, bf16[512,3584]{1,0:T(8,128)(2,1)S(1)} %bitcast.5, bf16[3584,4096]{1,0:T(8,128)(2,1)} %refs_1_.15, bf16[3584,4096]{1,0:T(8,128)(2,1)} %refs_1_.15, bf16[2,256,256]{2,1,0:T(8,128)(2,1)} %get-tuple-element.55.refs_2_), custom_call_target="tpu_custom_call" | custom-call | bytes 131072 | tf_op jit(solution)/shard_map/pallas_call | solution.py:108
  75.3 2.2 %collective-permute-start.10 = (bf16[1,2,128,512]{3,2,1,0:T(8,128)(2,1)S(1)}, bf16[1,2,128,512]{3,2,1,0:T(8,128)(2,1)S(1)}, u32[]{:S(2)}, u32[]{:S(2)}) collective-permute-start(bf16[1,2,128,512]{3,2,1,0:T(8,128)(2,1)S(1)} %shard_map.88.refs_2_.refs_0_), channel_id=1, source_target_pairs={{0,8},{2,10},{4,12},{6,14},{8,0},{10,2},{12,4},{14,6},{1,9},{3,11}... | collective-permute-start | bytes 786440 | tf_op jit(solution)/shard_map/ppermute | solution.py:279
  79.8 6.8 %shard_map.89 = (f32[4,256,256]{2,1,0:T(8,128)S(1)}, f32[4,256,256]{2,1,0:T(8,128)S(1)}) custom-call(s32[4]{0:T(128)S(1)} %copy-done.12, bf16[512,3584]{1,0:T(8,128)(2,1)S(1)} %bitcast.6, bf16[3584,4096]{1,0:T(8,128)(2,1)} %refs_1_.15, bf16[3584,4096]{1,0:T(8,128)(2,1)} %refs_1_.15, bf16[1,2,128,512]{3,2,1,0:T(8,128)(2,1)S(1)} %shard_map.88.refs_2_.refs_0_), custom_call_target="tpu_custom_call" | custom-call | bytes 131072 | tf_op jit(solution)/shard_map/pallas_call | solution.py:108
  86.6 9.4 %collective-permute-done.13.refs_3_.refs_0_ = bf16[1,256,256]{2,1,0:T(8,128)(2,1)S(1)} collective-permute-done((bf16[1,256,256]{2,1,0:T(8,128)(2,1)S(1)}, bf16[1,256,256]{2,1,0:T(8,128)(2,1)S(1)}, u32[]{:S(2)}, u32[]{:S(2)}) %collective-permute-start.13) | collective-permute-done | bytes 131104 | tf_op jit(solution)/shard_map/ppermute | solution.py:279
  100.8 3.4 %collective-permute-start.18 = (bf16[1,256,256]{2,1,0:T(8,128)(2,1)S(1)}, bf16[1,256,256]{2,1,0:T(8,128)(2,1)S(1)}, u32[]{:S(2)}, u32[]{:S(2)}) collective-permute-start(bf16[1,256,256]{2,1,0:T(8,128)(2,1)S(1)} %get-tuple-element.67.refs_2_), channel_id=1, source_target_pairs={{0,8},{2,10},{4,12},{6,14},{8,0},{10,2},{12,4},{14,6},{1,9},{3,11}... | collective-permute-start | bytes 393224 | tf_op jit(solution)/shard_map/ppermute | solution.py:279
  104.2 9.8 %collective-permute-done.15.refs_1_ = bf16[2,2,128,512]{3,2,1,0:T(8,128)(2,1)S(1)} collective-permute-done((bf16[2,2,128,512]{3,2,1,0:T(8,128)(2,1)S(1)}, bf16[2,2,128,512]{3,2,1,0:T(8,128)(2,1)S(1)}, u32[]{:S(2)}, u32[]{:S(2)}) %collective-permute-start.15) | collective-permute-done | bytes 524320 | tf_op jit(solution)/shard_map/ppermute | solution.py:279
  115.5 4.1 %collective-permute-done.20.refs_0_ = bf16[2,256,256]{2,1,0:T(8,128)(2,1)S(1)} collective-permute-done((bf16[2,256,256]{2,1,0:T(8,128)(2,1)S(1)}, bf16[2,256,256]{2,1,0:T(8,128)(2,1)S(1)}, u32[]{:S(2)}, u32[]{:S(2)}) %collective-permute-start.20) | collective-permute-done | bytes 262176 | tf_op jit(solution)/shard_map/ppermute | solution.py:279
  119.6 2.2 %collective-permute-done.18.refs_3_.refs_1_ = bf16[1,256,256]{2,1,0:T(8,128)(2,1)S(1)} collective-permute-done((bf16[1,256,256]{2,1,0:T(8,128)(2,1)S(1)}, bf16[1,256,256]{2,1,0:T(8,128)(2,1)S(1)}, u32[]{:S(2)}, u32[]{:S(2)}) %collective-permute-start.18) | collective-permute-done | bytes 131104 | tf_op jit(solution)/shard_map/ppermute | solution.py:279
  121.8 1.7 %collective-permute-done.19.refs_0_ = bf16[2,256,256]{2,1,0:T(8,128)(2,1)S(1)} collective-permute-done((bf16[2,256,256]{2,1,0:T(8,128)(2,1)S(1)}, bf16[2,256,256]{2,1,0:T(8,128)(2,1)S(1)}, u32[]{:S(2)}, u32[]{:S(2)}) %collective-permute-start.19) | collective-permute-done | bytes 262176 | tf_op jit(solution)/shard_map/ppermute | solution.py:279
  123.6 1.7 %collective-permute-start.24 = (bf16[1,256,256]{2,1,0:T(8,128)(2,1)S(1)}, bf16[1,256,256]{2,1,0:T(8,128)(2,1)S(1)}, u32[]{:S(2)}, u32[]{:S(2)}) collective-permute-start(bf16[1,256,256]{2,1,0:T(8,128)(2,1)S(1)} %get-tuple-element.78.refs_4_), channel_id=1, source_target_pairs={{0,8},{2,10},{4,12},{6,14},{8,0},{10,2},{12,4},{14,6},{1,9},{3,11}... | collective-permute-start | bytes 393224 | tf_op jit(solution)/shard_map/ppermute | solution.py:279
  127.2 8.2 %collective-permute-done.24.refs_1_ = bf16[1,256,256]{2,1,0:T(8,128)(2,1)S(1)} collective-permute-done((bf16[1,256,256]{2,1,0:T(8,128)(2,1)S(1)}, bf16[1,256,256]{2,1,0:T(8,128)(2,1)S(1)}, u32[]{:S(2)}, u32[]{:S(2)}) %collective-permute-start.24) | collective-permute-done | bytes 131104 | tf_op jit(solution)/shard_map/ppermute | solution.py:279
  138.9 4.4 %shard_map.99 = f32[1024,512]{1,0:T(8,128)} custom-call(s32[8]{0:T(128)S(1)} %broadcast_xor_fusion.1.refs_0_, bf16[2,2,128,512]{3,2,1,0:T(8,128)(2,1)S(1)} %shard_map.92.refs_2_.refs_1_, bf16[2,2,128,512]{3,2,1,0:T(8,128)(2,1)S(1)} %get-tuple-element.71.refs_2_, bf16[2,2,128,512]{3,2,1,0:T(8,128)(2,1)S(1)} %collective-permute-done.16.refs_3_, ...), custom_call_target="tpu_custom_call" | custom-call | bytes 131072 | tf_op jit(solution)/shard_map/pallas_call | solution.py:73
  (97 shorter events, 34.3 us)
Async XLA Ops:
  4.9 23.7 %collective-permute-start = (bf16[4,512,128]{2,1,0:T(8,128)(2,1)}, bf16[4,512,128]{2,1,0:T(8,128)(2,1)}, u32[]{:S(2)}, u32[]{:S(2)}) collective-permute-start(bf16[4,512,128]{2,1,0:T(8,128)(2,1)} %shard_map.73.refs_4_), channel_id=1, source_target_pairs={{0,2},{2,0},{4,6},{6,4},{8,10},{10,8},{12,14},{14,12},{1,3},{3,1},... | collective-permute-start | bytes 1572872 | tf_op jit(solution)/shard_map/ppermute | solution.py:279
  11.6 28.9 %collective-permute-start.3 = (bf16[4,512,128]{2,1,0:T(8,128)(2,1)}, bf16[4,512,128]{2,1,0:T(8,128)(2,1)}, u32[]{:S(2)}, u32[]{:S(2)}) collective-permute-start(bf16[4,512,128]{2,1,0:T(8,128)(2,1)} %shard_map.74.refs_4_), channel_id=1, source_target_pairs={{0,2},{2,0},{4,6},{6,4},{8,10},{10,8},{12,14},{14,12},{1,3},{3,1},... | collective-permute-start | bytes 1572872 | tf_op jit(solution)/shard_map/ppermute | solution.py:279
  29.8 10.5 %collective-permute-start.1 = (bf16[2,512,128]{2,1,0:T(8,128)(2,1)S(1)}, bf16[2,512,128]{2,1,0:T(8,128)(2,1)S(1)}, u32[]{:S(2)}, u32[]{:S(2)}) collective-permute-start(bf16[2,512,128]{2,1,0:T(8,128)(2,1)S(1)} %get-tuple-element.46.refs_2_), channel_id=1, source_target_pairs={{0,4},{2,6},{4,0},{6,2},{8,12},{10,14},{12,8},{14,10},{1,5},{3,7},... | collective-permute-start | bytes 786440 | tf_op jit(solution)/shard_map/ppermute | solution.py:279
  31.9 20.1 %collective-permute-start.6 = (bf16[4,256,256]{2,1,0:T(8,128)(2,1)S(1)}, bf16[4,256,256]{2,1,0:T(8,128)(2,1)S(1)}, u32[]{:S(2)}, u32[]{:S(2)}) collective-permute-start(bf16[4,256,256]{2,1,0:T(8,128)(2,1)S(1)} %get-tuple-element.45.refs_2_), channel_id=1, source_target_pairs={{0,2},{2,0},{4,6},{6,4},{8,10},{10,8},{12,14},{14,12},{1,3},{3,1},... | collective-permute-start | bytes 1572872 | tf_op jit(solution)/shard_map/ppermute | solution.py:279
  41.9 9.9 %collective-permute-start.4 = (bf16[2,512,128]{2,1,0:T(8,128)(2,1)S(1)}, bf16[2,512,128]{2,1,0:T(8,128)(2,1)S(1)}, u32[]{:S(2)}, u32[]{:S(2)}) collective-permute-start(bf16[2,512,128]{2,1,0:T(8,128)(2,1)S(1)} %get-tuple-element.50.refs_2_), channel_id=1, source_target_pairs={{0,4},{2,6},{4,0},{6,2},{8,12},{10,14},{12,8},{14,10},{1,5},{3,7},... | collective-permute-start | bytes 786440 | tf_op jit(solution)/shard_map/ppermute | solution.py:279
  42.5 7.3 %collective-permute-start.2 = (f16[1,528,128]{2,1,0:T(8,128)(2,1)S(1)}, f16[1,528,128]{2,1,0:T(8,128)(2,1)S(1)}, u32[]{:S(2)}, u32[]{:S(2)}) collective-permute-start(f16[1,528,128]{2,1,0:T(8,128)(2,1)S(1)} %convert_element_type.12), channel_id=1, source_target_pairs={{0,8},{2,10},{4,12},{6,14},{8,0},{10,2},{12,4},{14,6},{1,9},{3,11}... | collective-permute-start | bytes 405512 | tf_op jit(solution)/shard_map/ppermute | solution.py:279
  45.1 27.4 %collective-permute-start.9 = (bf16[4,256,256]{2,1,0:T(8,128)(2,1)}, bf16[4,256,256]{2,1,0:T(8,128)(2,1)}, u32[]{:S(2)}, u32[]{:S(2)}) collective-permute-start(bf16[4,256,256]{2,1,0:T(8,128)(2,1)} %get-tuple-element.61), channel_id=1, source_target_pairs={{0,2},{2,0},{4,6},{6,4},{8,10},{10,8},{12,14},{14,12},{1,3},{3,1},... | collective-permute-start | bytes 1572872 | tf_op jit(solution)/shard_map/ppermute | solution.py:279
  53.6 13.9 %collective-permute-start.7 = (bf16[2,256,256]{2,1,0:T(8,128)(2,1)}, bf16[2,256,256]{2,1,0:T(8,128)(2,1)}, u32[]{:S(2)}, u32[]{:S(2)}) collective-permute-start(bf16[2,256,256]{2,1,0:T(8,128)(2,1)} %get-tuple-element.55.refs_2_), channel_id=1, source_target_pairs={{0,4},{2,6},{4,0},{6,2},{8,12},{10,14},{12,8},{14,10},{1,5},{3,7},... | collective-permute-start | bytes 786440 | tf_op jit(solution)/shard_map/ppermute | solution.py:279
  56.3 10.1 %collective-permute-start.5 = (f16[1,528,128]{2,1,0:T(8,128)(2,1)S(1)}, f16[1,528,128]{2,1,0:T(8,128)(2,1)}, u32[]{:S(2)}, u32[]{:S(2)}) collective-permute-start(f16[1,528,128]{2,1,0:T(8,128)(2,1)S(1)} %convert_element_type.14), channel_id=1, source_target_pairs={{0,8},{2,10},{4,12},{6,14},{8,0},{10,2},{12,4},{14,6},{1,9},{3,11}... | collective-permute-start | bytes 405512 | tf_op jit(solution)/shard_map/ppermute | solution.py:279
  65.0 31.0 %collective-permute-start.12 = (bf16[4,256,256]{2,1,0:T(8,128)(2,1)}, bf16[4,256,256]{2,1,0:T(8,128)(2,1)S(1)}, u32[]{:S(2)}, u32[]{:S(2)}) collective-permute-start(bf16[4,256,256]{2,1,0:T(8,128)(2,1)} %get-tuple-element.57.refs_2_), channel_id=1, source_target_pairs={{0,2},{2,0},{4,6},{6,4},{8,10},{10,8},{12,14},{14,12},{1,3},{3,1},... | collective-permute-start | bytes 1572872 | tf_op jit(solution)/shard_map/ppermute | solution.py:279
  74.8 21.3 %collective-permute-start.11 = (bf16[2,256,256]{2,1,0:T(8,128)(2,1)S(1)}, bf16[2,256,256]{2,1,0:T(8,128)(2,1)S(1)}, u32[]{:S(2)}, u32[]{:S(2)}) collective-permute-start(bf16[2,256,256]{2,1,0:T(8,128)(2,1)S(1)} %get-tuple-element.63.refs_2_), channel_id=1, source_target_pairs={{0,4},{2,6},{4,0},{6,2},{8,12},{10,14},{12,8},{14,10},{1,5},{3,7},... | collective-permute-start | bytes 786440 | tf_op jit(solution)/shard_map/ppermute | solution.py:279
  75.3 20.9 %collective-permute-start.10 = (bf16[1,2,128,512]{3,2,1,0:T(8,128)(2,1)S(1)}, bf16[1,2,128,512]{3,2,1,0:T(8,128)(2,1)S(1)}, u32[]{:S(2)}, u32[]{:S(2)}) collective-permute-start(bf16[1,2,128,512]{3,2,1,0:T(8,128)(2,1)S(1)} %shard_map.88.refs_2_.refs_0_), channel_id=1, source_target_pairs={{0,8},{2,10},{4,12},{6,14},{8,0},{10,2},{12,4},{14,6},{1,9},{3,11}... | collective-permute-start | bytes 786440 | tf_op jit(solution)/shard_map/ppermute | solution.py:279
  77.5 22.3 %collective-permute-start.14 = (bf16[4,256,256]{2,1,0:T(8,128)(2,1)}, bf16[4,256,256]{2,1,0:T(8,128)(2,1)S(1)}, u32[]{:S(2)}, u32[]{:S(2)}) collective-permute-start(bf16[4,256,256]{2,1,0:T(8,128)(2,1)} %copy-done.14), channel_id=1, source_target_pairs={{0,2},{2,0},{4,6},{6,4},{8,10},{10,8},{12,14},{14,12},{1,3},{3,1},... | collective-permute-start | bytes 1572872 | tf_op jit(solution)/shard_map/ppermute | solution.py:279
  79.0 16.9 %collective-permute-start.13 = (bf16[1,256,256]{2,1,0:T(8,128)(2,1)S(1)}, bf16[1,256,256]{2,1,0:T(8,128)(2,1)S(1)}, u32[]{:S(2)}, u32[]{:S(2)}) collective-permute-start(bf16[1,256,256]{2,1,0:T(8,128)(2,1)S(1)} %get-tuple-element.58.refs_5_), channel_id=1, source_target_pairs={{0,8},{2,10},{4,12},{6,14},{8,0},{10,2},{12,4},{14,6},{1,9},{3,11}... | collective-permute-start | bytes 393224 | tf_op jit(solution)/shard_map/ppermute | solution.py:279
  96.2 17.7 %collective-permute-start.15 = (bf16[2,2,128,512]{3,2,1,0:T(8,128)(2,1)S(1)}, bf16[2,2,128,512]{3,2,1,0:T(8,128)(2,1)S(1)}, u32[]{:S(2)}, u32[]{:S(2)}) collective-permute-start(bf16[2,2,128,512]{3,2,1,0:T(8,128)(2,1)S(1)} %shard_map.92.refs_2_.refs_1_), channel_id=1, source_target_pairs={{0,4},{2,6},{4,0},{6,2},{8,12},{10,14},{12,8},{14,10},{1,5},{3,7},... | collective-permute-start | bytes 1572872 | tf_op jit(solution)/shard_map/ppermute | solution.py:279
  97.1 22.5 %collective-permute-start.16 = (bf16[2,2,128,512]{3,2,1,0:T(8,128)(2,1)S(1)}, bf16[2,2,128,512]{3,2,1,0:T(8,128)(2,1)S(1)}, u32[]{:S(2)}, u32[]{:S(2)}) collective-permute-start(bf16[2,2,128,512]{3,2,1,0:T(8,128)(2,1)S(1)} %shard_map.92.refs_2_.refs_1_), channel_id=1, source_target_pairs={{0,2},{2,0},{4,6},{6,4},{8,10},{10,8},{12,14},{14,12},{1,3},{3,1},... | collective-permute-start | bytes 1572872 | tf_op jit(solution)/shard_map/ppermute | solution.py:279
  98.6 21.0 %collective-permute-start.20 = (bf16[2,256,256]{2,1,0:T(8,128)(2,1)S(1)}, bf16[2,256,256]{2,1,0:T(8,128)(2,1)S(1)}, u32[]{:S(2)}, u32[]{:S(2)}) collective-permute-start(bf16[2,256,256]{2,1,0:T(8,128)(2,1)S(1)} %get-tuple-element.66.refs_2_), channel_id=1, source_target_pairs={{0,4},{2,6},{4,0},{6,2},{8,12},{10,14},{12,8},{14,10},{1,5},{3,7},... | collective-permute-start | bytes 786440 | tf_op jit(solution)/shard_map/ppermute | solution.py:279
  99.9 23.6 %collective-permute-start.19 = (bf16[2,256,256]{2,1,0:T(8,128)(2,1)S(1)}, bf16[2,256,256]{2,1,0:T(8,128)(2,1)S(1)}, u32[]{:S(2)}, u32[]{:S(2)}) collective-permute-start(bf16[2,256,256]{2,1,0:T(8,128)(2,1)S(1)} %get-tuple-element.70.refs_0_), channel_id=1, source_target_pairs={{0,4},{2,6},{4,0},{6,2},{8,12},{10,14},{12,8},{14,10},{1,5},{3,7},... | collective-permute-start | bytes 786440 | tf_op jit(solution)/shard_map/ppermute | solution.py:279
  100.8 21.1 %collective-permute-start.18 = (bf16[1,256,256]{2,1,0:T(8,128)(2,1)S(1)}, bf16[1,256,256]{2,1,0:T(8,128)(2,1)S(1)}, u32[]{:S(2)}, u32[]{:S(2)}) collective-permute-start(bf16[1,256,256]{2,1,0:T(8,128)(2,1)S(1)} %get-tuple-element.67.refs_2_), channel_id=1, source_target_pairs={{0,8},{2,10},{4,12},{6,14},{8,0},{10,2},{12,4},{14,6},{1,9},{3,11}... | collective-permute-start | bytes 393224 | tf_op jit(solution)/shard_map/ppermute | solution.py:279
  114.0 24.9 %collective-permute-start.17 = (bf16[2,2,128,512]{3,2,1,0:T(8,128)(2,1)S(1)}, bf16[2,2,128,512]{3,2,1,0:T(8,128)(2,1)S(1)}, u32[]{:S(2)}, u32[]{:S(2)}) collective-permute-start(bf16[2,2,128,512]{3,2,1,0:T(8,128)(2,1)S(1)} %get-tuple-element.71.refs_2_), channel_id=1, source_target_pairs={{0,2},{2,0},{4,6},{6,4},{8,10},{10,8},{12,14},{14,12},{1,3},{3,1},... | collective-permute-start | bytes 1572872 | tf_op jit(solution)/shard_map/ppermute | solution.py:279
  123.6 11.8 %collective-permute-start.24 = (bf16[1,256,256]{2,1,0:T(8,128)(2,1)S(1)}, bf16[1,256,256]{2,1,0:T(8,128)(2,1)S(1)}, u32[]{:S(2)}, u32[]{:S(2)}) collective-permute-start(bf16[1,256,256]{2,1,0:T(8,128)(2,1)S(1)} %get-tuple-element.78.refs_4_), channel_id=1, source_target_pairs={{0,8},{2,10},{4,12},{6,14},{8,0},{10,2},{12,4},{14,6},{1,9},{3,11}... | collective-permute-start | bytes 393224 | tf_op jit(solution)/shard_map/ppermute | solution.py:279
  125.4 11.5 %collective-permute-start.23 = (bf16[1,256,256]{2,1,0:T(8,128)(2,1)S(1)}, bf16[1,256,256]{2,1,0:T(8,128)(2,1)S(1)}, u32[]{:S(2)}, u32[]{:S(2)}) collective-permute-start(bf16[1,256,256]{2,1,0:T(8,128)(2,1)S(1)} %get-tuple-element.77.refs_2_), channel_id=1, source_target_pairs={{0,8},{2,10},{4,12},{6,14},{8,0},{10,2},{12,4},{14,6},{1,9},{3,11}... | collective-permute-start | bytes 393224 | tf_op jit(solution)/shard_map/ppermute | solution.py:279
  126.7 10.8 %collective-permute-start.22 = (f32[256,256]{1,0:T(8,128)S(1)}, f32[256,256]{1,0:T(8,128)S(1)}, u32[]{:S(2)}, u32[]{:S(2)}) collective-permute-start(f32[256,256]{1,0:T(8,128)S(1)} %get-tuple-element.80.refs_7_), channel_id=1, source_target_pairs={{0,1},{1,0},{2,3},{3,2},{4,5},{5,4},{6,7},{7,6},{8,9},{9,8},{10,11... | collective-permute-start | bytes 786440 | tf_op jit(solution)/shard_map/ppermute | solution.py:283
  126.7 10.8 %collective-permute-start.21 = (f32[256,256]{1,0:T(8,128)S(1)}, f32[256,256]{1,0:T(8,128)S(1)}, u32[]{:S(2)}, u32[]{:S(2)}) collective-permute-start(f32[256,256]{1,0:T(8,128)S(1)} %get-tuple-element.79.refs_4_.refs_5_), channel_id=1, source_target_pairs={{0,1},{1,0},{2,3},{3,2},{4,5},{5,4},{6,7},{7,6},{8,9},{9,8},{10,11... | collective-permute-start | bytes 786440 | tf_op jit(solution)/shard_map/ppermute | solution.py:283
  (19 other events, 127.2 us)

commit v5 on v4

--- a/solution.py
+++ b/solution.py
@@ -23,16 +23,17 @@
 LIGHT = pl.CostEstimate(flops=0, bytes_accessed=2**17, transcendentals=0)
 
 
-SEND_AT = (9.0, 43.0)
-KEEP_AT = (22.0, 59.0)
-STEPS_AT = ((21.0, 29.0), (30.0, 39.0), (42.0, 47.9), (48.5, 66.5), (66.2, 90.0), (74.0, 95.0))
-FINISH_AT = (99.0, 100.0)
-GRADS_AT = 48.0
-JOIN_WAIT = 18.0
-RELAY_WAIT = 14.0
-SIDE_WAIT = 20.0
+SEND_AT = (9.0, 21.9)
+KEEP_AT = (32.5, 55.3)
+STEPS_AT = ((21.7, 26.6), (30.0, 39.0), (42.0, 48.5), (52.0, 60.0), (61.0, 77.0), (72.3, 79.4))
+FINISH_AT = (97.5, 100.0)
+SQUARE_AT = (101.1, 200.0)
+GRADS_AT = 45.9
+JOIN_WAIT = 9.5
+RELAY_WAIT = 20.1
+SIDE_WAIT = 24.0
 ACROSS_WAIT = 100.0
-EXPECTED = {("g", 0): 9.5, ("a", 0, 0): 18.0, ("a", 0, 1): 28.0}
+EXPECTED = {("g", 0): 9.5, ("a", 0, 0): 15.4, ("a", 0, 1): 24.5, ("a", 1, 0): 8.5, ("a", 1, 1): 23.2}
 
 
 def decode(ref, rows):
@@ -57,7 +58,7 @@
         self.expected = [(due, array) for due, array in self.expected if due > self.clock]
         return self.last + arrived
 
-    def call(self, body, out_shape, inputs, specs, out_specs=None, scratch=(), limit=12 * MIB, aliases=None, carry=()):
+    def call(self, body, out_shape, inputs, specs, out_specs=None, scratch=(), limit=8 * MIB, aliases=None, carry=()):
         unread = self.waited_for()
         deps = len(unread)
 
@@ -83,9 +84,10 @@
         self.last = [outs[0]]
         return outs
 
-    def rotate(self, order, x, basis, width, start, stride, per_step, chunks, dtype, limit=32 * MIB):
+    def rotate(self, order, part, x, basis, width, start, stride, per_step, chunks, dtype):
         tokens, features = x.shape
-        count = order.shape[0]
+        count = order.shape[0] // 2
+        first = part * count
         rows = tokens // chunks
         unread = self.waited_for()
         deps = len(unread)
@@ -102,7 +104,7 @@
 
         def column_spec(at):
             return pl.BlockSpec(
-                (features, width), lambda step, order: (0, order[step * per_step + at] * stride + start)
+                (features, width), lambda step, order: (0, order[first + step * per_step + at] * stride + start)
             )
 
         outs = pl.pallas_call(
@@ -110,13 +112,13 @@
             grid_spec=pltpu.PrefetchScalarGridSpec(
                 num_scalar_prefetch=1,
                 grid=(count // per_step,),
-                in_specs=[pl.BlockSpec((tokens, features), lambda step, order: (0, 0))]
+                in_specs=[VMEM]
                 + [column_spec(at) for at in range(per_step)]
                 + [ANY] * deps,
                 out_specs=[pl.BlockSpec((per_step, rows, width), lambda step, order: (step, 0, 0))] * chunks,
             ),
             out_shape=[jax.ShapeDtypeStruct((count, rows, width), dtype)] * chunks,
-            compiler_params=pltpu.CompilerParams(vmem_limit_bytes=limit),
+            compiler_params=pltpu.CompilerParams(vmem_limit_bytes=24 * MIB),
             cost_estimate=LIGHT,
         )(order, x, *[basis] * per_step, *unread)
         self.last = [outs[0]]
@@ -211,22 +213,21 @@
 
         return self.call(body, [jax.ShapeDtypeStruct((8, LANES), jnp.float32)], [], [], carry=[x])[1]
 
-    def moments(self, place, grads, acts, out_shape):
+    def moments(self, place, grads, acts, block, out_shape, earlier=None):
         rows, tokens = grads[0].shape[2:]
         count = sum(x.shape[0] for x in grads)
-        blocks = len(acts)
-        flat_acts = [x for block in acts for chunk in block for x in chunk]
+        flat_acts = [x for chunk in acts for x in chunk]
+        wide = flat_acts[0].shape[1]
         scale = 1.0 / SEQ_LEN**0.5
 
         def body(place_ref, *refs):
             grad_refs = refs[: len(grads)]
             act_refs = refs[len(grads) : len(grads) + len(flat_acts)]
-            out_ref, result_ref, sems = refs[-3:]
+            token_ref, out_ref, result_ref, sems = refs[-4:]
+            token_ref[...] = jnp.zeros_like(token_ref)
             total = None
             for seq in range(SEQS):
-                own = iter(act_refs[seq::SEQS])
-                columns = [[next(own)[...] for _ in range(len(acts[block]))] for block in range(blocks)]
-                act = jnp.concatenate([jnp.concatenate(column, axis=0) for column in columns], axis=1)
+                act = jnp.concatenate([ref[...] for ref in act_refs[seq::SEQS]], axis=0)
                 high = act.astype(jnp.bfloat16)
                 low = (act - high.astype(jnp.float32)).astype(jnp.bfloat16)
                 grad = jnp.concatenate([ref[:, seq].reshape(-1, tokens) for ref in grad_refs], axis=0)
@@ -239,10 +240,9 @@
             copies = []
             for at in range(count):
                 start = pl.multiple_of(place_ref[at] * rows, rows)
+                target = out_ref.at[pl.ds(start, rows), pl.ds(block * wide, wide)]
                 copies.append(
-                    pltpu.make_async_copy(
-                        result_ref.at[pl.ds(at * rows, rows)], out_ref.at[pl.ds(start, rows)], sems.at[at]
-                    )
+                    pltpu.make_async_copy(result_ref.at[pl.ds(at * rows, rows)], target, sems.at[at])
                 )
                 copies[-1].start()
             for copy in copies:
@@ -250,18 +250,21 @@
 
         inputs = [place, *grads, *flat_acts]
         specs = [SMEM] + [VMEM] * (len(inputs) - 1)
+        aliases = {}
+        if earlier is not None:
+            aliases = {len(inputs): 1}
+            inputs.append(earlier)
+            specs.append(ANY)
         return self.call(
             body,
-            [out_shape],
+            [jax.ShapeDtypeStruct((8, LANES), jnp.float32), out_shape],
             inputs,
             specs,
-            out_specs=[ANY],
-            scratch=[
-                pltpu.VMEM((count * rows, out_shape.shape[1]), jnp.float32),
-                pltpu.SemaphoreType.DMA((count,)),
-            ],
-            limit=24 * MIB,
-        )[0]
+            out_specs=[VMEM, ANY],
+            scratch=[pltpu.VMEM((count * rows, wide), jnp.float32), pltpu.SemaphoreType.DMA((count,))],
+            limit=16 * MIB,
+            aliases=aliases,
+        )[1]
 
 
 def rotate_narrow(order, x, basis, width, start, slices, dtype):
@@ -298,7 +301,6 @@
     grad_keys = [("g", 0), ("g", 1)]
     act_keys = [("a", block, chunk) for block in range(blocks) for chunk in range(TOKEN_CHUNKS)]
     order = jnp.array(halving_order(n, bits), jnp.int32) ^ me
-    orders = (order[: n // 2], order[n // 2 :])
     kept, received, finished, gathered = {}, {}, {}, {}
     def keep_or_send(key, x, part):
         if part == 0:
@@ -308,18 +310,16 @@
 
     def rotate_grads(half, part):
         key = ("g", half)
-        order = orders[part]
         dtype = (jnp.bfloat16, jnp.float32)[part]
         if width_g % LANES == 0:
-            (x,) = chain.rotate(order, x_g, basis_g, width_g, half * n, 1, order.shape[0], 1, dtype, 60 * MIB)
+            (x,) = chain.rotate(order, part, x_g, basis_g, width_g, half * n, 1, n // 2, 1, dtype)
         else:
-            (x,) = rotate_narrow(order, x_g, basis_g, width_g, half * n, n, dtype)
+            (x,) = rotate_narrow(order[part * n // 2 : (part + 1) * n // 2], x_g, basis_g, width_g, half * n, n, dtype)
         keep_or_send(key, x, part)
 
     def rotate_acts(block, part):
-        order = orders[part]
         dtype = (jnp.bfloat16, jnp.float32)[part]
-        outs = chain.rotate(order, x_a, basis_a, wide, block, blocks, 2, TOKEN_CHUNKS, dtype)
+        outs = chain.rotate(order, part, x_a, basis_a, wide, block, blocks, 2, TOKEN_CHUNKS, dtype)
         for chunk, x in enumerate(outs):
             keep_or_send(("a", block, chunk), x, part)
 
@@ -381,16 +381,22 @@
         clock += JOIN_WAIT
         tasks.append((clock, join_grads, (bit,)))
     tasks.append((clock + RELAY_WAIT, relay_grads, ()))
+    out_shape = jax.ShapeDtypeStruct((n * width_g, width_a), jnp.float32)
+    result = []
+
+    def square(block):
+        low = gathered["order"]
+        offsets = low + [at ^ 2 for at in low] + [at ^ 1 for at in low] + [at ^ 3 for at in low]
+        place = jnp.array(offsets, jnp.int32) ^ me
+        grads = [gathered[name] for name in ("held", "in", "side", "across")]
+        earlier = result[-1] if result else None
+        result.append(chain.moments(place, grads, finished[block], block, out_shape, earlier))
+
+    for block in range(blocks):
+        tasks.append((SQUARE_AT[block] + 8.0 * (bits - 3), square, (block,)))
     for chain.clock, task, arguments in sorted(tasks, key=lambda task: task[0]):
         task(*arguments)
-
-    low = gathered["order"]
-    offsets = low + [at ^ 2 for at in low] + [at ^ 1 for at in low] + [at ^ 3 for at in low]
-    place = jnp.array(offsets, jnp.int32) ^ me
-    act_blocks = [finished[block] for block in range(blocks)]
-    out_shape = jax.ShapeDtypeStruct((n * width_g, width_a), jnp.float32)
-    grads = [gathered[name] for name in ("held", "in", "side", "across")]
-    return chain.moments(place, grads, act_blocks, out_shape)
+    return result[-1]
 
 
 def solution(mesh):

time: 144 us -> 126 us (0.88)
  Pallas kernels: 55.8 us -> 43.1 us
  starting transfers between devices: 32.4 us -> 29.8 us
  local copies, waits for them, and re-layouts: 7.6 us -> 5.76 us
    pallas_call x8, Pallas kernels: 44.1 us -> 33.6 us  [rotate(): pl.pallas_call(kernel, grid_spec=pltpu.PrefetchScalarGridSpec(num_scalar_...]
    ppermute x22, starting transfers between devices: 31.2 us -> 28.6 us  [swap(): lax.ppermute(x, 'inp', [(index, index ^ 1 << bit) for index in range(n)])]
    pallas_call x19 -> x20, Pallas kernels: 11.7 us -> 9.5 us  [call(): pl.pallas_call(kernel, out_shape=list(out_shape) + [jax.ShapeDtypeStruct(...]
    unnamed x32 -> x20, local copies, waits for them, and re-layouts: 7.01 us -> 5.76 us
  transfers between devices with their start and end apart: 27 -> 27, of which waited for: 11 -> 11; matrix products, arithmetic and copies ran while one was open for 1% -> 1% of each run, Pallas kernels for 33% -> 30%
where the time goes in v5:
time: 126 us
  waiting for transfers between devices  43.4 us (34%)
  Pallas kernels  43.1 us (34%)
  starting transfers between devices  29.8 us (24%)
  local copies, waits for them, and re-layouts  5.76 us (5%)
  other arithmetic  2.38 us (2%)
  between operations  1.33 us (1%)
    ppermute x22, waiting for transfers between devices, swap(): lax.ppermute(x, 'inp', [(index, index ^ 1 << bit) for index in range(n)])  42.2 us
    pallas_call x8, Pallas kernels, rotate(): pl.pallas_call(kernel, grid_spec=pltpu.PrefetchScalarGridSpec(num_scalar_...  33.6 us
    ppermute x22, starting transfers between devices, swap(): lax.ppermute(x, 'inp', [(index, index ^ 1 << bit) for index in range(n)])  28.6 us
    pallas_call x20, Pallas kernels, call(): pl.pallas_call(kernel, out_shape=list(out_shape) + [jax.ShapeDtypeStruct(...  9.5 us
    unnamed x20, local copies, waits for them, and re-layouts  5.76 us
  transfers between devices with their start and end apart: 27, of which 11 were waited for; matrix products, arithmetic and copies ran while one was open for 1% of the time, Pallas kernels for 30%

profile of v5, /device:TPU:0, one launch (start us, length us, event | category | flops | bytes accessed | tf_op | source)
XLA Modules:
  0.0 125.8 jit_solution(8494976021217585288)
XLA Ops:
  0.7 2.2 %copy-done = bf16[1024,2048]{1,0:T(8,128)(2,1)S(1)} copy-done((bf16[1024,2048]{1,0:T(8,128)(2,1)S(1)}, bf16[1024,2048]{1,0:T(8,128)(2,1)}, u32[]{:S(2)}) %copy-start) | copy-done | bytes 4194328
  5.5 3.0 %collective-permute-start = (bf16[4,512,128]{2,1,0:T(8,128)(2,1)S(1)}, bf16[4,512,128]{2,1,0:T(8,128)(2,1)S(1)}, u32[]{:S(2)}, u32[]{:S(2)}) collective-permute-start(bf16[4,512,128]{2,1,0:T(8,128)(2,1)S(1)} %shard_map.82.refs_4_), channel_id=1, source_target_pairs={{0,2},{2,0},{4,6},{6,4},{8,10},{10,8},{12,14},{14,12},{1,3},{3,1},... | collective-permute-start | bytes 1572872 | tf_op jit(solution)/shard_map/ppermute | solution.py:282
  13.5 7.5 %shard_map.86 = (bf16[4,256,256]{2,1,0:T(8,128)(2,1)}, bf16[4,256,256]{2,1,0:T(8,128)(2,1)}) custom-call(s32[8]{0:T(128)S(1)} %broadcast_xor_fusion.order_ref, bf16[512,3584]{1,0:T(8,128)(2,1)S(1)} %bitcast.3, bf16[3584,4096]{1,0:T(8,128)(2,1)} %refs_1_.15, bf16[3584,4096]{1,0:T(8,128)(2,1)} %refs_1_.15, f32[4,512,128]{2,1,0:T(8,128)S(1)} %shard_map.85.refs_2_.refs_1_), custom_call_target="tpu_custom_call" | custom-call | bytes 131072 | tf_op jit(solution)/shard_map/pallas_call | solution.py:110
  21.4 2.2 %collective-permute-start.1 = (bf16[2,512,128]{2,1,0:T(8,128)(2,1)S(1)}, bf16[2,512,128]{2,1,0:T(8,128)(2,1)S(1)}, u32[]{:S(2)}, u32[]{:S(2)}) collective-permute-start(bf16[2,512,128]{2,1,0:T(8,128)(2,1)S(1)} %get-tuple-element.49.refs_2_), channel_id=1, source_target_pairs={{0,4},{2,6},{4,0},{6,2},{8,12},{10,14},{12,8},{14,10},{1,5},{3,7},... | collective-permute-start | bytes 786440 | tf_op jit(solution)/shard_map/ppermute | solution.py:282
  23.6 1.5 %collective-permute-start.6 = (bf16[4,256,256]{2,1,0:T(8,128)(2,1)}, bf16[4,256,256]{2,1,0:T(8,128)(2,1)S(1)}, u32[]{:S(2)}, u32[]{:S(2)}) collective-permute-start(bf16[4,256,256]{2,1,0:T(8,128)(2,1)} %get-tuple-element.48.refs_2_), channel_id=1, source_target_pairs={{0,2},{2,0},{4,6},{6,4},{8,10},{10,8},{12,14},{14,12},{1,3},{3,1},... | collective-permute-start | bytes 1572872 | tf_op jit(solution)/shard_map/ppermute | solution.py:282
  25.1 6.8 %shard_map.88 = (bf16[4,256,256]{2,1,0:T(8,128)(2,1)S(1)}, bf16[4,256,256]{2,1,0:T(8,128)(2,1)S(1)}) custom-call(s32[8]{0:T(128)S(1)} %broadcast_xor_fusion.order_ref, bf16[512,3584]{1,0:T(8,128)(2,1)S(1)} %bitcast.4, bf16[3584,4096]{1,0:T(8,128)(2,1)} %refs_1_.15, bf16[3584,4096]{1,0:T(8,128)(2,1)} %refs_1_.15, ...), custom_call_target="tpu_custom_call" | custom-call | bytes 131072 | tf_op jit(solution)/shard_map/pallas_call | solution.py:110
  32.7 2.1 %collective-permute-start.4 = (bf16[2,512,128]{2,1,0:T(8,128)(2,1)S(1)}, bf16[2,512,128]{2,1,0:T(8,128)(2,1)S(1)}, u32[]{:S(2)}, u32[]{:S(2)}) collective-permute-start(bf16[2,512,128]{2,1,0:T(8,128)(2,1)S(1)} %get-tuple-element.53.refs_2_), channel_id=1, source_target_pairs={{0,4},{2,6},{4,0},{6,2},{8,12},{10,14},{12,8},{14,10},{1,5},{3,7},... | collective-permute-start | bytes 786440 | tf_op jit(solution)/shard_map/ppermute | solution.py:282
  34.8 2.7 %collective-permute-start.2 = (f16[1,528,128]{2,1,0:T(8,128)(2,1)S(1)}, f16[1,528,128]{2,1,0:T(8,128)(2,1)S(1)}, u32[]{:S(2)}, u32[]{:S(2)}) collective-permute-start(f16[1,528,128]{2,1,0:T(8,128)(2,1)S(1)} %convert_element_type.12), channel_id=1, source_target_pairs={{0,8},{2,10},{4,12},{6,14},{8,0},{10,2},{12,4},{14,6},{1,9},{3,11}... | collective-permute-start | bytes 405512 | tf_op jit(solution)/shard_map/ppermute | solution.py:282
  37.5 6.8 %shard_map.91 = (f32[4,256,256]{2,1,0:T(8,128)S(1)}, f32[4,256,256]{2,1,0:T(8,128)S(1)}) custom-call(s32[8]{0:T(128)S(1)} %broadcast_xor_fusion.order_ref, bf16[512,3584]{1,0:T(8,128)(2,1)S(1)} %bitcast.5, bf16[3584,4096]{1,0:T(8,128)(2,1)} %refs_1_.15, bf16[3584,4096]{1,0:T(8,128)(2,1)} %refs_1_.15, bf16[2,512,128]{2,1,0:T(8,128)(2,1)S(1)} %get-tuple-element.53.refs_2_), custom_call_target="tpu_custom_call" | custom-call | bytes 131072 | tf_op jit(solution)/shard_map/pallas_call | solution.py:110
  46.3 1.5 %collective-permute-start.9 = (bf16[4,256,256]{2,1,0:T(8,128)(2,1)}, bf16[4,256,256]{2,1,0:T(8,128)(2,1)}, u32[]{:S(2)}, u32[]{:S(2)}) collective-permute-start(bf16[4,256,256]{2,1,0:T(8,128)(2,1)} %get-tuple-element.62), channel_id=1, source_target_pairs={{0,2},{2,0},{4,6},{6,4},{8,10},{10,8},{12,14},{14,12},{1,3},{3,1},... | collective-permute-start | bytes 1572872 | tf_op jit(solution)/shard_map/ppermute | solution.py:282
  48.8 4.8 %collective-permute-done.5 = f16[1,528,128]{2,1,0:T(8,128)(2,1)} collective-permute-done((f16[1,528,128]{2,1,0:T(8,128)(2,1)}, f16[1,528,128]{2,1,0:T(8,128)(2,1)}, u32[]{:S(2)}, u32[]{:S(2)}) %collective-permute-start.5) | collective-permute-done | bytes 135200 | tf_op jit(solution)/shard_map/ppermute | solution.py:282
  58.4 1.5 %collective-permute-start.12 = (bf16[4,256,256]{2,1,0:T(8,128)(2,1)S(1)}, bf16[4,256,256]{2,1,0:T(8,128)(2,1)S(1)}, u32[]{:S(2)}, u32[]{:S(2)}) collective-permute-start(bf16[4,256,256]{2,1,0:T(8,128)(2,1)S(1)} %copy-done.5), channel_id=1, source_target_pairs={{0,2},{2,0},{4,6},{6,4},{8,10},{10,8},{12,14},{14,12},{1,3},{3,1},... | collective-permute-start | bytes 1572872 | tf_op jit(solution)/shard_map/ppermute | solution.py:282
  60.5 7.9 %collective-permute-done.10.refs_0_ = bf16[2,256,256]{2,1,0:T(8,128)(2,1)S(1)} collective-permute-done((bf16[2,256,256]{2,1,0:T(8,128)(2,1)S(1)}, bf16[2,256,256]{2,1,0:T(8,128)(2,1)S(1)}, u32[]{:S(2)}, u32[]{:S(2)}) %collective-permute-start.10) | collective-permute-done | bytes 262176 | tf_op jit(solution)/shard_map/ppermute | solution.py:282
  69.7 6.8 %shard_map.98 = (f32[4,256,256]{2,1,0:T(8,128)S(1)}, f32[4,256,256]{2,1,0:T(8,128)S(1)}) custom-call(s32[8]{0:T(128)S(1)} %broadcast_xor_fusion.order_ref, bf16[512,3584]{1,0:T(8,128)(2,1)S(1)} %bitcast.6, bf16[3584,4096]{1,0:T(8,128)(2,1)} %refs_1_.15, bf16[3584,4096]{1,0:T(8,128)(2,1)} %refs_1_.15, bf16[2,256,256]{2,1,0:T(8,128)(2,1)S(1)} %get-tuple-element.66.refs_2_), custom_call_target="tpu_custom_call" | custom-call | bytes 131072 | tf_op jit(solution)/shard_map/pallas_call | solution.py:110
  76.5 2.1 %collective-permute-start.15 = (bf16[2,2,128,512]{3,2,1,0:T(8,128)(2,1)S(1)}, bf16[2,2,128,512]{3,2,1,0:T(8,128)(2,1)S(1)}, u32[]{:S(2)}, u32[]{:S(2)}) collective-permute-start(bf16[2,2,128,512]{3,2,1,0:T(8,128)(2,1)S(1)} %shard_map.99.refs_2_.refs_1_), channel_id=1, source_target_pairs={{0,4},{2,6},{4,0},{6,2},{8,12},{10,14},{12,8},{14,10},{1,5},{3,7},... | collective-permute-start | bytes 1572872 | tf_op jit(solution)/shard_map/ppermute | solution.py:282
  78.6 1.5 %collective-permute-start.16 = (bf16[2,2,128,512]{3,2,1,0:T(8,128)(2,1)S(1)}, bf16[2,2,128,512]{3,2,1,0:T(8,128)(2,1)S(1)}, u32[]{:S(2)}, u32[]{:S(2)}) collective-permute-start(bf16[2,2,128,512]{3,2,1,0:T(8,128)(2,1)S(1)} %shard_map.99.refs_2_.refs_1_), channel_id=1, source_target_pairs={{0,2},{2,0},{4,6},{6,4},{8,10},{10,8},{12,14},{14,12},{1,3},{3,1},... | collective-permute-start | bytes 1572872 | tf_op jit(solution)/shard_map/ppermute | solution.py:282
  81.4 2.0 %collective-permute-start.18 = (bf16[2,256,256]{2,1,0:T(8,128)(2,1)S(1)}, bf16[2,256,256]{2,1,0:T(8,128)(2,1)S(1)}, u32[]{:S(2)}, u32[]{:S(2)}) collective-permute-start(bf16[2,256,256]{2,1,0:T(8,128)(2,1)S(1)} %get-tuple-element.72.refs_2_), channel_id=1, source_target_pairs={{0,4},{2,6},{4,0},{6,2},{8,12},{10,14},{12,8},{14,10},{1,5},{3,7},... | collective-permute-start | bytes 786440 | tf_op jit(solution)/shard_map/ppermute | solution.py:282
  84.5 9.3 %collective-permute-done.14.refs_3_.refs_0_ = bf16[1,256,256]{2,1,0:T(8,128)(2,1)S(1)} collective-permute-done((bf16[1,256,256]{2,1,0:T(8,128)(2,1)S(1)}, bf16[1,256,256]{2,1,0:T(8,128)(2,1)S(1)}, u32[]{:S(2)}, u32[]{:S(2)}) %collective-permute-start.14) | collective-permute-done | bytes 131104 | tf_op jit(solution)/shard_map/ppermute | solution.py:282
  93.9 3.6 %collective-permute-start.20 = (bf16[2,256,256]{2,1,0:T(8,128)(2,1)S(1)}, bf16[2,256,256]{2,1,0:T(8,128)(2,1)S(1)}, u32[]{:S(2)}, u32[]{:S(2)}) collective-permute-start(bf16[2,256,256]{2,1,0:T(8,128)(2,1)S(1)} %get-tuple-element.73.refs_0_), channel_id=1, source_target_pairs={{0,4},{2,6},{4,0},{6,2},{8,12},{10,14},{12,8},{14,10},{1,5},{3,7},... | collective-permute-start | bytes 786440 | tf_op jit(solution)/shard_map/ppermute | solution.py:282
  99.0 3.7 %collective-permute-done.18.refs_0_ = bf16[2,256,256]{2,1,0:T(8,128)(2,1)S(1)} collective-permute-done((bf16[2,256,256]{2,1,0:T(8,128)(2,1)S(1)}, bf16[2,256,256]{2,1,0:T(8,128)(2,1)S(1)}, u32[]{:S(2)}, u32[]{:S(2)}) %collective-permute-start.18) | collective-permute-done | bytes 262176 | tf_op jit(solution)/shard_map/ppermute | solution.py:282
  103.1 5.8 %collective-permute-done.20.refs_0_ = bf16[2,256,256]{2,1,0:T(8,128)(2,1)S(1)} collective-permute-done((bf16[2,256,256]{2,1,0:T(8,128)(2,1)S(1)}, bf16[2,256,256]{2,1,0:T(8,128)(2,1)S(1)}, u32[]{:S(2)}, u32[]{:S(2)}) %collective-permute-start.20) | collective-permute-done | bytes 262176 | tf_op jit(solution)/shard_map/ppermute | solution.py:282
  109.1 7.6 %collective-permute-done.19.refs_7_.refs_0_ = bf16[1,256,256]{2,1,0:T(8,128)(2,1)S(1)} collective-permute-done((bf16[1,256,256]{2,1,0:T(8,128)(2,1)S(1)}, bf16[1,256,256]{2,1,0:T(8,128)(2,1)S(1)}, u32[]{:S(2)}, u32[]{:S(2)}) %collective-permute-start.19) | collective-permute-done | bytes 131104 | tf_op jit(solution)/shard_map/ppermute | solution.py:282
  119.3 2.8 %shard_map.108 = (f32[8,128]{1,0:T(8,128)S(1)}, f32[1024,512]{1,0:T(8,128)}) custom-call(s32[8]{0:T(128)S(1)} %broadcast_xor_fusion.1.refs_0_, bf16[2,2,128,512]{3,2,1,0:T(8,128)(2,1)S(1)} %shard_map.99.refs_2_.refs_1_, bf16[2,2,128,512]{3,2,1,0:T(8,128)(2,1)S(1)} %get-tuple-element.74.refs_2_, ...), custom_call_target="tpu_custom_call" | custom-call | bytes 131072 | tf_op jit(solution)/shard_map/pallas_call | solution.py:74
  122.2 3.4 %shard_map.109 = (f32[8,128]{1,0:T(8,128)}, f32[1024,512]{1,0:T(8,128)}) custom-call(s32[8]{0:T(128)S(1)} %broadcast_xor_fusion.1.refs_0_, bf16[2,2,128,512]{3,2,1,0:T(8,128)(2,1)S(1)} %shard_map.99.refs_2_.refs_1_, bf16[2,2,128,512]{3,2,1,0:T(8,128)(2,1)S(1)} %get-tuple-element.74.refs_2_, ...), custom_call_target="tpu_custom_call", output_to_operand_aliasing={{1}: (9, {})} | custom-call | bytes 131072 | tf_op jit(solution)/shard_map/pallas_call | solution.py:74
  (85 shorter events, 25.2 us)
Async XLA Ops:
  5.5 15.8 %collective-permute-start = (bf16[4,512,128]{2,1,0:T(8,128)(2,1)S(1)}, bf16[4,512,128]{2,1,0:T(8,128)(2,1)S(1)}, u32[]{:S(2)}, u32[]{:S(2)}) collective-permute-start(bf16[4,512,128]{2,1,0:T(8,128)(2,1)S(1)} %shard_map.82.refs_4_), channel_id=1, source_target_pairs={{0,2},{2,0},{4,6},{6,4},{8,10},{10,8},{12,14},{14,12},{1,3},{3,1},... | collective-permute-start | bytes 1572872 | tf_op jit(solution)/shard_map/ppermute | solution.py:282
  10.0 22.6 %collective-permute-start.3 = (bf16[4,512,128]{2,1,0:T(8,128)(2,1)S(1)}, bf16[4,512,128]{2,1,0:T(8,128)(2,1)S(1)}, u32[]{:S(2)}, u32[]{:S(2)}) collective-permute-start(bf16[4,512,128]{2,1,0:T(8,128)(2,1)S(1)} %shard_map.83.refs_4_), channel_id=1, source_target_pairs={{0,2},{2,0},{4,6},{6,4},{8,10},{10,8},{12,14},{14,12},{1,3},{3,1},... | collective-permute-start | bytes 1572872 | tf_op jit(solution)/shard_map/ppermute | solution.py:282
  21.4 10.5 %collective-permute-start.1 = (bf16[2,512,128]{2,1,0:T(8,128)(2,1)S(1)}, bf16[2,512,128]{2,1,0:T(8,128)(2,1)S(1)}, u32[]{:S(2)}, u32[]{:S(2)}) collective-permute-start(bf16[2,512,128]{2,1,0:T(8,128)(2,1)S(1)} %get-tuple-element.49.refs_2_), channel_id=1, source_target_pairs={{0,4},{2,6},{4,0},{6,2},{8,12},{10,14},{12,8},{14,10},{1,5},{3,7},... | collective-permute-start | bytes 786440 | tf_op jit(solution)/shard_map/ppermute | solution.py:282
  23.6 25.1 %collective-permute-start.6 = (bf16[4,256,256]{2,1,0:T(8,128)(2,1)}, bf16[4,256,256]{2,1,0:T(8,128)(2,1)S(1)}, u32[]{:S(2)}, u32[]{:S(2)}) collective-permute-start(bf16[4,256,256]{2,1,0:T(8,128)(2,1)} %get-tuple-element.48.refs_2_), channel_id=1, source_target_pairs={{0,2},{2,0},{4,6},{6,4},{8,10},{10,8},{12,14},{14,12},{1,3},{3,1},... | collective-permute-start | bytes 1572872 | tf_op jit(solution)/shard_map/ppermute | solution.py:282
  32.7 11.6 %collective-permute-start.4 = (bf16[2,512,128]{2,1,0:T(8,128)(2,1)S(1)}, bf16[2,512,128]{2,1,0:T(8,128)(2,1)S(1)}, u32[]{:S(2)}, u32[]{:S(2)}) collective-permute-start(bf16[2,512,128]{2,1,0:T(8,128)(2,1)S(1)} %get-tuple-element.53.refs_2_), channel_id=1, source_target_pairs={{0,4},{2,6},{4,0},{6,2},{8,12},{10,14},{12,8},{14,10},{1,5},{3,7},... | collective-permute-start | bytes 786440 | tf_op jit(solution)/shard_map/ppermute | solution.py:282
  34.8 9.5 %collective-permute-start.2 = (f16[1,528,128]{2,1,0:T(8,128)(2,1)S(1)}, f16[1,528,128]{2,1,0:T(8,128)(2,1)S(1)}, u32[]{:S(2)}, u32[]{:S(2)}) collective-permute-start(f16[1,528,128]{2,1,0:T(8,128)(2,1)S(1)} %convert_element_type.12), channel_id=1, source_target_pairs={{0,8},{2,10},{4,12},{6,14},{8,0},{10,2},{12,4},{14,6},{1,9},{3,11}... | collective-permute-start | bytes 405512 | tf_op jit(solution)/shard_map/ppermute | solution.py:282
  45.9 7.6 %collective-permute-start.5 = (f16[1,528,128]{2,1,0:T(8,128)(2,1)}, f16[1,528,128]{2,1,0:T(8,128)(2,1)}, u32[]{:S(2)}, u32[]{:S(2)}) collective-permute-start(f16[1,528,128]{2,1,0:T(8,128)(2,1)} %convert_element_type.14), channel_id=1, source_target_pairs={{0,8},{2,10},{4,12},{6,14},{8,0},{10,2},{12,4},{14,6},{1,9},{3,11}... | collective-permute-start | bytes 405512 | tf_op jit(solution)/shard_map/ppermute | solution.py:282
  46.3 22.2 %collective-permute-start.9 = (bf16[4,256,256]{2,1,0:T(8,128)(2,1)}, bf16[4,256,256]{2,1,0:T(8,128)(2,1)}, u32[]{:S(2)}, u32[]{:S(2)}) collective-permute-start(bf16[4,256,256]{2,1,0:T(8,128)(2,1)} %get-tuple-element.62), channel_id=1, source_target_pairs={{0,2},{2,0},{4,6},{6,4},{8,10},{10,8},{12,14},{14,12},{1,3},{3,1},... | collective-permute-start | bytes 1572872 | tf_op jit(solution)/shard_map/ppermute | solution.py:282
  56.4 12.0 %collective-permute-start.10 = (bf16[2,256,256]{2,1,0:T(8,128)(2,1)S(1)}, bf16[2,256,256]{2,1,0:T(8,128)(2,1)S(1)}, u32[]{:S(2)}, u32[]{:S(2)}) collective-permute-start(bf16[2,256,256]{2,1,0:T(8,128)(2,1)S(1)} %get-tuple-element.59.refs_5_), channel_id=1, source_target_pairs={{0,4},{2,6},{4,0},{6,2},{8,12},{10,14},{12,8},{14,10},{1,5},{3,7},... | collective-permute-start | bytes 786440 | tf_op jit(solution)/shard_map/ppermute | solution.py:282
  57.8 18.7 %collective-permute-start.8 = (bf16[1,2,128,512]{3,2,1,0:T(8,128)(2,1)S(1)}, bf16[1,2,128,512]{3,2,1,0:T(8,128)(2,1)S(1)}, u32[]{:S(2)}, u32[]{:S(2)}) collective-permute-start(bf16[1,2,128,512]{3,2,1,0:T(8,128)(2,1)S(1)} %shard_map.95.refs_2_.refs_0_), channel_id=1, source_target_pairs={{0,8},{2,10},{4,12},{6,14},{8,0},{10,2},{12,4},{14,6},{1,9},{3,11}... | collective-permute-start | bytes 786440 | tf_op jit(solution)/shard_map/ppermute | solution.py:282
  58.4 22.8 %collective-permute-start.12 = (bf16[4,256,256]{2,1,0:T(8,128)(2,1)S(1)}, bf16[4,256,256]{2,1,0:T(8,128)(2,1)S(1)}, u32[]{:S(2)}, u32[]{:S(2)}) collective-permute-start(bf16[4,256,256]{2,1,0:T(8,128)(2,1)S(1)} %copy-done.5), channel_id=1, source_target_pairs={{0,2},{2,0},{4,6},{6,4},{8,10},{10,8},{12,14},{14,12},{1,3},{3,1},... | collective-permute-start | bytes 1572872 | tf_op jit(solution)/shard_map/ppermute | solution.py:282
  60.0 24.5 %collective-permute-start.11 = (bf16[4,256,256]{2,1,0:T(8,128)(2,1)}, bf16[4,256,256]{2,1,0:T(8,128)(2,1)S(1)}, u32[]{:S(2)}, u32[]{:S(2)}) collective-permute-start(bf16[4,256,256]{2,1,0:T(8,128)(2,1)} %copy-done.8), channel_id=1, source_target_pairs={{0,2},{2,0},{4,6},{6,4},{8,10},{10,8},{12,14},{14,12},{1,3},{3,1},... | collective-permute-start | bytes 1572872 | tf_op jit(solution)/shard_map/ppermute | solution.py:282
  69.6 10.5 %collective-permute-start.13 = (bf16[2,256,256]{2,1,0:T(8,128)(2,1)S(1)}, bf16[2,256,256]{2,1,0:T(8,128)(2,1)S(1)}, u32[]{:S(2)}, u32[]{:S(2)}) collective-permute-start(bf16[2,256,256]{2,1,0:T(8,128)(2,1)S(1)} %get-tuple-element.66.refs_2_), channel_id=1, source_target_pairs={{0,4},{2,6},{4,0},{6,2},{8,12},{10,14},{12,8},{14,10},{1,5},{3,7},... | collective-permute-start | bytes 786440 | tf_op jit(solution)/shard_map/ppermute | solution.py:282
  76.5 21.0 %collective-permute-start.15 = (bf16[2,2,128,512]{3,2,1,0:T(8,128)(2,1)S(1)}, bf16[2,2,128,512]{3,2,1,0:T(8,128)(2,1)S(1)}, u32[]{:S(2)}, u32[]{:S(2)}) collective-permute-start(bf16[2,2,128,512]{3,2,1,0:T(8,128)(2,1)S(1)} %shard_map.99.refs_2_.refs_1_), channel_id=1, source_target_pairs={{0,4},{2,6},{4,0},{6,2},{8,12},{10,14},{12,8},{14,10},{1,5},{3,7},... | collective-permute-start | bytes 1572872 | tf_op jit(solution)/shard_map/ppermute | solution.py:282
  78.6 30.5 %collective-permute-start.16 = (bf16[2,2,128,512]{3,2,1,0:T(8,128)(2,1)S(1)}, bf16[2,2,128,512]{3,2,1,0:T(8,128)(2,1)S(1)}, u32[]{:S(2)}, u32[]{:S(2)}) collective-permute-start(bf16[2,2,128,512]{3,2,1,0:T(8,128)(2,1)S(1)} %shard_map.99.refs_2_.refs_1_), channel_id=1, source_target_pairs={{0,2},{2,0},{4,6},{6,4},{8,10},{10,8},{12,14},{14,12},{1,3},{3,1},... | collective-permute-start | bytes 1572872 | tf_op jit(solution)/shard_map/ppermute | solution.py:282
  80.1 13.7 %collective-permute-start.14 = (bf16[1,256,256]{2,1,0:T(8,128)(2,1)S(1)}, bf16[1,256,256]{2,1,0:T(8,128)(2,1)S(1)}, u32[]{:S(2)}, u32[]{:S(2)}) collective-permute-start(bf16[1,256,256]{2,1,0:T(8,128)(2,1)S(1)} %get-tuple-element.65.refs_2_), channel_id=1, source_target_pairs={{0,8},{2,10},{4,12},{6,14},{8,0},{10,2},{12,4},{14,6},{1,9},{3,11}... | collective-permute-start | bytes 393224 | tf_op jit(solution)/shard_map/ppermute | solution.py:282
  81.4 21.3 %collective-permute-start.18 = (bf16[2,256,256]{2,1,0:T(8,128)(2,1)S(1)}, bf16[2,256,256]{2,1,0:T(8,128)(2,1)S(1)}, u32[]{:S(2)}, u32[]{:S(2)}) collective-permute-start(bf16[2,256,256]{2,1,0:T(8,128)(2,1)S(1)} %get-tuple-element.72.refs_2_), channel_id=1, source_target_pairs={{0,4},{2,6},{4,0},{6,2},{8,12},{10,14},{12,8},{14,10},{1,5},{3,7},... | collective-permute-start | bytes 786440 | tf_op jit(solution)/shard_map/ppermute | solution.py:282
  93.9 14.9 %collective-permute-start.20 = (bf16[2,256,256]{2,1,0:T(8,128)(2,1)S(1)}, bf16[2,256,256]{2,1,0:T(8,128)(2,1)S(1)}, u32[]{:S(2)}, u32[]{:S(2)}) collective-permute-start(bf16[2,256,256]{2,1,0:T(8,128)(2,1)S(1)} %get-tuple-element.73.refs_0_), channel_id=1, source_target_pairs={{0,4},{2,6},{4,0},{6,2},{8,12},{10,14},{12,8},{14,10},{1,5},{3,7},... | collective-permute-start | bytes 786440 | tf_op jit(solution)/shard_map/ppermute | solution.py:282
  97.5 21.8 %collective-permute-start.17 = (bf16[2,2,128,512]{3,2,1,0:T(8,128)(2,1)S(1)}, bf16[2,2,128,512]{3,2,1,0:T(8,128)(2,1)S(1)}, u32[]{:S(2)}, u32[]{:S(2)}) collective-permute-start(bf16[2,2,128,512]{3,2,1,0:T(8,128)(2,1)S(1)} %get-tuple-element.74.refs_2_), channel_id=1, source_target_pairs={{0,2},{2,0},{4,6},{6,4},{8,10},{10,8},{12,14},{14,12},{1,3},{3,1},... | collective-permute-start | bytes 1572872 | tf_op jit(solution)/shard_map/ppermute | solution.py:282
  99.0 10.1 %collective-permute-start.22 = (bf16[1,256,256]{2,1,0:T(8,128)(2,1)S(1)}, bf16[1,256,256]{2,1,0:T(8,128)(2,1)S(1)}, u32[]{:S(2)}, u32[]{:S(2)}) collective-permute-start(bf16[1,256,256]{2,1,0:T(8,128)(2,1)S(1)} %get-tuple-element.71.refs_2_), channel_id=1, source_target_pairs={{0,8},{2,10},{4,12},{6,14},{8,0},{10,2},{12,4},{14,6},{1,9},{3,11}... | collective-permute-start | bytes 393224 | tf_op jit(solution)/shard_map/ppermute | solution.py:282
  102.7 13.9 %collective-permute-start.19 = (bf16[1,256,256]{2,1,0:T(8,128)(2,1)S(1)}, bf16[1,256,256]{2,1,0:T(8,128)(2,1)S(1)}, u32[]{:S(2)}, u32[]{:S(2)}) collective-permute-start(bf16[1,256,256]{2,1,0:T(8,128)(2,1)S(1)} %get-tuple-element.77.refs_2_), channel_id=1, source_target_pairs={{0,8},{2,10},{4,12},{6,14},{8,0},{10,2},{12,4},{14,6},{1,9},{3,11}... | collective-permute-start | bytes 393224 | tf_op jit(solution)/shard_map/ppermute | solution.py:282
  108.9 9.7 %collective-permute-start.21 = (bf16[1,256,256]{2,1,0:T(8,128)(2,1)S(1)}, bf16[1,256,256]{2,1,0:T(8,128)(2,1)S(1)}, u32[]{:S(2)}, u32[]{:S(2)}) collective-permute-start(bf16[1,256,256]{2,1,0:T(8,128)(2,1)S(1)} %get-tuple-element.79.refs_4_), channel_id=1, source_target_pairs={{0,8},{2,10},{4,12},{6,14},{8,0},{10,2},{12,4},{14,6},{1,9},{3,11}... | collective-permute-start | bytes 393224 | tf_op jit(solution)/shard_map/ppermute | solution.py:282
  118.7 3.5 %collective-permute-start.24 = (f32[256,256]{1,0:T(8,128)S(1)}, f32[256,256]{1,0:T(8,128)S(1)}, u32[]{:S(2)}, u32[]{:S(2)}) collective-permute-start(f32[256,256]{1,0:T(8,128)S(1)} %get-tuple-element.86.refs_7_), channel_id=1, source_target_pairs={{0,1},{1,0},{2,3},{3,2},{4,5},{5,4},{6,7},{7,6},{8,9},{9,8},{10,11... | collective-permute-start | bytes 786440 | tf_op jit(solution)/shard_map/ppermute | solution.py:286
  118.8 3.4 %collective-permute-start.23 = (f32[256,256]{1,0:T(8,128)S(1)}, f32[256,256]{1,0:T(8,128)S(1)}, u32[]{:S(2)}, u32[]{:S(2)}) collective-permute-start(f32[256,256]{1,0:T(8,128)S(1)} %get-tuple-element.85.refs_9_.refs_5_), channel_id=1, source_target_pairs={{0,1},{1,0},{2,3},{3,2},{4,5},{5,4},{6,7},{7,6},{8,9},{9,8},{10,11... | collective-permute-start | bytes 786440 | tf_op jit(solution)/shard_map/ppermute | solution.py:286
  (13 other events, 97.2 us)

commit v6 on v5

--- a/solution.py
+++ b/solution.py
@@ -24,14 +24,15 @@
 
 
 SEND_AT = (9.0, 21.9)
-KEEP_AT = (32.5, 55.3)
-STEPS_AT = ((21.7, 26.6), (30.0, 39.0), (42.0, 48.5), (52.0, 60.0), (61.0, 77.0), (72.3, 79.4))
+KEEP_AT = (32.5, 50.1)
+STEPS_AT = ((21.7, 26.6), (30.0, 38.7), (42.0, 48.5), (52.0, 60.0), (55.6, 77.0), (72.3, 79.4))
 FINISH_AT = (97.5, 100.0)
 SQUARE_AT = (101.1, 200.0)
-GRADS_AT = 45.9
-JOIN_WAIT = 9.5
+GRADS_AT = 44.0
+JOIN_WAIT = 10.6
 RELAY_WAIT = 20.1
-SIDE_WAIT = 24.0
+NEAR_WAIT = 14.0
+SIDE_WAIT = 29.2
 ACROSS_WAIT = 100.0
 EXPECTED = {("g", 0): 9.5, ("a", 0, 0): 15.4, ("a", 0, 1): 24.5, ("a", 1, 0): 8.5, ("a", 1, 1): 23.2}
 
@@ -206,12 +207,6 @@
 
         shape = jax.ShapeDtypeStruct((2 * count,) + held.shape[1:], held.dtype)
         return self.call(body, [shape], [held, received], [VMEM] * 2)[0]
-
-    def relay(self, x):
-        def body(out_ref):
-            out_ref[...] = jnp.zeros_like(out_ref)
-
-        return self.call(body, [jax.ShapeDtypeStruct((8, LANES), jnp.float32)], [], [], carry=[x])[1]
 
     def moments(self, place, grads, acts, block, out_shape, earlier=None):
         rows, tokens = grads[0].shape[2:]
@@ -301,7 +296,7 @@
     grad_keys = [("g", 0), ("g", 1)]
     act_keys = [("a", block, chunk) for block in range(blocks) for chunk in range(TOKEN_CHUNKS)]
     order = jnp.array(halving_order(n, bits), jnp.int32) ^ me
-    kept, received, finished, gathered = {}, {}, {}, {}
+    kept, received, finished, gathered, advanced = {}, {}, {}, {}, {}
     def keep_or_send(key, x, part):
         if part == 0:
             received[key] = swap(x, n, 0)
@@ -324,6 +319,8 @@
             keep_or_send(("a", block, chunk), x, part)
 
     def advance(key, step):
+        assert step == advanced.get(key, 0)
+        advanced[key] = step + 1
         wider = jnp.float16 if key[0] == "g" else jnp.float32
         dtype = jnp.bfloat16 if step + 1 < ROUNDED_STEPS[key[0]] else wider
         send, kept[key] = chain.combine(received[key], kept[key], dtype)
@@ -334,10 +331,12 @@
 
     def finish_acts(block):
         keys = [("a", block, chunk) for chunk in range(TOKEN_CHUNKS)]
+        assert all(advanced[key] == bits - 1 for key in keys)
         own = chain.finish([received[key] for key in keys], [kept[key] for key in keys])
         finished[block] = [(x, swap_cores(x)) for x in own]
 
     def finish_grads():
+        assert all(advanced[key] == bits - 1 for key in grad_keys)
         mine, other = chain.finish_grads(
             scalars, [received[key] for key in grad_keys], [kept[key] for key in grad_keys]
         )
@@ -346,17 +345,26 @@
     def pair_grads():
         gathered["held"] = chain.pair(gathered["mine"], gathered["other"])
         gathered["order"] = [0]
-        gathered["in"] = swap(gathered["held"], n, bits - 1)
+        send_grads(bits - 1)
+
+    def send_grads(bit):
+        gathered["in"] = swap(gathered["held"], n, bit)
+        if bit == 2:
+            gathered["near"] = chain.expect(swap(gathered["held"], n, 1), NEAR_WAIT)
 
     def join_grads(bit):
-        gathered["held"] = chain.join(gathered["held"], gathered["in"])
+        received = gathered["in"]
+        if bit == 2:
+            gathered["far"] = swap(received, n, 1)
+        gathered["held"] = chain.join(gathered["held"], received)
         gathered["order"] = gathered["order"] + [at ^ (1 << bit) for at in gathered["order"]]
-        gathered["in"] = swap(gathered["held"], n, bit - 1)
         if bit == 2:
             gathered["side"] = chain.expect(swap(gathered["held"], n, 0), SIDE_WAIT)
+        else:
+            send_grads(bit - 1)
 
     def relay_grads():
-        gathered["in"] = chain.relay(gathered["in"])
+        gathered["in"] = chain.join(gathered["near"], gathered["far"])
         gathered["across"] = chain.expect(swap(gathered["in"], n, 0), ACROSS_WAIT)
 
     tasks = [
@@ -389,6 +397,7 @@
         offsets = low + [at ^ 2 for at in low] + [at ^ 1 for at in low] + [at ^ 3 for at in low]
         place = jnp.array(offsets, jnp.int32) ^ me
         grads = [gathered[name] for name in ("held", "in", "side", "across")]
+        assert "across" in gathered
         earlier = result[-1] if result else None
         result.append(chain.moments(place, grads, finished[block], block, out_shape, earlier))
 

time: 126 us -> 121 us (0.960)
  waiting for transfers between devices: 43.4 us -> 34.1 us
  local copies, waits for them, and re-layouts: 5.76 us -> 9.36 us
    ppermute x22 -> x23, waiting for transfers between devices: 42.2 us -> 33.4 us  [swap(): lax.ppermute(x, 'inp', [(index, index ^ 1 << bit) for index in range(n)])]
    unnamed x20, local copies, waits for them, and re-layouts: 5.76 us -> 9.36 us
    ppermute x22 -> x23, starting transfers between devices: 28.6 us -> 29.1 us  [swap(): lax.ppermute(x, 'inp', [(index, index ^ 1 << bit) for index in range(n)])]
  transfers between devices with their start and end apart: 27 -> 28, of which waited for: 11 -> 9; matrix products, arithmetic and copies ran while one was open for 1% -> 1% of each run, Pallas kernels for 30% -> 32%
where the time goes in v6:
time: 121 us; the launch traced here: 120 us
  Pallas kernels  43.8 us (36%)
  waiting for transfers between devices  34.1 us (28%)
  starting transfers between devices  30.4 us (25%)
  local copies, waits for them, and re-layouts  9.36 us (8%)
  other arithmetic  1.47 us (1%)
    pallas_call x8, Pallas kernels, rotate(): pl.pallas_call(kernel, grid_spec=pltpu.PrefetchScalarGridSpec(num_scalar_...  33.6 us
    ppermute x23, waiting for transfers between devices, swap(): lax.ppermute(x, 'inp', [(index, index ^ 1 << bit) for index in range(n)])  33.4 us
    ppermute x23, starting transfers between devices, swap(): lax.ppermute(x, 'inp', [(index, index ^ 1 << bit) for index in range(n)])  29.1 us
    pallas_call x20, Pallas kernels, call(): pl.pallas_call(kernel, out_shape=list(out_shape) + [jax.ShapeDtypeStruct(...  10.2 us
    unnamed x20, local copies, waits for them, and re-layouts  9.36 us
  transfers between devices with their start and end apart: 28, of which 9 were waited for; matrix products, arithmetic and copies ran while one was open for 1% of the time, Pallas kernels for 32%

profile of v6, /device:TPU:0, one launch (start us, length us, event | category | flops | bytes accessed | tf_op | source)
XLA Modules:
  0.0 120.2 jit_solution(14126181220977392175)
XLA Ops:
  0.7 2.2 %copy-done = bf16[1024,2048]{1,0:T(8,128)(2,1)S(1)} copy-done((bf16[1024,2048]{1,0:T(8,128)(2,1)S(1)}, bf16[1024,2048]{1,0:T(8,128)(2,1)}, u32[]{:S(2)}) %copy-start) | copy-done | bytes 4194328
  5.5 3.0 %collective-permute-start = (bf16[4,512,128]{2,1,0:T(8,128)(2,1)S(1)}, bf16[4,512,128]{2,1,0:T(8,128)(2,1)S(1)}, u32[]{:S(2)}, u32[]{:S(2)}) collective-permute-start(bf16[4,512,128]{2,1,0:T(8,128)(2,1)S(1)} %shard_map.82.refs_4_), channel_id=1, source_target_pairs={{0,2},{2,0},{4,6},{6,4},{8,10},{10,8},{12,14},{14,12},{1,3},{3,1},... | collective-permute-start | bytes 1572872 | tf_op jit(solution)/shard_map/ppermute | solution.py:277
  13.5 7.5 %shard_map.86 = (bf16[4,256,256]{2,1,0:T(8,128)(2,1)S(1)}, bf16[4,256,256]{2,1,0:T(8,128)(2,1)}) custom-call(s32[8]{0:T(128)S(1)} %broadcast_xor_fusion.order_ref, bf16[512,3584]{1,0:T(8,128)(2,1)S(1)} %bitcast.3, bf16[3584,4096]{1,0:T(8,128)(2,1)} %refs_1_.15, bf16[3584,4096]{1,0:T(8,128)(2,1)} %refs_1_.15, f32[4,512,128]{2,1,0:T(8,128)S(1)} %shard_map.85.refs_2_.refs_1_), custom_call_target="tpu_custom_call" | custom-call | bytes 131072 | tf_op jit(solution)/shard_map/pallas_call | solution.py:111
  21.4 2.2 %collective-permute-start.1 = (bf16[2,512,128]{2,1,0:T(8,128)(2,1)S(1)}, bf16[2,512,128]{2,1,0:T(8,128)(2,1)S(1)}, u32[]{:S(2)}, u32[]{:S(2)}) collective-permute-start(bf16[2,512,128]{2,1,0:T(8,128)(2,1)S(1)} %get-tuple-element.47.refs_2_), channel_id=1, source_target_pairs={{0,4},{2,6},{4,0},{6,2},{8,12},{10,14},{12,8},{14,10},{1,5},{3,7},... | collective-permute-start | bytes 786440 | tf_op jit(solution)/shard_map/ppermute | solution.py:277
  25.1 6.8 %shard_map.88 = (bf16[4,256,256]{2,1,0:T(8,128)(2,1)S(1)}, bf16[4,256,256]{2,1,0:T(8,128)(2,1)S(1)}) custom-call(s32[8]{0:T(128)S(1)} %broadcast_xor_fusion.order_ref, bf16[512,3584]{1,0:T(8,128)(2,1)S(1)} %bitcast.4, bf16[3584,4096]{1,0:T(8,128)(2,1)} %refs_1_.15, bf16[3584,4096]{1,0:T(8,128)(2,1)} %refs_1_.15, ...), custom_call_target="tpu_custom_call" | custom-call | bytes 131072 | tf_op jit(solution)/shard_map/pallas_call | solution.py:111
  32.9 1.9 %collective-permute-start.4 = (bf16[2,512,128]{2,1,0:T(8,128)(2,1)S(1)}, bf16[2,512,128]{2,1,0:T(8,128)(2,1)S(1)}, u32[]{:S(2)}, u32[]{:S(2)}) collective-permute-start(bf16[2,512,128]{2,1,0:T(8,128)(2,1)S(1)} %get-tuple-element.51.refs_2_), channel_id=1, source_target_pairs={{0,4},{2,6},{4,0},{6,2},{8,12},{10,14},{12,8},{14,10},{1,5},{3,7},... | collective-permute-start | bytes 786440 | tf_op jit(solution)/shard_map/ppermute | solution.py:277
  34.8 2.7 %collective-permute-start.2 = (f16[1,528,128]{2,1,0:T(8,128)(2,1)S(1)}, f16[1,528,128]{2,1,0:T(8,128)(2,1)S(1)}, u32[]{:S(2)}, u32[]{:S(2)}) collective-permute-start(f16[1,528,128]{2,1,0:T(8,128)(2,1)S(1)} %convert_element_type.12), channel_id=1, source_target_pairs={{0,8},{2,10},{4,12},{6,14},{8,0},{10,2},{12,4},{14,6},{1,9},{3,11}... | collective-permute-start | bytes 405512 | tf_op jit(solution)/shard_map/ppermute | solution.py:277
  37.5 1.5 %collective-permute-start.11 = (bf16[4,256,256]{2,1,0:T(8,128)(2,1)}, bf16[4,256,256]{2,1,0:T(8,128)(2,1)S(1)}, u32[]{:S(2)}, u32[]{:S(2)}) collective-permute-start(bf16[4,256,256]{2,1,0:T(8,128)(2,1)} %get-tuple-element.63), channel_id=1, source_target_pairs={{0,2},{2,0},{4,6},{6,4},{8,10},{10,8},{12,14},{14,12},{1,3},{3,1},... | collective-permute-start | bytes 1572872 | tf_op jit(solution)/shard_map/ppermute | solution.py:277
  39.0 6.8 %shard_map.91 = (f32[4,256,256]{2,1,0:T(8,128)S(1)}, f32[4,256,256]{2,1,0:T(8,128)S(1)}) custom-call(s32[8]{0:T(128)S(1)} %broadcast_xor_fusion.order_ref, bf16[512,3584]{1,0:T(8,128)(2,1)S(1)} %bitcast.5, bf16[3584,4096]{1,0:T(8,128)(2,1)} %refs_1_.15, bf16[3584,4096]{1,0:T(8,128)(2,1)} %refs_1_.15, bf16[2,512,128]{2,1,0:T(8,128)(2,1)S(1)} %get-tuple-element.51.refs_2_), custom_call_target="tpu_custom_call" | custom-call | bytes 131072 | tf_op jit(solution)/shard_map/pallas_call | solution.py:111
  50.9 4.1 %collective-permute-done.5 = f16[1,528,128]{2,1,0:T(8,128)(2,1)S(1)} collective-permute-done((f16[1,528,128]{2,1,0:T(8,128)(2,1)}, f16[1,528,128]{2,1,0:T(8,128)(2,1)S(1)}, u32[]{:S(2)}, u32[]{:S(2)}) %collective-permute-start.5) | collective-permute-done | bytes 135200 | tf_op jit(solution)/shard_map/ppermute | solution.py:277
  60.8 2.0 %copy-done.2 = bf16[1,512,3584]{2,1,0:T(8,128)(2,1)S(1)} copy-done((bf16[1,512,3584]{2,1,0:T(8,128)(2,1)S(1)}, bf16[1,512,3584]{2,1,0:T(8,128)(2,1)}, u32[]{:S(2)}) %copy-start.2) | copy-done | bytes 3670040
  62.8 6.8 %shard_map.97 = (f32[4,256,256]{2,1,0:T(8,128)S(1)}, f32[4,256,256]{2,1,0:T(8,128)S(1)}) custom-call(s32[8]{0:T(128)S(1)} %broadcast_xor_fusion.order_ref, bf16[512,3584]{1,0:T(8,128)(2,1)S(1)} %bitcast.6, bf16[3584,4096]{1,0:T(8,128)(2,1)} %refs_1_.15, bf16[3584,4096]{1,0:T(8,128)(2,1)} %refs_1_.15, bf16[1,256,256]{2,1,0:T(8,128)(2,1)S(1)} %get-tuple-element.61.refs_2_), custom_call_target="tpu_custom_call" | custom-call | bytes 131072 | tf_op jit(solution)/shard_map/pallas_call | solution.py:111
  69.7 2.0 %collective-permute-start.15 = (bf16[2,256,256]{2,1,0:T(8,128)(2,1)S(1)}, bf16[2,256,256]{2,1,0:T(8,128)(2,1)S(1)}, u32[]{:S(2)}, u32[]{:S(2)}) collective-permute-start(bf16[2,256,256]{2,1,0:T(8,128)(2,1)S(1)} %get-tuple-element.65.refs_2_), channel_id=1, source_target_pairs={{0,4},{2,6},{4,0},{6,2},{8,12},{10,14},{12,8},{14,10},{1,5},{3,7},... | collective-permute-start | bytes 786440 | tf_op jit(solution)/shard_map/ppermute | solution.py:277
  71.7 2.6 %collective-permute-start.16 = (bf16[1,256,256]{2,1,0:T(8,128)(2,1)S(1)}, bf16[1,256,256]{2,1,0:T(8,128)(2,1)S(1)}, u32[]{:S(2)}, u32[]{:S(2)}) collective-permute-start(bf16[1,256,256]{2,1,0:T(8,128)(2,1)S(1)} %get-tuple-element.61.refs_2_), channel_id=1, source_target_pairs={{0,8},{2,10},{4,12},{6,14},{8,0},{10,2},{12,4},{14,6},{1,9},{3,11}... | collective-permute-start | bytes 393224 | tf_op jit(solution)/shard_map/ppermute | solution.py:277
  75.6 6.8 %collective-permute-done.15.refs_0_ = bf16[2,256,256]{2,1,0:T(8,128)(2,1)S(1)} collective-permute-done((bf16[2,256,256]{2,1,0:T(8,128)(2,1)S(1)}, bf16[2,256,256]{2,1,0:T(8,128)(2,1)S(1)}, u32[]{:S(2)}, u32[]{:S(2)}) %collective-permute-start.15) | collective-permute-done | bytes 262176 | tf_op jit(solution)/shard_map/ppermute | solution.py:277
  82.6 2.1 %collective-permute-start.21 = (bf16[2,256,256]{2,1,0:T(8,128)(2,1)S(1)}, bf16[2,256,256]{2,1,0:T(8,128)(2,1)S(1)}, u32[]{:S(2)}, u32[]{:S(2)}) collective-permute-start(bf16[2,256,256]{2,1,0:T(8,128)(2,1)S(1)} %get-tuple-element.71.refs_2_), channel_id=1, source_target_pairs={{0,4},{2,6},{4,0},{6,2},{8,12},{10,14},{12,8},{14,10},{1,5},{3,7},... | collective-permute-start | bytes 786440 | tf_op jit(solution)/shard_map/ppermute | solution.py:277
  84.8 3.3 %collective-permute-done.13.refs_1_ = bf16[1,2,128,512]{3,2,1,0:T(8,128)(2,1)S(1)} collective-permute-done((bf16[1,2,128,512]{3,2,1,0:T(8,128)(2,1)S(1)}, bf16[1,2,128,512]{3,2,1,0:T(8,128)(2,1)S(1)}, u32[]{:S(2)}, u32[]{:S(2)}) %collective-permute-start.13) | collective-permute-done | bytes 262176 | tf_op jit(solution)/shard_map/ppermute | solution.py:277
  88.9 2.1 %collective-permute-start.23 = (bf16[1,256,256]{2,1,0:T(8,128)(2,1)S(1)}, bf16[1,256,256]{2,1,0:T(8,128)(2,1)S(1)}, u32[]{:S(2)}, u32[]{:S(2)}) collective-permute-start(bf16[1,256,256]{2,1,0:T(8,128)(2,1)S(1)} %get-tuple-element.70.refs_2_), channel_id=1, source_target_pairs={{0,8},{2,10},{4,12},{6,14},{8,0},{10,2},{12,4},{14,6},{1,9},{3,11}... | collective-permute-start | bytes 393224 | tf_op jit(solution)/shard_map/ppermute | solution.py:277
  91.1 5.4 %collective-permute-done.19.refs_0_ = bf16[2,256,256]{2,1,0:T(8,128)(2,1)S(1)} collective-permute-done((bf16[2,256,256]{2,1,0:T(8,128)(2,1)S(1)}, bf16[2,256,256]{2,1,0:T(8,128)(2,1)S(1)}, u32[]{:S(2)}, u32[]{:S(2)}) %collective-permute-start.19) | collective-permute-done | bytes 262176 | tf_op jit(solution)/shard_map/ppermute | solution.py:277
  97.8 4.8 %collective-permute-done.21.refs_0_ = bf16[2,256,256]{2,1,0:T(8,128)(2,1)S(1)} collective-permute-done((bf16[2,256,256]{2,1,0:T(8,128)(2,1)S(1)}, bf16[2,256,256]{2,1,0:T(8,128)(2,1)S(1)}, u32[]{:S(2)}, u32[]{:S(2)}) %collective-permute-start.21) | collective-permute-done | bytes 262176 | tf_op jit(solution)/shard_map/ppermute | solution.py:277
  103.8 7.1 %collective-permute-done.20.refs_7_.refs_0_ = bf16[1,256,256]{2,1,0:T(8,128)(2,1)S(1)} collective-permute-done((bf16[1,256,256]{2,1,0:T(8,128)(2,1)S(1)}, bf16[1,256,256]{2,1,0:T(8,128)(2,1)S(1)}, u32[]{:S(2)}, u32[]{:S(2)}) %collective-permute-start.20) | collective-permute-done | bytes 131104 | tf_op jit(solution)/shard_map/ppermute | solution.py:277
  111.5 1.6 %collective-permute-done.22.refs_1_.refs_12_ = bf16[1,256,256]{2,1,0:T(8,128)(2,1)S(1)} collective-permute-done((bf16[1,256,256]{2,1,0:T(8,128)(2,1)S(1)}, bf16[1,256,256]{2,1,0:T(8,128)(2,1)S(1)}, u32[]{:S(2)}, u32[]{:S(2)}) %collective-permute-start.22) | collective-permute-done | bytes 131104 | tf_op jit(solution)/shard_map/ppermute | solution.py:277
  113.8 2.8 %shard_map.108 = (f32[8,128]{1,0:T(8,128)S(1)}, f32[1024,512]{1,0:T(8,128)}) custom-call(s32[8]{0:T(128)S(1)} %broadcast_xor_fusion.1.refs_0_, bf16[2,2,128,512]{3,2,1,0:T(8,128)(2,1)S(1)} %shard_map.100.refs_2_.refs_1_, bf16[2,2,128,512]{3,2,1,0:T(8,128)(2,1)S(1)} %shard_map.103.refs_2_, ...), custom_call_target="tpu_custom_call" | custom-call | bytes 131072 | tf_op jit(solution)/shard_map/pallas_call | solution.py:75
  116.7 3.4 %shard_map.109 = (f32[8,128]{1,0:T(8,128)}, f32[1024,512]{1,0:T(8,128)}) custom-call(s32[8]{0:T(128)S(1)} %broadcast_xor_fusion.1.refs_0_, bf16[2,2,128,512]{3,2,1,0:T(8,128)(2,1)S(1)} %shard_map.100.refs_2_.refs_1_, bf16[2,2,128,512]{3,2,1,0:T(8,128)(2,1)S(1)} %shard_map.103.refs_2_, ...), custom_call_target="tpu_custom_call", output_to_operand_aliasing={{1}: (9, {})} | custom-call | bytes 131072 | tf_op jit(solution)/shard_map/pallas_call | solution.py:75
  (87 shorter events, 27.5 us)
Async XLA Ops:
  5.5 15.8 %collective-permute-start = (bf16[4,512,128]{2,1,0:T(8,128)(2,1)S(1)}, bf16[4,512,128]{2,1,0:T(8,128)(2,1)S(1)}, u32[]{:S(2)}, u32[]{:S(2)}) collective-permute-start(bf16[4,512,128]{2,1,0:T(8,128)(2,1)S(1)} %shard_map.82.refs_4_), channel_id=1, source_target_pairs={{0,2},{2,0},{4,6},{6,4},{8,10},{10,8},{12,14},{14,12},{1,3},{3,1},... | collective-permute-start | bytes 1572872 | tf_op jit(solution)/shard_map/ppermute | solution.py:277
  10.0 22.9 %collective-permute-start.3 = (bf16[4,512,128]{2,1,0:T(8,128)(2,1)S(1)}, bf16[4,512,128]{2,1,0:T(8,128)(2,1)S(1)}, u32[]{:S(2)}, u32[]{:S(2)}) collective-permute-start(bf16[4,512,128]{2,1,0:T(8,128)(2,1)S(1)} %shard_map.83.refs_4_), channel_id=1, source_target_pairs={{0,2},{2,0},{4,6},{6,4},{8,10},{10,8},{12,14},{14,12},{1,3},{3,1},... | collective-permute-start | bytes 1572872 | tf_op jit(solution)/shard_map/ppermute | solution.py:277
  21.4 10.5 %collective-permute-start.1 = (bf16[2,512,128]{2,1,0:T(8,128)(2,1)S(1)}, bf16[2,512,128]{2,1,0:T(8,128)(2,1)S(1)}, u32[]{:S(2)}, u32[]{:S(2)}) collective-permute-start(bf16[2,512,128]{2,1,0:T(8,128)(2,1)S(1)} %get-tuple-element.47.refs_2_), channel_id=1, source_target_pairs={{0,4},{2,6},{4,0},{6,2},{8,12},{10,14},{12,8},{14,10},{1,5},{3,7},... | collective-permute-start | bytes 786440 | tf_op jit(solution)/shard_map/ppermute | solution.py:277
  23.6 24.7 %collective-permute-start.6 = (bf16[4,256,256]{2,1,0:T(8,128)(2,1)S(1)}, bf16[4,256,256]{2,1,0:T(8,128)(2,1)S(1)}, u32[]{:S(2)}, u32[]{:S(2)}) collective-permute-start(bf16[4,256,256]{2,1,0:T(8,128)(2,1)S(1)} %get-tuple-element.46.refs_2_), channel_id=1, source_target_pairs={{0,2},{2,0},{4,6},{6,4},{8,10},{10,8},{12,14},{14,12},{1,3},{3,1},... | collective-permute-start | bytes 1572872 | tf_op jit(solution)/shard_map/ppermute | solution.py:277
  32.9 12.9 %collective-permute-start.4 = (bf16[2,512,128]{2,1,0:T(8,128)(2,1)S(1)}, bf16[2,512,128]{2,1,0:T(8,128)(2,1)S(1)}, u32[]{:S(2)}, u32[]{:S(2)}) collective-permute-start(bf16[2,512,128]{2,1,0:T(8,128)(2,1)S(1)} %get-tuple-element.51.refs_2_), channel_id=1, source_target_pairs={{0,4},{2,6},{4,0},{6,2},{8,12},{10,14},{12,8},{14,10},{1,5},{3,7},... | collective-permute-start | bytes 786440 | tf_op jit(solution)/shard_map/ppermute | solution.py:277
  34.8 11.0 %collective-permute-start.2 = (f16[1,528,128]{2,1,0:T(8,128)(2,1)S(1)}, f16[1,528,128]{2,1,0:T(8,128)(2,1)S(1)}, u32[]{:S(2)}, u32[]{:S(2)}) collective-permute-start(f16[1,528,128]{2,1,0:T(8,128)(2,1)S(1)} %convert_element_type.12), channel_id=1, source_target_pairs={{0,8},{2,10},{4,12},{6,14},{8,0},{10,2},{12,4},{14,6},{1,9},{3,11}... | collective-permute-start | bytes 405512 | tf_op jit(solution)/shard_map/ppermute | solution.py:277
  37.5 32.2 %collective-permute-start.11 = (bf16[4,256,256]{2,1,0:T(8,128)(2,1)}, bf16[4,256,256]{2,1,0:T(8,128)(2,1)S(1)}, u32[]{:S(2)}, u32[]{:S(2)}) collective-permute-start(bf16[4,256,256]{2,1,0:T(8,128)(2,1)} %get-tuple-element.63), channel_id=1, source_target_pairs={{0,2},{2,0},{4,6},{6,4},{8,10},{10,8},{12,14},{14,12},{1,3},{3,1},... | collective-permute-start | bytes 1572872 | tf_op jit(solution)/shard_map/ppermute | solution.py:277
  47.4 7.6 %collective-permute-start.5 = (f16[1,528,128]{2,1,0:T(8,128)(2,1)}, f16[1,528,128]{2,1,0:T(8,128)(2,1)S(1)}, u32[]{:S(2)}, u32[]{:S(2)}) collective-permute-start(f16[1,528,128]{2,1,0:T(8,128)(2,1)} %convert_element_type.14), channel_id=1, source_target_pairs={{0,8},{2,10},{4,12},{6,14},{8,0},{10,2},{12,4},{14,6},{1,9},{3,11}... | collective-permute-start | bytes 405512 | tf_op jit(solution)/shard_map/ppermute | solution.py:277
  47.8 24.0 %collective-permute-start.9 = (bf16[4,256,256]{2,1,0:T(8,128)(2,1)S(1)}, bf16[4,256,256]{2,1,0:T(8,128)(2,1)S(1)}, u32[]{:S(2)}, u32[]{:S(2)}) collective-permute-start(bf16[4,256,256]{2,1,0:T(8,128)(2,1)S(1)} %get-tuple-element.49.refs_2_), channel_id=1, source_target_pairs={{0,2},{2,0},{4,6},{6,4},{8,10},{10,8},{12,14},{14,12},{1,3},{3,1},... | collective-permute-start | bytes 1572872 | tf_op jit(solution)/shard_map/ppermute | solution.py:277
  49.1 10.6 %collective-permute-start.10 = (bf16[2,256,256]{2,1,0:T(8,128)(2,1)}, bf16[2,256,256]{2,1,0:T(8,128)(2,1)}, u32[]{:S(2)}, u32[]{:S(2)}) collective-permute-start(bf16[2,256,256]{2,1,0:T(8,128)(2,1)} %get-tuple-element.57.refs_5_), channel_id=1, source_target_pairs={{0,4},{2,6},{4,0},{6,2},{8,12},{10,14},{12,8},{14,10},{1,5},{3,7},... | collective-permute-start | bytes 786440 | tf_op jit(solution)/shard_map/ppermute | solution.py:277
  58.0 24.5 %collective-permute-start.14 = (bf16[4,256,256]{2,1,0:T(8,128)(2,1)}, bf16[4,256,256]{2,1,0:T(8,128)(2,1)S(1)}, u32[]{:S(2)}, u32[]{:S(2)}) collective-permute-start(bf16[4,256,256]{2,1,0:T(8,128)(2,1)} %copy-done.8), channel_id=1, source_target_pairs={{0,2},{2,0},{4,6},{6,4},{8,10},{10,8},{12,14},{14,12},{1,3},{3,1},... | collective-permute-start | bytes 1572872 | tf_op jit(solution)/shard_map/ppermute | solution.py:277
  59.3 15.2 %collective-permute-start.8 = (bf16[1,2,128,512]{3,2,1,0:T(8,128)(2,1)S(1)}, bf16[1,2,128,512]{3,2,1,0:T(8,128)(2,1)S(1)}, u32[]{:S(2)}, u32[]{:S(2)}) collective-permute-start(bf16[1,2,128,512]{3,2,1,0:T(8,128)(2,1)S(1)} %shard_map.95.refs_2_.refs_0_), channel_id=1, source_target_pairs={{0,8},{2,10},{4,12},{6,14},{8,0},{10,2},{12,4},{14,6},{1,9},{3,11}... | collective-permute-start | bytes 786440 | tf_op jit(solution)/shard_map/ppermute | solution.py:277
  59.7 15.7 %collective-permute-start.12 = (bf16[1,2,128,512]{3,2,1,0:T(8,128)(2,1)S(1)}, bf16[1,2,128,512]{3,2,1,0:T(8,128)(2,1)S(1)}, u32[]{:S(2)}, u32[]{:S(2)}) collective-permute-start(bf16[1,2,128,512]{3,2,1,0:T(8,128)(2,1)S(1)} %shard_map.95.refs_2_.refs_0_), channel_id=1, source_target_pairs={{0,4},{2,6},{4,0},{6,2},{8,12},{10,14},{12,8},{14,10},{1,5},{3,7},... | collective-permute-start | bytes 786440 | tf_op jit(solution)/shard_map/ppermute | solution.py:277
  69.7 12.7 %collective-permute-start.15 = (bf16[2,256,256]{2,1,0:T(8,128)(2,1)S(1)}, bf16[2,256,256]{2,1,0:T(8,128)(2,1)S(1)}, u32[]{:S(2)}, u32[]{:S(2)}) collective-permute-start(bf16[2,256,256]{2,1,0:T(8,128)(2,1)S(1)} %get-tuple-element.65.refs_2_), channel_id=1, source_target_pairs={{0,4},{2,6},{4,0},{6,2},{8,12},{10,14},{12,8},{14,10},{1,5},{3,7},... | collective-permute-start | bytes 786440 | tf_op jit(solution)/shard_map/ppermute | solution.py:277
  71.7 10.8 %collective-permute-start.16 = (bf16[1,256,256]{2,1,0:T(8,128)(2,1)S(1)}, bf16[1,256,256]{2,1,0:T(8,128)(2,1)S(1)}, u32[]{:S(2)}, u32[]{:S(2)}) collective-permute-start(bf16[1,256,256]{2,1,0:T(8,128)(2,1)S(1)} %get-tuple-element.61.refs_2_), channel_id=1, source_target_pairs={{0,8},{2,10},{4,12},{6,14},{8,0},{10,2},{12,4},{14,6},{1,9},{3,11}... | collective-permute-start | bytes 393224 | tf_op jit(solution)/shard_map/ppermute | solution.py:277
  74.6 36.3 %collective-permute-start.17 = (bf16[2,2,128,512]{3,2,1,0:T(8,128)(2,1)S(1)}, bf16[2,2,128,512]{3,2,1,0:T(8,128)(2,1)S(1)}, u32[]{:S(2)}, u32[]{:S(2)}) collective-permute-start(bf16[2,2,128,512]{3,2,1,0:T(8,128)(2,1)S(1)} %shard_map.100.refs_2_.refs_1_), channel_id=1, source_target_pairs={{0,2},{2,0},{4,6},{6,4},{8,10},{10,8},{12,14},{14,12},{1,3},{3,1},... | collective-permute-start | bytes 1572872 | tf_op jit(solution)/shard_map/ppermute | solution.py:277
  75.4 12.7 %collective-permute-start.13 = (bf16[1,2,128,512]{3,2,1,0:T(8,128)(2,1)S(1)}, bf16[1,2,128,512]{3,2,1,0:T(8,128)(2,1)S(1)}, u32[]{:S(2)}, u32[]{:S(2)}) collective-permute-start(bf16[1,2,128,512]{3,2,1,0:T(8,128)(2,1)S(1)} %collective-permute-done.8.refs_1_), channel_id=1, source_target_pairs={{0,4},{2,6},{4,0},{6,2},{8,12},{10,14},{12,8},{14,10},{1,5},{3,7},... | collective-permute-start | bytes 786440 | tf_op jit(solution)/shard_map/ppermute | solution.py:277
  82.4 14.0 %collective-permute-start.19 = (bf16[2,256,256]{2,1,0:T(8,128)(2,1)S(1)}, bf16[2,256,256]{2,1,0:T(8,128)(2,1)S(1)}, u32[]{:S(2)}, u32[]{:S(2)}) collective-permute-start(bf16[2,256,256]{2,1,0:T(8,128)(2,1)S(1)} %get-tuple-element.66.refs_2_), channel_id=1, source_target_pairs={{0,4},{2,6},{4,0},{6,2},{8,12},{10,14},{12,8},{14,10},{1,5},{3,7},... | collective-permute-start | bytes 786440 | tf_op jit(solution)/shard_map/ppermute | solution.py:277
  82.6 19.9 %collective-permute-start.21 = (bf16[2,256,256]{2,1,0:T(8,128)(2,1)S(1)}, bf16[2,256,256]{2,1,0:T(8,128)(2,1)S(1)}, u32[]{:S(2)}, u32[]{:S(2)}) collective-permute-start(bf16[2,256,256]{2,1,0:T(8,128)(2,1)S(1)} %get-tuple-element.71.refs_2_), channel_id=1, source_target_pairs={{0,4},{2,6},{4,0},{6,2},{8,12},{10,14},{12,8},{14,10},{1,5},{3,7},... | collective-permute-start | bytes 786440 | tf_op jit(solution)/shard_map/ppermute | solution.py:277
  88.1 25.7 %collective-permute-start.18 = (bf16[2,2,128,512]{3,2,1,0:T(8,128)(2,1)S(1)}, bf16[2,2,128,512]{3,2,1,0:T(8,128)(2,1)S(1)}, u32[]{:S(2)}, u32[]{:S(2)}) collective-permute-start(bf16[2,2,128,512]{3,2,1,0:T(8,128)(2,1)S(1)} %shard_map.103.refs_2_), channel_id=1, source_target_pairs={{0,2},{2,0},{4,6},{6,4},{8,10},{10,8},{12,14},{14,12},{1,3},{3,1},... | collective-permute-start | bytes 1572872 | tf_op jit(solution)/shard_map/ppermute | solution.py:277
  88.9 14.9 %collective-permute-start.23 = (bf16[1,256,256]{2,1,0:T(8,128)(2,1)S(1)}, bf16[1,256,256]{2,1,0:T(8,128)(2,1)S(1)}, u32[]{:S(2)}, u32[]{:S(2)}) collective-permute-start(bf16[1,256,256]{2,1,0:T(8,128)(2,1)S(1)} %get-tuple-element.70.refs_2_), channel_id=1, source_target_pairs={{0,8},{2,10},{4,12},{6,14},{8,0},{10,2},{12,4},{14,6},{1,9},{3,11}... | collective-permute-start | bytes 393224 | tf_op jit(solution)/shard_map/ppermute | solution.py:277
  96.5 14.3 %collective-permute-start.20 = (bf16[1,256,256]{2,1,0:T(8,128)(2,1)S(1)}, bf16[1,256,256]{2,1,0:T(8,128)(2,1)S(1)}, u32[]{:S(2)}, u32[]{:S(2)}) collective-permute-start(bf16[1,256,256]{2,1,0:T(8,128)(2,1)S(1)} %get-tuple-element.73.refs_2_), channel_id=1, source_target_pairs={{0,8},{2,10},{4,12},{6,14},{8,0},{10,2},{12,4},{14,6},{1,9},{3,11}... | collective-permute-start | bytes 393224 | tf_op jit(solution)/shard_map/ppermute | solution.py:277
  102.6 10.5 %collective-permute-start.22 = (bf16[1,256,256]{2,1,0:T(8,128)(2,1)S(1)}, bf16[1,256,256]{2,1,0:T(8,128)(2,1)S(1)}, u32[]{:S(2)}, u32[]{:S(2)}) collective-permute-start(bf16[1,256,256]{2,1,0:T(8,128)(2,1)S(1)} %get-tuple-element.75.refs_4_), channel_id=1, source_target_pairs={{0,8},{2,10},{4,12},{6,14},{8,0},{10,2},{12,4},{14,6},{1,9},{3,11}... | collective-permute-start | bytes 393224 | tf_op jit(solution)/shard_map/ppermute | solution.py:277
  113.2 3.5 %collective-permute-start.25 = (f32[256,256]{1,0:T(8,128)S(1)}, f32[256,256]{1,0:T(8,128)S(1)}, u32[]{:S(2)}, u32[]{:S(2)}) collective-permute-start(f32[256,256]{1,0:T(8,128)S(1)} %get-tuple-element.82.refs_7_), channel_id=1, source_target_pairs={{0,1},{1,0},{2,3},{3,2},{4,5},{5,4},{6,7},{7,6},{8,9},{9,8},{10,11... | collective-permute-start | bytes 786440 | tf_op jit(solution)/shard_map/ppermute | solution.py:281
  (14 other events, 66.4 us)

commit v7 on v6

--- a/solution.py
+++ b/solution.py
@@ -25,14 +25,14 @@
 
 SEND_AT = (9.0, 21.9)
 KEEP_AT = (32.5, 50.1)
-STEPS_AT = ((21.7, 26.6), (30.0, 38.7), (42.0, 48.5), (52.0, 60.0), (55.6, 77.0), (72.3, 79.4))
+STEPS_AT = ((21.7, 26.6), (30.0, 38.7), (42.0, 48.5), (52.0, 60.0), (55.4, 77.0), (72.3, 79.4))
 FINISH_AT = (97.5, 100.0)
 SQUARE_AT = (101.1, 200.0)
 GRADS_AT = 44.0
 JOIN_WAIT = 10.6
 RELAY_WAIT = 20.1
 NEAR_WAIT = 14.0
-SIDE_WAIT = 29.2
+SIDE_WAIT = 100.0
 ACROSS_WAIT = 100.0
 EXPECTED = {("g", 0): 9.5, ("a", 0, 0): 15.4, ("a", 0, 1): 24.5, ("a", 1, 0): 8.5, ("a", 1, 1): 23.2}
 

time: 121 us -> 121 us (level)
  no operation moved by 1% of the time
where the time goes in v7:
time: 121 us; the launch traced here: 120 us
  Pallas kernels  43.8 us (36%)
  waiting for transfers between devices  33.9 us (28%)
  starting transfers between devices  30.6 us (25%)
  local copies, waits for them, and re-layouts  9.36 us (8%)
  other arithmetic  1.47 us (1%)
    pallas_call x8, Pallas kernels, rotate(): pl.pallas_call(kernel, grid_spec=pltpu.PrefetchScalarGridSpec(num_scalar_...  33.6 us
    ppermute x23, waiting for transfers between devices, swap(): lax.ppermute(x, 'inp', [(index, index ^ 1 << bit) for index in range(n)])  32.6 us
    ppermute x23, starting transfers between devices, swap(): lax.ppermute(x, 'inp', [(index, index ^ 1 << bit) for index in range(n)])  29.4 us
    pallas_call x20, Pallas kernels, call(): pl.pallas_call(kernel, out_shape=list(out_shape) + [jax.ShapeDtypeStruct(...  10.2 us
    unnamed x20, local copies, waits for them, and re-layouts  9.36 us
  transfers between devices with their start and end apart: 28, of which 9 were waited for; matrix products, arithmetic and copies ran while one was open for 1% of the time, Pallas kernels for 32%

profile of v7, /device:TPU:0, one launch (start us, length us, event | category | flops | bytes accessed | tf_op | source)
XLA Modules:
  0.0 120.2 jit_solution(13225238206856054209)
XLA Ops:
  0.7 2.2 %copy-done = bf16[1024,2048]{1,0:T(8,128)(2,1)S(1)} copy-done((bf16[1024,2048]{1,0:T(8,128)(2,1)S(1)}, bf16[1024,2048]{1,0:T(8,128)(2,1)}, u32[]{:S(2)}) %copy-start) | copy-done | bytes 4194328
  5.5 3.0 %collective-permute-start = (bf16[4,512,128]{2,1,0:T(8,128)(2,1)S(1)}, bf16[4,512,128]{2,1,0:T(8,128)(2,1)S(1)}, u32[]{:S(2)}, u32[]{:S(2)}) collective-permute-start(bf16[4,512,128]{2,1,0:T(8,128)(2,1)S(1)} %shard_map.82.refs_4_), channel_id=1, source_target_pairs={{0,2},{2,0},{4,6},{6,4},{8,10},{10,8},{12,14},{14,12},{1,3},{3,1},... | collective-permute-start | bytes 1572872 | tf_op jit(solution)/shard_map/ppermute | solution.py:277
  13.5 7.5 %shard_map.86 = (bf16[4,256,256]{2,1,0:T(8,128)(2,1)S(1)}, bf16[4,256,256]{2,1,0:T(8,128)(2,1)}) custom-call(s32[8]{0:T(128)S(1)} %broadcast_xor_fusion.order_ref, bf16[512,3584]{1,0:T(8,128)(2,1)S(1)} %bitcast.3, bf16[3584,4096]{1,0:T(8,128)(2,1)} %refs_1_.15, bf16[3584,4096]{1,0:T(8,128)(2,1)} %refs_1_.15, f32[4,512,128]{2,1,0:T(8,128)S(1)} %shard_map.85.refs_2_.refs_1_), custom_call_target="tpu_custom_call" | custom-call | bytes 131072 | tf_op jit(solution)/shard_map/pallas_call | solution.py:111
  21.4 2.2 %collective-permute-start.1 = (bf16[2,512,128]{2,1,0:T(8,128)(2,1)S(1)}, bf16[2,512,128]{2,1,0:T(8,128)(2,1)S(1)}, u32[]{:S(2)}, u32[]{:S(2)}) collective-permute-start(bf16[2,512,128]{2,1,0:T(8,128)(2,1)S(1)} %get-tuple-element.47.refs_2_), channel_id=1, source_target_pairs={{0,4},{2,6},{4,0},{6,2},{8,12},{10,14},{12,8},{14,10},{1,5},{3,7},... | collective-permute-start | bytes 786440 | tf_op jit(solution)/shard_map/ppermute | solution.py:277
  23.6 1.5 %collective-permute-start.6 = (bf16[4,256,256]{2,1,0:T(8,128)(2,1)S(1)}, bf16[4,256,256]{2,1,0:T(8,128)(2,1)S(1)}, u32[]{:S(2)}, u32[]{:S(2)}) collective-permute-start(bf16[4,256,256]{2,1,0:T(8,128)(2,1)S(1)} %get-tuple-element.46.refs_2_), channel_id=1, source_target_pairs={{0,2},{2,0},{4,6},{6,4},{8,10},{10,8},{12,14},{14,12},{1,3},{3,1},... | collective-permute-start | bytes 1572872 | tf_op jit(solution)/shard_map/ppermute | solution.py:277
  25.1 6.8 %shard_map.88 = (bf16[4,256,256]{2,1,0:T(8,128)(2,1)S(1)}, bf16[4,256,256]{2,1,0:T(8,128)(2,1)S(1)}) custom-call(s32[8]{0:T(128)S(1)} %broadcast_xor_fusion.order_ref, bf16[512,3584]{1,0:T(8,128)(2,1)S(1)} %bitcast.4, bf16[3584,4096]{1,0:T(8,128)(2,1)} %refs_1_.15, bf16[3584,4096]{1,0:T(8,128)(2,1)} %refs_1_.15, ...), custom_call_target="tpu_custom_call" | custom-call | bytes 131072 | tf_op jit(solution)/shard_map/pallas_call | solution.py:111
  32.9 1.9 %collective-permute-start.4 = (bf16[2,512,128]{2,1,0:T(8,128)(2,1)S(1)}, bf16[2,512,128]{2,1,0:T(8,128)(2,1)S(1)}, u32[]{:S(2)}, u32[]{:S(2)}) collective-permute-start(bf16[2,512,128]{2,1,0:T(8,128)(2,1)S(1)} %get-tuple-element.51.refs_2_), channel_id=1, source_target_pairs={{0,4},{2,6},{4,0},{6,2},{8,12},{10,14},{12,8},{14,10},{1,5},{3,7},... | collective-permute-start | bytes 786440 | tf_op jit(solution)/shard_map/ppermute | solution.py:277
  34.8 2.7 %collective-permute-start.2 = (f16[1,528,128]{2,1,0:T(8,128)(2,1)S(1)}, f16[1,528,128]{2,1,0:T(8,128)(2,1)S(1)}, u32[]{:S(2)}, u32[]{:S(2)}) collective-permute-start(f16[1,528,128]{2,1,0:T(8,128)(2,1)S(1)} %convert_element_type.12), channel_id=1, source_target_pairs={{0,8},{2,10},{4,12},{6,14},{8,0},{10,2},{12,4},{14,6},{1,9},{3,11}... | collective-permute-start | bytes 405512 | tf_op jit(solution)/shard_map/ppermute | solution.py:277
  37.5 1.5 %collective-permute-start.11 = (bf16[4,256,256]{2,1,0:T(8,128)(2,1)}, bf16[4,256,256]{2,1,0:T(8,128)(2,1)S(1)}, u32[]{:S(2)}, u32[]{:S(2)}) collective-permute-start(bf16[4,256,256]{2,1,0:T(8,128)(2,1)} %get-tuple-element.63), channel_id=1, source_target_pairs={{0,2},{2,0},{4,6},{6,4},{8,10},{10,8},{12,14},{14,12},{1,3},{3,1},... | collective-permute-start | bytes 1572872 | tf_op jit(solution)/shard_map/ppermute | solution.py:277
  39.0 6.8 %shard_map.91 = (f32[4,256,256]{2,1,0:T(8,128)S(1)}, f32[4,256,256]{2,1,0:T(8,128)S(1)}) custom-call(s32[8]{0:T(128)S(1)} %broadcast_xor_fusion.order_ref, bf16[512,3584]{1,0:T(8,128)(2,1)S(1)} %bitcast.5, bf16[3584,4096]{1,0:T(8,128)(2,1)} %refs_1_.15, bf16[3584,4096]{1,0:T(8,128)(2,1)} %refs_1_.15, bf16[2,512,128]{2,1,0:T(8,128)(2,1)S(1)} %get-tuple-element.51.refs_2_), custom_call_target="tpu_custom_call" | custom-call | bytes 131072 | tf_op jit(solution)/shard_map/pallas_call | solution.py:111
  51.8 3.2 %collective-permute-done.5 = f16[1,528,128]{2,1,0:T(8,128)(2,1)S(1)} collective-permute-done((f16[1,528,128]{2,1,0:T(8,128)(2,1)}, f16[1,528,128]{2,1,0:T(8,128)(2,1)S(1)}, u32[]{:S(2)}, u32[]{:S(2)}) %collective-permute-start.5) | collective-permute-done | bytes 135200 | tf_op jit(solution)/shard_map/ppermute | solution.py:277
  61.4 2.0 %copy-done.2 = bf16[1,512,3584]{2,1,0:T(8,128)(2,1)S(1)} copy-done((bf16[1,512,3584]{2,1,0:T(8,128)(2,1)S(1)}, bf16[1,512,3584]{2,1,0:T(8,128)(2,1)}, u32[]{:S(2)}) %copy-start.2) | copy-done | bytes 3670040
  63.4 6.8 %shard_map.97 = (f32[4,256,256]{2,1,0:T(8,128)S(1)}, f32[4,256,256]{2,1,0:T(8,128)S(1)}) custom-call(s32[8]{0:T(128)S(1)} %broadcast_xor_fusion.order_ref, bf16[512,3584]{1,0:T(8,128)(2,1)S(1)} %bitcast.6, bf16[3584,4096]{1,0:T(8,128)(2,1)} %refs_1_.15, bf16[3584,4096]{1,0:T(8,128)(2,1)} %refs_1_.15, bf16[1,256,256]{2,1,0:T(8,128)(2,1)S(1)} %get-tuple-element.61.refs_2_), custom_call_target="tpu_custom_call" | custom-call | bytes 131072 | tf_op jit(solution)/shard_map/pallas_call | solution.py:111
  71.7 2.6 %collective-permute-start.16 = (bf16[1,256,256]{2,1,0:T(8,128)(2,1)S(1)}, bf16[1,256,256]{2,1,0:T(8,128)(2,1)S(1)}, u32[]{:S(2)}, u32[]{:S(2)}) collective-permute-start(bf16[1,256,256]{2,1,0:T(8,128)(2,1)S(1)} %get-tuple-element.61.refs_2_), channel_id=1, source_target_pairs={{0,8},{2,10},{4,12},{6,14},{8,0},{10,2},{12,4},{14,6},{1,9},{3,11}... | collective-permute-start | bytes 393224 | tf_op jit(solution)/shard_map/ppermute | solution.py:277
  75.6 6.8 %collective-permute-done.15.refs_0_ = bf16[2,256,256]{2,1,0:T(8,128)(2,1)S(1)} collective-permute-done((bf16[2,256,256]{2,1,0:T(8,128)(2,1)S(1)}, bf16[2,256,256]{2,1,0:T(8,128)(2,1)S(1)}, u32[]{:S(2)}, u32[]{:S(2)}) %collective-permute-start.15) | collective-permute-done | bytes 262176 | tf_op jit(solution)/shard_map/ppermute | solution.py:277
  82.6 2.1 %collective-permute-start.21 = (bf16[2,256,256]{2,1,0:T(8,128)(2,1)S(1)}, bf16[2,256,256]{2,1,0:T(8,128)(2,1)S(1)}, u32[]{:S(2)}, u32[]{:S(2)}) collective-permute-start(bf16[2,256,256]{2,1,0:T(8,128)(2,1)S(1)} %get-tuple-element.71.refs_2_), channel_id=1, source_target_pairs={{0,4},{2,6},{4,0},{6,2},{8,12},{10,14},{12,8},{14,10},{1,5},{3,7},... | collective-permute-start | bytes 786440 | tf_op jit(solution)/shard_map/ppermute | solution.py:277
  84.8 3.3 %collective-permute-done.13.refs_1_ = bf16[1,2,128,512]{3,2,1,0:T(8,128)(2,1)S(1)} collective-permute-done((bf16[1,2,128,512]{3,2,1,0:T(8,128)(2,1)S(1)}, bf16[1,2,128,512]{3,2,1,0:T(8,128)(2,1)S(1)}, u32[]{:S(2)}, u32[]{:S(2)}) %collective-permute-start.13) | collective-permute-done | bytes 262176 | tf_op jit(solution)/shard_map/ppermute | solution.py:277
  88.8 2.2 %collective-permute-start.23 = (bf16[1,256,256]{2,1,0:T(8,128)(2,1)S(1)}, bf16[1,256,256]{2,1,0:T(8,128)(2,1)S(1)}, u32[]{:S(2)}, u32[]{:S(2)}) collective-permute-start(bf16[1,256,256]{2,1,0:T(8,128)(2,1)S(1)} %get-tuple-element.70.refs_2_), channel_id=1, source_target_pairs={{0,8},{2,10},{4,12},{6,14},{8,0},{10,2},{12,4},{14,6},{1,9},{3,11}... | collective-permute-start | bytes 393224 | tf_op jit(solution)/shard_map/ppermute | solution.py:277
  91.0 5.5 %collective-permute-done.19.refs_0_ = bf16[2,256,256]{2,1,0:T(8,128)(2,1)S(1)} collective-permute-done((bf16[2,256,256]{2,1,0:T(8,128)(2,1)S(1)}, bf16[2,256,256]{2,1,0:T(8,128)(2,1)S(1)}, u32[]{:S(2)}, u32[]{:S(2)}) %collective-permute-start.19) | collective-permute-done | bytes 262176 | tf_op jit(solution)/shard_map/ppermute | solution.py:277
  97.8 4.8 %collective-permute-done.21.refs_0_ = bf16[2,256,256]{2,1,0:T(8,128)(2,1)S(1)} collective-permute-done((bf16[2,256,256]{2,1,0:T(8,128)(2,1)S(1)}, bf16[2,256,256]{2,1,0:T(8,128)(2,1)S(1)}, u32[]{:S(2)}, u32[]{:S(2)}) %collective-permute-start.21) | collective-permute-done | bytes 262176 | tf_op jit(solution)/shard_map/ppermute | solution.py:277
  103.8 7.1 %collective-permute-done.20.refs_6_.refs_0_ = bf16[1,256,256]{2,1,0:T(8,128)(2,1)S(1)} collective-permute-done((bf16[1,256,256]{2,1,0:T(8,128)(2,1)S(1)}, bf16[1,256,256]{2,1,0:T(8,128)(2,1)S(1)}, u32[]{:S(2)}, u32[]{:S(2)}) %collective-permute-start.20) | collective-permute-done | bytes 131104 | tf_op jit(solution)/shard_map/ppermute | solution.py:277
  111.5 1.6 %collective-permute-done.22.refs_1_.refs_13_ = bf16[1,256,256]{2,1,0:T(8,128)(2,1)S(1)} collective-permute-done((bf16[1,256,256]{2,1,0:T(8,128)(2,1)S(1)}, bf16[1,256,256]{2,1,0:T(8,128)(2,1)S(1)}, u32[]{:S(2)}, u32[]{:S(2)}) %collective-permute-start.22) | collective-permute-done | bytes 131104 | tf_op jit(solution)/shard_map/ppermute | solution.py:277
  113.8 2.8 %shard_map.108 = (f32[8,128]{1,0:T(8,128)S(1)}, f32[1024,512]{1,0:T(8,128)}) custom-call(s32[8]{0:T(128)S(1)} %broadcast_xor_fusion.1.refs_0_, bf16[2,2,128,512]{3,2,1,0:T(8,128)(2,1)S(1)} %shard_map.100.refs_2_.refs_1_, bf16[2,2,128,512]{3,2,1,0:T(8,128)(2,1)S(1)} %shard_map.103.refs_2_, ...), custom_call_target="tpu_custom_call" | custom-call | bytes 131072 | tf_op jit(solution)/shard_map/pallas_call | solution.py:75
  116.7 3.4 %shard_map.109 = (f32[8,128]{1,0:T(8,128)}, f32[1024,512]{1,0:T(8,128)}) custom-call(s32[8]{0:T(128)S(1)} %broadcast_xor_fusion.1.refs_0_, bf16[2,2,128,512]{3,2,1,0:T(8,128)(2,1)S(1)} %shard_map.100.refs_2_.refs_1_, bf16[2,2,128,512]{3,2,1,0:T(8,128)(2,1)S(1)} %shard_map.103.refs_2_, ...), custom_call_target="tpu_custom_call", output_to_operand_aliasing={{1}: (9, {})} | custom-call | bytes 131072 | tf_op jit(solution)/shard_map/pallas_call | solution.py:75
  (87 shorter events, 28.7 us)
Async XLA Ops:
  5.5 15.8 %collective-permute-start = (bf16[4,512,128]{2,1,0:T(8,128)(2,1)S(1)}, bf16[4,512,128]{2,1,0:T(8,128)(2,1)S(1)}, u32[]{:S(2)}, u32[]{:S(2)}) collective-permute-start(bf16[4,512,128]{2,1,0:T(8,128)(2,1)S(1)} %shard_map.82.refs_4_), channel_id=1, source_target_pairs={{0,2},{2,0},{4,6},{6,4},{8,10},{10,8},{12,14},{14,12},{1,3},{3,1},... | collective-permute-start | bytes 1572872 | tf_op jit(solution)/shard_map/ppermute | solution.py:277
  10.0 22.9 %collective-permute-start.3 = (bf16[4,512,128]{2,1,0:T(8,128)(2,1)S(1)}, bf16[4,512,128]{2,1,0:T(8,128)(2,1)S(1)}, u32[]{:S(2)}, u32[]{:S(2)}) collective-permute-start(bf16[4,512,128]{2,1,0:T(8,128)(2,1)S(1)} %shard_map.83.refs_4_), channel_id=1, source_target_pairs={{0,2},{2,0},{4,6},{6,4},{8,10},{10,8},{12,14},{14,12},{1,3},{3,1},... | collective-permute-start | bytes 1572872 | tf_op jit(solution)/shard_map/ppermute | solution.py:277
  21.4 10.5 %collective-permute-start.1 = (bf16[2,512,128]{2,1,0:T(8,128)(2,1)S(1)}, bf16[2,512,128]{2,1,0:T(8,128)(2,1)S(1)}, u32[]{:S(2)}, u32[]{:S(2)}) collective-permute-start(bf16[2,512,128]{2,1,0:T(8,128)(2,1)S(1)} %get-tuple-element.47.refs_2_), channel_id=1, source_target_pairs={{0,4},{2,6},{4,0},{6,2},{8,12},{10,14},{12,8},{14,10},{1,5},{3,7},... | collective-permute-start | bytes 786440 | tf_op jit(solution)/shard_map/ppermute | solution.py:277
  23.6 24.7 %collective-permute-start.6 = (bf16[4,256,256]{2,1,0:T(8,128)(2,1)S(1)}, bf16[4,256,256]{2,1,0:T(8,128)(2,1)S(1)}, u32[]{:S(2)}, u32[]{:S(2)}) collective-permute-start(bf16[4,256,256]{2,1,0:T(8,128)(2,1)S(1)} %get-tuple-element.46.refs_2_), channel_id=1, source_target_pairs={{0,2},{2,0},{4,6},{6,4},{8,10},{10,8},{12,14},{14,12},{1,3},{3,1},... | collective-permute-start | bytes 1572872 | tf_op jit(solution)/shard_map/ppermute | solution.py:277
  32.9 12.9 %collective-permute-start.4 = (bf16[2,512,128]{2,1,0:T(8,128)(2,1)S(1)}, bf16[2,512,128]{2,1,0:T(8,128)(2,1)S(1)}, u32[]{:S(2)}, u32[]{:S(2)}) collective-permute-start(bf16[2,512,128]{2,1,0:T(8,128)(2,1)S(1)} %get-tuple-element.51.refs_2_), channel_id=1, source_target_pairs={{0,4},{2,6},{4,0},{6,2},{8,12},{10,14},{12,8},{14,10},{1,5},{3,7},... | collective-permute-start | bytes 786440 | tf_op jit(solution)/shard_map/ppermute | solution.py:277
  34.8 11.0 %collective-permute-start.2 = (f16[1,528,128]{2,1,0:T(8,128)(2,1)S(1)}, f16[1,528,128]{2,1,0:T(8,128)(2,1)S(1)}, u32[]{:S(2)}, u32[]{:S(2)}) collective-permute-start(f16[1,528,128]{2,1,0:T(8,128)(2,1)S(1)} %convert_element_type.12), channel_id=1, source_target_pairs={{0,8},{2,10},{4,12},{6,14},{8,0},{10,2},{12,4},{14,6},{1,9},{3,11}... | collective-permute-start | bytes 405512 | tf_op jit(solution)/shard_map/ppermute | solution.py:277
  37.5 32.8 %collective-permute-start.11 = (bf16[4,256,256]{2,1,0:T(8,128)(2,1)}, bf16[4,256,256]{2,1,0:T(8,128)(2,1)S(1)}, u32[]{:S(2)}, u32[]{:S(2)}) collective-permute-start(bf16[4,256,256]{2,1,0:T(8,128)(2,1)} %get-tuple-element.63), channel_id=1, source_target_pairs={{0,2},{2,0},{4,6},{6,4},{8,10},{10,8},{12,14},{14,12},{1,3},{3,1},... | collective-permute-start | bytes 1572872 | tf_op jit(solution)/shard_map/ppermute | solution.py:277
  47.4 7.6 %collective-permute-start.5 = (f16[1,528,128]{2,1,0:T(8,128)(2,1)}, f16[1,528,128]{2,1,0:T(8,128)(2,1)S(1)}, u32[]{:S(2)}, u32[]{:S(2)}) collective-permute-start(f16[1,528,128]{2,1,0:T(8,128)(2,1)} %convert_element_type.14), channel_id=1, source_target_pairs={{0,8},{2,10},{4,12},{6,14},{8,0},{10,2},{12,4},{14,6},{1,9},{3,11}... | collective-permute-start | bytes 405512 | tf_op jit(solution)/shard_map/ppermute | solution.py:277
  47.8 24.0 %collective-permute-start.9 = (bf16[4,256,256]{2,1,0:T(8,128)(2,1)S(1)}, bf16[4,256,256]{2,1,0:T(8,128)(2,1)S(1)}, u32[]{:S(2)}, u32[]{:S(2)}) collective-permute-start(bf16[4,256,256]{2,1,0:T(8,128)(2,1)S(1)} %get-tuple-element.49.refs_2_), channel_id=1, source_target_pairs={{0,2},{2,0},{4,6},{6,4},{8,10},{10,8},{12,14},{14,12},{1,3},{3,1},... | collective-permute-start | bytes 1572872 | tf_op jit(solution)/shard_map/ppermute | solution.py:277
  49.1 10.6 %collective-permute-start.10 = (bf16[2,256,256]{2,1,0:T(8,128)(2,1)}, bf16[2,256,256]{2,1,0:T(8,128)(2,1)}, u32[]{:S(2)}, u32[]{:S(2)}) collective-permute-start(bf16[2,256,256]{2,1,0:T(8,128)(2,1)} %get-tuple-element.57.refs_5_), channel_id=1, source_target_pairs={{0,4},{2,6},{4,0},{6,2},{8,12},{10,14},{12,8},{14,10},{1,5},{3,7},... | collective-permute-start | bytes 786440 | tf_op jit(solution)/shard_map/ppermute | solution.py:277
  50.9 31.6 %collective-permute-start.14 = (bf16[4,256,256]{2,1,0:T(8,128)(2,1)}, bf16[4,256,256]{2,1,0:T(8,128)(2,1)S(1)}, u32[]{:S(2)}, u32[]{:S(2)}) collective-permute-start(bf16[4,256,256]{2,1,0:T(8,128)(2,1)} %copy-done.8), channel_id=1, source_target_pairs={{0,2},{2,0},{4,6},{6,4},{8,10},{10,8},{12,14},{14,12},{1,3},{3,1},... | collective-permute-start | bytes 1572872 | tf_op jit(solution)/shard_map/ppermute | solution.py:277
  59.3 15.2 %collective-permute-start.8 = (bf16[1,2,128,512]{3,2,1,0:T(8,128)(2,1)S(1)}, bf16[1,2,128,512]{3,2,1,0:T(8,128)(2,1)S(1)}, u32[]{:S(2)}, u32[]{:S(2)}) collective-permute-start(bf16[1,2,128,512]{3,2,1,0:T(8,128)(2,1)S(1)} %shard_map.95.refs_2_.refs_0_), channel_id=1, source_target_pairs={{0,8},{2,10},{4,12},{6,14},{8,0},{10,2},{12,4},{14,6},{1,9},{3,11}... | collective-permute-start | bytes 786440 | tf_op jit(solution)/shard_map/ppermute | solution.py:277
  59.7 15.2 %collective-permute-start.12 = (bf16[1,2,128,512]{3,2,1,0:T(8,128)(2,1)S(1)}, bf16[1,2,128,512]{3,2,1,0:T(8,128)(2,1)S(1)}, u32[]{:S(2)}, u32[]{:S(2)}) collective-permute-start(bf16[1,2,128,512]{3,2,1,0:T(8,128)(2,1)S(1)} %shard_map.95.refs_2_.refs_0_), channel_id=1, source_target_pairs={{0,4},{2,6},{4,0},{6,2},{8,12},{10,14},{12,8},{14,10},{1,5},{3,7},... | collective-permute-start | bytes 786440 | tf_op jit(solution)/shard_map/ppermute | solution.py:277
  70.3 12.1 %collective-permute-start.15 = (bf16[2,256,256]{2,1,0:T(8,128)(2,1)S(1)}, bf16[2,256,256]{2,1,0:T(8,128)(2,1)S(1)}, u32[]{:S(2)}, u32[]{:S(2)}) collective-permute-start(bf16[2,256,256]{2,1,0:T(8,128)(2,1)S(1)} %get-tuple-element.65.refs_2_), channel_id=1, source_target_pairs={{0,4},{2,6},{4,0},{6,2},{8,12},{10,14},{12,8},{14,10},{1,5},{3,7},... | collective-permute-start | bytes 786440 | tf_op jit(solution)/shard_map/ppermute | solution.py:277
  71.7 10.8 %collective-permute-start.16 = (bf16[1,256,256]{2,1,0:T(8,128)(2,1)S(1)}, bf16[1,256,256]{2,1,0:T(8,128)(2,1)S(1)}, u32[]{:S(2)}, u32[]{:S(2)}) collective-permute-start(bf16[1,256,256]{2,1,0:T(8,128)(2,1)S(1)} %get-tuple-element.61.refs_2_), channel_id=1, source_target_pairs={{0,8},{2,10},{4,12},{6,14},{8,0},{10,2},{12,4},{14,6},{1,9},{3,11}... | collective-permute-start | bytes 393224 | tf_op jit(solution)/shard_map/ppermute | solution.py:277
  74.5 13.5 %collective-permute-start.13 = (bf16[1,2,128,512]{3,2,1,0:T(8,128)(2,1)S(1)}, bf16[1,2,128,512]{3,2,1,0:T(8,128)(2,1)S(1)}, u32[]{:S(2)}, u32[]{:S(2)}) collective-permute-start(bf16[1,2,128,512]{3,2,1,0:T(8,128)(2,1)S(1)} %collective-permute-done.8.refs_1_), channel_id=1, source_target_pairs={{0,4},{2,6},{4,0},{6,2},{8,12},{10,14},{12,8},{14,10},{1,5},{3,7},... | collective-permute-start | bytes 786440 | tf_op jit(solution)/shard_map/ppermute | solution.py:277
  74.9 38.4 %collective-permute-start.17 = (bf16[2,2,128,512]{3,2,1,0:T(8,128)(2,1)S(1)}, bf16[2,2,128,512]{3,2,1,0:T(8,128)(2,1)S(1)}, u32[]{:S(2)}, u32[]{:S(2)}) collective-permute-start(bf16[2,2,128,512]{3,2,1,0:T(8,128)(2,1)S(1)} %shard_map.100.refs_2_.refs_1_), channel_id=1, source_target_pairs={{0,2},{2,0},{4,6},{6,4},{8,10},{10,8},{12,14},{14,12},{1,3},{3,1},... | collective-permute-start | bytes 1572872 | tf_op jit(solution)/shard_map/ppermute | solution.py:277
  82.4 14.0 %collective-permute-start.19 = (bf16[2,256,256]{2,1,0:T(8,128)(2,1)S(1)}, bf16[2,256,256]{2,1,0:T(8,128)(2,1)S(1)}, u32[]{:S(2)}, u32[]{:S(2)}) collective-permute-start(bf16[2,256,256]{2,1,0:T(8,128)(2,1)S(1)} %get-tuple-element.66.refs_2_), channel_id=1, source_target_pairs={{0,4},{2,6},{4,0},{6,2},{8,12},{10,14},{12,8},{14,10},{1,5},{3,7},... | collective-permute-start | bytes 786440 | tf_op jit(solution)/shard_map/ppermute | solution.py:277
  82.6 19.9 %collective-permute-start.21 = (bf16[2,256,256]{2,1,0:T(8,128)(2,1)S(1)}, bf16[2,256,256]{2,1,0:T(8,128)(2,1)S(1)}, u32[]{:S(2)}, u32[]{:S(2)}) collective-permute-start(bf16[2,256,256]{2,1,0:T(8,128)(2,1)S(1)} %get-tuple-element.71.refs_2_), channel_id=1, source_target_pairs={{0,4},{2,6},{4,0},{6,2},{8,12},{10,14},{12,8},{14,10},{1,5},{3,7},... | collective-permute-start | bytes 786440 | tf_op jit(solution)/shard_map/ppermute | solution.py:277
  88.1 25.7 %collective-permute-start.18 = (bf16[2,2,128,512]{3,2,1,0:T(8,128)(2,1)S(1)}, bf16[2,2,128,512]{3,2,1,0:T(8,128)(2,1)S(1)}, u32[]{:S(2)}, u32[]{:S(2)}) collective-permute-start(bf16[2,2,128,512]{3,2,1,0:T(8,128)(2,1)S(1)} %shard_map.103.refs_2_), channel_id=1, source_target_pairs={{0,2},{2,0},{4,6},{6,4},{8,10},{10,8},{12,14},{14,12},{1,3},{3,1},... | collective-permute-start | bytes 1572872 | tf_op jit(solution)/shard_map/ppermute | solution.py:277
  88.8 15.0 %collective-permute-start.23 = (bf16[1,256,256]{2,1,0:T(8,128)(2,1)S(1)}, bf16[1,256,256]{2,1,0:T(8,128)(2,1)S(1)}, u32[]{:S(2)}, u32[]{:S(2)}) collective-permute-start(bf16[1,256,256]{2,1,0:T(8,128)(2,1)S(1)} %get-tuple-element.70.refs_2_), channel_id=1, source_target_pairs={{0,8},{2,10},{4,12},{6,14},{8,0},{10,2},{12,4},{14,6},{1,9},{3,11}... | collective-permute-start | bytes 393224 | tf_op jit(solution)/shard_map/ppermute | solution.py:277
  96.5 14.3 %collective-permute-start.20 = (bf16[1,256,256]{2,1,0:T(8,128)(2,1)S(1)}, bf16[1,256,256]{2,1,0:T(8,128)(2,1)S(1)}, u32[]{:S(2)}, u32[]{:S(2)}) collective-permute-start(bf16[1,256,256]{2,1,0:T(8,128)(2,1)S(1)} %get-tuple-element.73.refs_2_), channel_id=1, source_target_pairs={{0,8},{2,10},{4,12},{6,14},{8,0},{10,2},{12,4},{14,6},{1,9},{3,11}... | collective-permute-start | bytes 393224 | tf_op jit(solution)/shard_map/ppermute | solution.py:277
  102.6 10.5 %collective-permute-start.22 = (bf16[1,256,256]{2,1,0:T(8,128)(2,1)S(1)}, bf16[1,256,256]{2,1,0:T(8,128)(2,1)S(1)}, u32[]{:S(2)}, u32[]{:S(2)}) collective-permute-start(bf16[1,256,256]{2,1,0:T(8,128)(2,1)S(1)} %get-tuple-element.75.refs_4_), channel_id=1, source_target_pairs={{0,8},{2,10},{4,12},{6,14},{8,0},{10,2},{12,4},{14,6},{1,9},{3,11}... | collective-permute-start | bytes 393224 | tf_op jit(solution)/shard_map/ppermute | solution.py:277
  113.2 3.5 %collective-permute-start.25 = (f32[256,256]{1,0:T(8,128)S(1)}, f32[256,256]{1,0:T(8,128)S(1)}, u32[]{:S(2)}, u32[]{:S(2)}) collective-permute-start(f32[256,256]{1,0:T(8,128)S(1)} %get-tuple-element.82.refs_7_), channel_id=1, source_target_pairs={{0,1},{1,0},{2,3},{3,2},{4,5},{5,4},{6,7},{7,6},{8,9},{9,8},{10,11... | collective-permute-start | bytes 786440 | tf_op jit(solution)/shard_map/ppermute | solution.py:281
  (14 other events, 66.4 us)
